TPU v7x, 32 devices: a whole 2x2x4 slice. The times are simulated.
32 devices in a mesh: section: 2 (over core), dp: 16 (over z, y, x).
Axes of the slice: x: 2, y: 2, z: 4, core: 2. Of those that a mesh axis runs over, the one named last changes fastest.
Arguments:
- layer_input: bfloat16 [128, 340, 256], P('dp'), may hold values from -6 to 6
- out_cotangent: bfloat16 [128, 340, 256], P('dp'), may hold values from -6 to 6
- segment_ids: int32 [128, 340], P('dp'), may hold values from 0 to 3, never falling along the last dimension, each value on 1 to 170 neighbouring positions
- gain_attn: bfloat16 [2, 256], P('section'), may hold values from 0.099609375 to 1.8984375
- weight_qkv: bfloat16 [2, 256, 768], P('section'), may hold values from -0.375 to 0.375
- weight_out: bfloat16 [2, 256, 256], P('section'), may hold values from -1.5 to 1.5
- gain_mlp: bfloat16 [2, 256], P('section'), may hold values from 0.099609375 to 1.8984375
- weight_up: bfloat16 [2, 256, 1024], P('section'), may hold values from -0.375 to 0.375
- weight_down: bfloat16 [2, 1024, 256], P('section'), may hold values from -0.25 to 0.25
Outputs:
- activations: bfloat16 [2, 128, 340, 256], P('section', 'dp')
- input_grads: float32 [2, 128, 340, 256], P('section', 'dp')
- grad_qkv: float32 [2, 256, 768], P('section')
- grad_out: float32 [2, 256, 256], P('section')
- grad_up: float32 [2, 256, 1024], P('section')
- grad_down: float32 [2, 1024, 256], P('section')
- grad_gain_attn: float32 [2, 256], P('section')
- grad_gain_mlp: float32 [2, 256], P('section')
Inputs may be any that keep to these rules, and one draw needn't show every extreme that they name: `segment_ids`: within each row the ids never fall; each of 0 to 3 occurs as one run of 1 to 170 tokens.
All inputs are finite; a program needn't handle non-finite values.
Results may differ from a plain program's by a relative error of at most 0.019.
Values may be sent and summed in bfloat16 or wider, within the bound.
No kernel may reach another device: no remote copies, remote signals or barrier semaphores. Data moves between devices by JAX's collectives and lax.ppermute only.
A program may use at most 128 MiB of HBM per device.

v0:
```python
import jax
import jax.numpy as jnp
from jax import lax
from jax.sharding import PartitionSpec as P

HEADS = 4
FRAME = 17
MICRO = 4


EPS = 1e-05
NEG = -1e30


def from_partner(value, axis, bit):
    mask = 2**bit
    pairs = [(source, source ^ mask) for source in range(lax.axis_size(axis))]
    return lax.ppermute(value, axis, pairs)


def normalize(values, gain):
    center = values - jnp.mean(values, axis=-1, keepdims=True)
    scale = lax.rsqrt(jnp.mean(center * center, axis=-1, keepdims=True) + EPS)
    return center * scale * gain


def softmax_rows(scores):
    highest = jnp.max(scores, axis=-1, keepdims=True)
    expo = jnp.exp(scores - highest)
    return expo / jnp.sum(expo, axis=-1, keepdims=True)


def gelu_exact(values):
    return jax.nn.gelu(values, approximate=False)


def block_mask(segments):
    length = segments.shape[1]
    frames = lax.iota(jnp.int32, length) // FRAME
    causal = frames[None, :] <= frames[:, None]
    same = segments[:, :, None] == segments[:, None, :]
    return jnp.logical_and(same, causal[None])


def layer_parts(inputs, params, mask):
    gain_attn, weight_qkv, weight_out, gain_mlp, weight_up, weight_down = params
    count, length, width = inputs.shape
    resid = inputs.astype(jnp.float32).reshape(count * length, width)
    normed_attn = normalize(resid, gain_attn).astype(jnp.bfloat16)
    packed = jnp.dot(normed_attn, weight_qkv, preferred_element_type=jnp.float32).astype(
        jnp.bfloat16
    )
    packed = packed.reshape(count, length, 3, HEADS, width // HEADS)
    query, key, value = (packed[:, :, 0], packed[:, :, 1], packed[:, :, 2])
    factor = (width // HEADS) ** (-0.5)
    scores = jnp.einsum("bqhd,bkhd->bhqk", query, key, preferred_element_type=jnp.float32) * factor
    scores = jnp.where(mask[:, None], scores, NEG)
    probs = softmax_rows(scores)
    probs_low = probs.astype(jnp.bfloat16)
    mixed = jnp.einsum("bhqk,bkhd->bqhd", probs_low, value, preferred_element_type=jnp.float32)
    mixed = mixed.astype(jnp.bfloat16).reshape(count * length, width)
    middle = resid + jnp.dot(mixed, weight_out, preferred_element_type=jnp.float32)
    normed_mlp = normalize(middle, gain_mlp).astype(jnp.bfloat16)
    upper = jnp.dot(normed_mlp, weight_up, preferred_element_type=jnp.float32)
    active = gelu_exact(upper).astype(jnp.bfloat16)
    result = middle + jnp.dot(active, weight_down, preferred_element_type=jnp.float32)
    saved = (
        resid,
        normed_attn,
        query,
        key,
        value,
        probs,
        probs_low,
        mixed,
        middle,
        normed_mlp,
        upper,
        active,
    )
    return (result, saved)


def layer_backward(inputs, upstream, params, mask):
    gain_attn, weight_qkv, weight_out, gain_mlp, weight_up, weight_down = params
    count, length, width = inputs.shape
    result, saved = layer_parts(inputs, params, mask)
    (
        resid,
        normed_attn,
        query,
        key,
        value,
        probs,
        probs_low,
        mixed,
        middle,
        normed_mlp,
        upper,
        active,
    ) = saved
    factor = (width // HEADS) ** (-0.5)
    grad_flat = upstream.reshape(count * length, width)
    grad_low = grad_flat.astype(jnp.bfloat16)
    grad_down = jnp.einsum("nf,nd->fd", active, grad_low, preferred_element_type=jnp.float32)
    d_active = jnp.einsum("nd,fd->nf", grad_low, weight_down, preferred_element_type=jnp.float32)
    unused, gelu_back = jax.vjp(gelu_exact, upper)
    d_upper = gelu_back(d_active)[0].astype(jnp.bfloat16)
    grad_up = jnp.einsum("nd,nf->df", normed_mlp, d_upper, preferred_element_type=jnp.float32)
    d_normed_mlp = jnp.einsum("nf,df->nd", d_upper, weight_up, preferred_element_type=jnp.float32)
    unused, norm_back_mlp = jax.vjp(normalize, middle, gain_mlp)
    d_middle_part, grad_gain_mlp = norm_back_mlp(d_normed_mlp)
    d_middle = grad_flat + d_middle_part
    d_middle_low = d_middle.astype(jnp.bfloat16)
    grad_out = jnp.einsum("nd,ne->de", mixed, d_middle_low, preferred_element_type=jnp.float32)
    d_mixed = jnp.einsum("ne,de->nd", d_middle_low, weight_out, preferred_element_type=jnp.float32)
    d_mixed = d_mixed.astype(jnp.bfloat16).reshape(count, length, HEADS, width // HEADS)
    d_value = jnp.einsum("bhqk,bqhd->bkhd", probs_low, d_mixed, preferred_element_type=jnp.float32)
    d_probs = jnp.einsum("bqhd,bkhd->bhqk", d_mixed, value, preferred_element_type=jnp.float32)
    d_scores = probs * (d_probs - jnp.sum(d_probs * probs, axis=-1, keepdims=True))
    d_scores = d_scores.astype(jnp.bfloat16)
    d_query = (
        jnp.einsum("bhqk,bkhd->bqhd", d_scores, key, preferred_element_type=jnp.float32) * factor
    )
    d_key = (
        jnp.einsum("bhqk,bqhd->bkhd", d_scores, query, preferred_element_type=jnp.float32) * factor
    )
    d_packed = (
        jnp.stack([d_query, d_key, d_value], axis=2)
        .reshape(count * length, 3 * width)
        .astype(jnp.bfloat16)
    )
    grad_qkv = jnp.einsum("nd,ne->de", normed_attn, d_packed, preferred_element_type=jnp.float32)
    d_normed_attn = jnp.einsum(
        "ne,de->nd", d_packed, weight_qkv, preferred_element_type=jnp.float32
    )
    unused, norm_back_attn = jax.vjp(normalize, resid, gain_attn)
    d_resid_part, grad_gain_attn = norm_back_attn(d_normed_attn)
    d_inputs = (d_middle + d_resid_part).reshape(count, length, width)
    return (
        d_inputs,
        (
            grad_qkv,
            grad_out,
            grad_up,
            grad_down,
            grad_gain_attn.astype(jnp.float32),
            grad_gain_mlp.astype(jnp.float32),
        ),
    )


def split_plan(layer_input, out_cotangent, segment_ids, params, first):
    rows, length, width = layer_input.shape
    micro_rows = rows // MICRO
    halfway = rows // 2
    others = (
        from_partner(params[0].astype(jnp.bfloat16), "section", 0).astype(jnp.float32),
        from_partner(params[1], "section", 0),
        from_partner(params[2], "section", 0),
        from_partner(params[3].astype(jnp.bfloat16), "section", 0).astype(jnp.float32),
        from_partner(params[4], "section", 0),
        from_partner(params[5], "section", 0),
    )
    first_params = tuple((jnp.where(first, mine, theirs) for mine, theirs in zip(params, others)))
    second_params = tuple((jnp.where(first, theirs, mine) for mine, theirs in zip(params, others)))
    offset = lax.axis_index("section") * halfway
    my_input = lax.dynamic_slice_in_dim(layer_input, offset, halfway, 0)
    my_cotangent = lax.dynamic_slice_in_dim(out_cotangent, offset, halfway, 0)
    my_segments = lax.dynamic_slice_in_dim(segment_ids, offset, halfway, 0)
    zero_grads = tuple(
        (
            jnp.zeros(p.shape, jnp.float32)
            for p in (params[1], params[2], params[4], params[5], params[0], params[3])
        )
    )

    def one_micro(carry, index):
        totals_first, totals_second = carry
        begin = index * micro_rows
        inputs = lax.dynamic_slice_in_dim(my_input, begin, micro_rows, 0)
        cotangent = lax.dynamic_slice_in_dim(my_cotangent, begin, micro_rows, 0).astype(jnp.float32)
        mask = block_mask(lax.dynamic_slice_in_dim(my_segments, begin, micro_rows, 0))
        result, unused = layer_parts(inputs, first_params, mask)
        hidden = result.reshape(inputs.shape).astype(jnp.bfloat16)
        second_result, unused = layer_parts(hidden, second_params, mask)
        output = second_result.reshape(inputs.shape).astype(jnp.bfloat16)
        d_second, grads_second = layer_backward(hidden, cotangent, second_params, mask)
        d_first, grads_first = layer_backward(
            inputs, d_second.astype(jnp.bfloat16).astype(jnp.float32), first_params, mask
        )
        totals_first = tuple((a + b for a, b in zip(totals_first, grads_first)))
        totals_second = tuple((a + b for a, b in zip(totals_second, grads_second)))
        return ((totals_first, totals_second), (hidden, output, d_first, d_second))

    indices = jnp.arange(halfway // micro_rows, dtype=jnp.int32)
    (totals_first, totals_second), (hidden_all, output_all, first_all, second_all) = lax.scan(
        one_micro, (zero_grads, zero_grads), indices
    )
    both = lax.psum(
        (
            totals_first[0],
            totals_first[1],
            totals_first[2],
            totals_first[3],
            totals_first[4],
            totals_first[5],
            totals_second[0],
            totals_second[1],
            totals_second[2],
            totals_second[3],
            totals_second[4],
            totals_second[5],
        ),
        ("section", "dp"),
    )
    summed = tuple((jnp.where(first, both[index], both[index + 6]) for index in range(6)))
    shape = (halfway, length, width)
    hidden_all = hidden_all.reshape(shape)
    output_all = output_all.reshape(shape)
    first_all = first_all.reshape(shape)
    second_all = second_all.reshape(shape)
    keep_acts = jnp.where(first, hidden_all, output_all)
    keep_grads = jnp.where(first, first_all, second_all)
    send_acts = jnp.where(first, output_all, hidden_all).astype(jnp.float32)
    send_grads = jnp.where(first, second_all, first_all)
    got_acts, got_grads = (
        from_partner(send_acts.astype(jnp.bfloat16), "section", 0).astype(send_acts.dtype),
        from_partner(send_grads.astype(jnp.bfloat16), "section", 0).astype(send_grads.dtype),
    )
    got_acts = got_acts.astype(jnp.bfloat16)
    activations = jnp.where(
        first,
        jnp.concatenate([keep_acts, got_acts], axis=0),
        jnp.concatenate([got_acts, keep_acts], axis=0),
    )
    input_grads = jnp.where(
        first,
        jnp.concatenate([keep_grads, got_grads], axis=0),
        jnp.concatenate([got_grads, keep_grads], axis=0),
    )
    return (activations, input_grads, summed)


def shards(
    layer_input,
    out_cotangent,
    segment_ids,
    gain_attn,
    weight_qkv,
    weight_out,
    gain_mlp,
    weight_up,
    weight_down,
):
    params = (
        gain_attn[0].astype(jnp.float32),
        weight_qkv[0],
        weight_out[0],
        gain_mlp[0].astype(jnp.float32),
        weight_up[0],
        weight_down[0],
    )
    first = lax.axis_index("section") == 0
    activations, input_grads, summed = split_plan(
        layer_input, out_cotangent, segment_ids, params, first
    )
    return (
        activations[None],
        input_grads[None],
        summed[0][None],
        summed[1][None],
        summed[2][None],
        summed[3][None],
        summed[4][None],
        summed[5][None],
    )


def solution(mesh):
    placed = (
        P("dp", None, None),
        P("dp", None, None),
        P("dp", None),
        P("section", None),
        P("section", None, None),
        P("section", None, None),
        P("section", None),
        P("section", None, None),
        P("section", None, None),
    )
    return jax.shard_map(
        shards,
        mesh=mesh,
        in_specs=placed,
        out_specs=(
            P("section", "dp", None, None),
            P("section", "dp", None, None),
            P("section", None, None),
            P("section", None, None),
            P("section", None, None),
            P("section", None, None),
            P("section", None),
            P("section", None),
        ),
        check_vma=False,
    )
```

profile of v0, /device:TPU:0, one launch (start us, length us, event | category | flops | bytes accessed | tf_op | source)
XLA Modules:
  0.0 478.6 jit_solution(16514194338157799374)
XLA Ops:
  10.4 3.6 constant_dynamic-slice_fusion.3
  19.0 283.2 %while.43 = (s32[]{:T(128)}, f32[256,768]{1,0:T(8,128)}, f32[256,256]{1,0:T(8,128)}, f32[256,1024]{1,0:T(8,128)}, f32[1024,256]{1,0:T(8,128)}, /*index=5*/f32[25...) while((s32[]{:T(128)}, f32[256,768]{1,0:T(8,128)}, ...), condition=%wide.region_27.28_spmd.clone, body=%wide.region_0.27_spmd.clone.sunk | while | flops 8010267136 | bytes 382136256 | solution.py:197
  30.0 3.5 reshape.535
  39.0 3.8 fusion.338
  47.0 8.5 %multiply_convert_fusion.25 = (bf16[680,1024]{1,0:T(8,128)(2,1)S(1)}, f32[680,1024]{1,0:T(8,128)}, f32[680,1024]{1,0:T(8,128)}) fusion(bf16[256,1024]{1,0:T(8,128)(2,1)S(1)} %copy-done.74, f32[680,256]{1,0:T(8,128)S(1)} %get-tuple-element.973, f32[256]{0:T(256)} %get-tuple-element.1121, f32[680]{0:T(1024)S(1)} %fusion.341, ...), kind=kOutput, calls=%fused_computation.31.clone.1 | convolution fusion | flops 402472960 | bytes 8190272 | tf_op jit(solution)/shard_map/while/body/eval_jaxpr/dot_general | solution.py:64
  62.1 3.1 fusion.344
  68.7 4.9 %fusion.345 = (f32[2,4,340]{2,1,0:T(4,128)S(1)}, f32[2,4,340,340]{2,3,1,0:T(8,128)}) fusion(pred[2,340,340]{1,2,0:T(8,128)(4,1)} %compare_and_fusion.2, bf16[2,340,1,4,64]{1,4,3,0,2:T(8,128)(2,1)S(1)} %copy.164, bf16[2,340,1,4,64]{1,4,3,0,2:T(8,128)(2,1)S(1)} %copy.165), kind=kOutput, calls=%fused_computation.241.clone.1 | convolution fusion | flops 122073936 | bytes 4637600 | tf_op jit(solution)/shard_map/while/body/eval_jaxpr/sub | solution.py:29
  77.9 7.3 %multiply_convert_fusion.26 = (bf16[680,1024]{1,0:T(8,128)(2,1)S(1)}, f32[680,1024]{1,0:T(8,128)S(1)}, f32[680,1024]{1,0:T(8,128)S(1)}) fusion(bf16[256,1024]{1,0:T(8,128)(2,1)} %get-tuple-element.1128, f32[680,256]{1,0:T(8,128)S(1)} %get-tuple-element.985, f32[256]{0:T(256)S(1)} %copy-done.82, f32[680]{0:T(1024)S(1)} %fusion.348, ...), kind=kOutput, calls=%fused_computation.16.clone.1 | convolution fusion | flops 402472960 | bytes 8190272 | tf_op jit(solution)/shard_map/while/body/eval_jaxpr/dot_general | solution.py:64
  91.1 3.0 multiply_reduce_fusion.22
  98.5 3.1 fusion.351
  101.8 3.7 multiply_reduce_fusion.23
  110.9 4.0 convert_element_type.494
  135.5 3.1 convolution_bitcast_fusion.2
  138.7 3.2 multiply_reduce_fusion.25
  147.2 3.0 convert_element_type.495
  167.6 3.7 reshape.535
  176.9 3.8 fusion.338
  185.0 8.5 %multiply_convert_fusion.25 = (bf16[680,1024]{1,0:T(8,128)(2,1)S(1)}, f32[680,1024]{1,0:T(8,128)}, f32[680,1024]{1,0:T(8,128)}) fusion(bf16[256,1024]{1,0:T(8,128)(2,1)S(1)} %copy-done.74, f32[680,256]{1,0:T(8,128)S(1)} %get-tuple-element.973, f32[256]{0:T(256)} %get-tuple-element.1121, f32[680]{0:T(1024)S(1)} %fusion.341, ...), kind=kOutput, calls=%fused_computation.31.clone.1 | convolution fusion | flops 402472960 | bytes 8190272 | tf_op jit(solution)/shard_map/while/body/eval_jaxpr/dot_general | solution.py:64
  200.1 3.1 fusion.344
  206.6 4.9 %fusion.345 = (f32[2,4,340]{2,1,0:T(4,128)S(1)}, f32[2,4,340,340]{2,3,1,0:T(8,128)}) fusion(pred[2,340,340]{1,2,0:T(8,128)(4,1)} %compare_and_fusion.2, bf16[2,340,1,4,64]{1,4,3,0,2:T(8,128)(2,1)S(1)} %copy.164, bf16[2,340,1,4,64]{1,4,3,0,2:T(8,128)(2,1)S(1)} %copy.165), kind=kOutput, calls=%fused_computation.241.clone.1 | convolution fusion | flops 122073936 | bytes 4637600 | tf_op jit(solution)/shard_map/while/body/eval_jaxpr/sub | solution.py:29
  215.8 7.3 %multiply_convert_fusion.26 = (bf16[680,1024]{1,0:T(8,128)(2,1)S(1)}, f32[680,1024]{1,0:T(8,128)S(1)}, f32[680,1024]{1,0:T(8,128)S(1)}) fusion(bf16[256,1024]{1,0:T(8,128)(2,1)} %get-tuple-element.1128, f32[680,256]{1,0:T(8,128)S(1)} %get-tuple-element.985, f32[256]{0:T(256)S(1)} %copy-done.82, f32[680]{0:T(1024)S(1)} %fusion.348, ...), kind=kOutput, calls=%fused_computation.16.clone.1 | convolution fusion | flops 402472960 | bytes 8190272 | tf_op jit(solution)/shard_map/while/body/eval_jaxpr/dot_general | solution.py:64
  226.1 3.1 convolution_add_fusion.27
  230.0 3.0 multiply_reduce_fusion.22
  237.4 3.1 fusion.351
  240.7 3.7 multiply_reduce_fusion.23
  249.9 4.2 convert_element_type.494
  268.5 3.0 convolution_add_fusion.22
  276.2 3.1 convolution_bitcast_fusion.2
  279.4 3.2 multiply_reduce_fusion.25
  287.9 3.0 convert_element_type.495
  307.1 43.4 %all-reduce = (f32[256]{0:T(256)S(1)}, f32[256]{0:T(256)S(1)}, f32[256]{0:T(256)S(1)}, f32[256]{0:T(256)S(1)}) all-reduce(f32[256]{0:T(256)S(1)} %copy-done.98, f32[256]{0:T(256)S(1)} %copy-done.92, f32[256]{0:T(256)S(1)} %copy-done.95, f32[256]{0:T(256)S(1)} %copy-done.89), channel_id=1, replica_groups=mesh['section'=2,'dp'=16] {'section','dp'}, use_global_device_ids=true, to_apply=%region_36.37 | all-reduce | flops 1024 | bytes 8192 | tf_op jit(solution)/shard_map/psum | solution.py:200
  358.6 106.7 %all-reduce.4.cloned.1.call-done = (f32[256,768]{1,0:T(8,128)}, f32[256,768]{1,0:T(8,128)}, f32[256,256]{1,0:T(8,128)}, f32[256,256]{1,0:T(8,128)}, f32[256,1024...) async-done(((f32[256,768]{1,0:T(8,128)}, f32[256,768]{1,0:T(8,128)}, f32[256,256]{1,0:T(8,128)}, f32[256,256]{1,0:T(8,128)}, ...) | async-done | bytes 6291472 | tf_op jit(solution)/shard_map/psum | solution.py:200
  (663 shorter events, 186.8 us)
Async XLA Ops:
  7.2 8.1 %copy-start.81 = (bf16[1,256,256]{2,1,0:T(8,128)(2,1)S(1)}, bf16[1,256,256]{2,1,0:T(8,128)(2,1)}, u32[]{:S(2)}) copy-start(bf16[1,256,256]{2,1,0:T(8,128)(2,1)} %param.16) | copy-start | bytes 393220
  7.2 8.8 %copy-start.76 = (bf16[1,256,768]{2,1,0:T(8,128)(2,1)S(1)}, bf16[1,256,768]{2,1,0:T(8,128)(2,1)}, u32[]{:S(2)}) copy-start(bf16[1,256,768]{2,1,0:T(8,128)(2,1)} %param.15) | copy-start | bytes 1179652
  7.2 9.6 %copy-start.72 = (bf16[1,1024,256]{2,1,0:T(8,128)(2,1)S(1)}, bf16[1,1024,256]{2,1,0:T(8,128)(2,1)}, u32[]{:S(2)}) copy-start(bf16[1,1024,256]{2,1,0:T(8,128)(2,1)} %param.19) | copy-start | bytes 1572868
  7.2 458.1 %all-reduce.4.cloned.1.call-start = ((), (), s32[]{:S(2)}) async-start(), calls=%async_computation | async-start | bytes 12582912 | tf_op jit(solution)/shard_map/psum | solution.py:200
  8.1 5.9 %collective-permute-start.3 = (bf16[256]{0:T(256)(128)(2,1)S(1)}, bf16[256]{0:T(256)(128)(2,1)S(1)}, u32[]{:S(2)}, u32[]{:S(2)}) collective-permute-start(bf16[256]{0:T(256)(128)(2,1)S(1)} %reduce.9), channel_id=1, source_target_pairs={{0,16},{16,0},{1,17},{17,1},{2,18},{18,2},{3,19},{19,3},{4,20},{20... | collective-permute-start | bytes 1544 | tf_op jit(solution)/shard_map/ppermute | solution.py:18
  9.3 5.4 %collective-permute-start = (bf16[256]{0:T(256)(128)(2,1)S(1)}, bf16[256]{0:T(256)(128)(2,1)S(1)}, u32[]{:S(2)}, u32[]{:S(2)}) collective-permute-start(bf16[256]{0:T(256)(128)(2,1)S(1)} %reduce.8), channel_id=1, source_target_pairs={{0,16},{16,0},{1,17},{17,1},{2,18},{18,2},{3,19},{19,3},{4,20},{20... | collective-permute-start | bytes 1544 | tf_op jit(solution)/shard_map/ppermute | solution.py:18
  9.4 5.9 %collective-permute-start.2 = (bf16[256,256]{1,0:T(8,128)(2,1)}, bf16[256,256]{1,0:T(8,128)(2,1)S(1)}, u32[]{:S(2)}, u32[]{:S(2)}) collective-permute-start(bf16[256,256]{1,0:T(8,128)(2,1)} %bitcast.340), channel_id=1, source_target_pairs={{0,16},{16,0},{1,17},{17,1},{2,18},{18,2},{3,19},{19,3},{4,20},{20... | collective-permute-start | bytes 393224 | tf_op jit(solution)/shard_map/ppermute | solution.py:18
  9.9 6.2 %collective-permute-start.1 = (bf16[256,768]{1,0:T(8,128)(2,1)}, bf16[256,768]{1,0:T(8,128)(2,1)S(1)}, u32[]{:S(2)}, u32[]{:S(2)}) collective-permute-start(bf16[256,768]{1,0:T(8,128)(2,1)} %bitcast.339), channel_id=1, source_target_pairs={{0,16},{16,0},{1,17},{17,1},{2,18},{18,2},{3,19},{19,3},{4,20},{20... | collective-permute-start | bytes 1179656 | tf_op jit(solution)/shard_map/ppermute | solution.py:18
  9.9 6.9 %collective-permute-start.5 = (bf16[1024,256]{1,0:T(8,128)(2,1)}, bf16[1024,256]{1,0:T(8,128)(2,1)S(1)}, u32[]{:S(2)}, u32[]{:S(2)}) collective-permute-start(bf16[1024,256]{1,0:T(8,128)(2,1)} %bitcast.337), channel_id=1, source_target_pairs={{0,16},{16,0},{1,17},{17,1},{2,18},{18,2},{3,19},{19,3},{4,20},{20... | collective-permute-start | bytes 1572872 | tf_op jit(solution)/shard_map/ppermute | solution.py:18
  14.0 3.9 collective-permute-start.4
  19.0 7.8 %copy-start.85 = (s32[4,340]{1,0:T(4,128)}, s32[4,340]{1,0:T(4,128)S(1)}, u32[]{:S(2)}) copy-start(s32[4,340]{1,0:T(4,128)S(1)} %get-tuple-element.1118) | copy-start | bytes 16324 | tf_op jit(solution)/shard_map/while
  19.0 8.8 %copy-start.38 = (bf16[256,768]{1,0:T(8,128)(2,1)}, bf16[256,768]{1,0:T(8,128)(2,1)S(1)}, u32[]{:S(2)}) copy-start(bf16[256,768]{1,0:T(8,128)(2,1)S(1)} %get-tuple-element.1117) | copy-start | bytes 1179652 | tf_op jit(solution)/shard_map/while
  46.3 9.3 %copy-start.3 = (bf16[680,256]{0,1:T(8,128)(2,1)}, bf16[680,256]{0,1:T(8,128)(2,1)S(1)}, u32[]{:S(2)}) copy-start(bf16[680,256]{0,1:T(8,128)(2,1)S(1)} %reshape.536) | copy-start | bytes 1044484 | tf_op jit(solution)/shard_map/while
  47.0 8.5 %copy-start.58 = (f32[680]{0:T(1024)}, f32[680]{0:T(1024)S(1)}, u32[]{:S(2)}) copy-start(f32[680]{0:T(1024)S(1)} %multiply_reduce_fusion.20) | copy-start | bytes 8164 | tf_op jit(solution)/shard_map/while
  47.0 9.6 %copy-start.31 = (bf16[1024,256]{1,0:T(8,128)(2,1)S(1)}, bf16[1024,256]{1,0:T(8,128)(2,1)}, u32[]{:S(2)}) copy-start(bf16[1024,256]{1,0:T(8,128)(2,1)} %get-tuple-element.1123) | copy-start | bytes 1572868 | tf_op jit(solution)/shard_map/while
  77.8 7.4 %copy-start.62 = (f32[680]{0:T(1024)}, f32[680]{0:T(1024)S(1)}, u32[]{:S(2)}) copy-start(f32[680]{0:T(1024)S(1)} %multiply_reduce_fusion.21) | copy-start | bytes 8164 | tf_op jit(solution)/shard_map/while
  77.8 7.3 %copy-start.55 = (f32[680]{0:T(1024)}, f32[680]{0:T(1024)S(1)}, u32[]{:S(2)}) copy-start(f32[680]{0:T(1024)S(1)} %fusion.348) | copy-start | bytes 8164 | tf_op jit(solution)/shard_map/while
  77.8 7.3 %copy-start.7 = (bf16[680,256]{1,0:T(8,128)(2,1)S(1)}, bf16[680,256]{1,0:T(8,128)(2,1)}, u32[]{:S(2)}) copy-start(bf16[680,256]{1,0:T(8,128)(2,1)} %reshape.539) | copy-start | bytes 1044484 | tf_op jit(solution)/shard_map/while
  77.8 7.3 %copy-start.30 = (bf16[1024,256]{1,0:T(8,128)(2,1)S(1)}, bf16[1024,256]{1,0:T(8,128)(2,1)}, u32[]{:S(2)}) copy-start(bf16[1024,256]{1,0:T(8,128)(2,1)} %get-tuple-element.1129) | copy-start | bytes 1572868 | tf_op jit(solution)/shard_map/while
  121.5 11.4 %copy-start.5 = (bf16[680,256]{1,0:T(8,128)(2,1)}, bf16[680,256]{1,0:T(8,128)(2,1)S(1)}, u32[]{:S(2)}) copy-start(bf16[680,256]{1,0:T(8,128)(2,1)S(1)} %get-tuple-element.998) | copy-start | bytes 1044484 | tf_op jit(solution)/shard_map/while
  156.7 7.8 %copy-start.85 = (s32[4,340]{1,0:T(4,128)}, s32[4,340]{1,0:T(4,128)S(1)}, u32[]{:S(2)}) copy-start(s32[4,340]{1,0:T(4,128)S(1)} %get-tuple-element.1118) | copy-start | bytes 16324 | tf_op jit(solution)/shard_map/while
  156.7 8.8 %copy-start.38 = (bf16[256,768]{1,0:T(8,128)(2,1)}, bf16[256,768]{1,0:T(8,128)(2,1)S(1)}, u32[]{:S(2)}) copy-start(bf16[256,768]{1,0:T(8,128)(2,1)S(1)} %get-tuple-element.1117) | copy-start | bytes 1179652 | tf_op jit(solution)/shard_map/while
  184.2 9.3 %copy-start.3 = (bf16[680,256]{0,1:T(8,128)(2,1)}, bf16[680,256]{0,1:T(8,128)(2,1)S(1)}, u32[]{:S(2)}) copy-start(bf16[680,256]{0,1:T(8,128)(2,1)S(1)} %reshape.536) | copy-start | bytes 1044484 | tf_op jit(solution)/shard_map/while
  184.9 8.5 %copy-start.58 = (f32[680]{0:T(1024)}, f32[680]{0:T(1024)S(1)}, u32[]{:S(2)}) copy-start(f32[680]{0:T(1024)S(1)} %multiply_reduce_fusion.20) | copy-start | bytes 8164 | tf_op jit(solution)/shard_map/while
  185.0 9.6 %copy-start.31 = (bf16[1024,256]{1,0:T(8,128)(2,1)S(1)}, bf16[1024,256]{1,0:T(8,128)(2,1)}, u32[]{:S(2)}) copy-start(bf16[1024,256]{1,0:T(8,128)(2,1)} %get-tuple-element.1123) | copy-start | bytes 1572868 | tf_op jit(solution)/shard_map/while
  215.7 7.4 %copy-start.62 = (f32[680]{0:T(1024)}, f32[680]{0:T(1024)S(1)}, u32[]{:S(2)}) copy-start(f32[680]{0:T(1024)S(1)} %multiply_reduce_fusion.21) | copy-start | bytes 8164 | tf_op jit(solution)/shard_map/while
  215.7 7.3 %copy-start.55 = (f32[680]{0:T(1024)}, f32[680]{0:T(1024)S(1)}, u32[]{:S(2)}) copy-start(f32[680]{0:T(1024)S(1)} %fusion.348) | copy-start | bytes 8164 | tf_op jit(solution)/shard_map/while
  215.7 7.3 %copy-start.7 = (bf16[680,256]{1,0:T(8,128)(2,1)S(1)}, bf16[680,256]{1,0:T(8,128)(2,1)}, u32[]{:S(2)}) copy-start(bf16[680,256]{1,0:T(8,128)(2,1)} %reshape.539) | copy-start | bytes 1044484 | tf_op jit(solution)/shard_map/while
  215.8 7.3 %copy-start.30 = (bf16[1024,256]{1,0:T(8,128)(2,1)S(1)}, bf16[1024,256]{1,0:T(8,128)(2,1)}, u32[]{:S(2)}) copy-start(bf16[1024,256]{1,0:T(8,128)(2,1)} %get-tuple-element.1129) | copy-start | bytes 1572868 | tf_op jit(solution)/shard_map/while
  260.7 12.0 %copy-start.5 = (bf16[680,256]{1,0:T(8,128)(2,1)}, bf16[680,256]{1,0:T(8,128)(2,1)S(1)}, u32[]{:S(2)}) copy-start(bf16[680,256]{1,0:T(8,128)(2,1)S(1)} %get-tuple-element.998) | copy-start | bytes 1044484 | tf_op jit(solution)/shard_map/while
  306.6 45.3 %collective-permute-start.6 = (bf16[4,340,256]{2,0,1:T(4,128)(2,1)}, bf16[4,340,256]{2,0,1:T(4,128)(2,1)}, u32[]{:S(2)}, u32[]{:S(2)}) collective-permute-start(bf16[4,340,256]{2,0,1:T(4,128)(2,1)} %copy.99), channel_id=1, source_target_pairs={{0,16},{16,0},{1,17},{17,1},{2,18},{18,2},{3,19},{19,3},{4,20},{20... | collective-permute-start | bytes 2088968 | tf_op jit(solution)/shard_map/ppermute | solution.py:18
  307.0 47.7 %collective-permute-start.7 = (bf16[4,340,256]{2,0,1:T(4,128)(2,1)}, bf16[4,340,256]{2,0,1:T(4,128)(2,1)}, u32[]{:S(2)}, u32[]{:S(2)}) collective-permute-start(bf16[4,340,256]{2,0,1:T(4,128)(2,1)} %copy.101), channel_id=1, source_target_pairs={{0,16},{16,0},{1,17},{17,1},{2,18},{18,2},{3,19},{19,3},{4,20},{20... | collective-permute-start | bytes 2088968 | tf_op jit(solution)/shard_map/ppermute | solution.py:18
  (175 other events, 521.6 us)
Sparse Core Ops, SparseCore 0:
  302.3 162.9 all-reduce.3
where the time goes:
time: 483 us; the launch traced here: 479 us
  matrix products  157 us (33%)
  local copies, waits for them, and re-layouts  108 us (22%)
  waiting for transfers between devices  107 us (22%)
  blocking collectives  43.4 us (9%)
  other arithmetic  37.9 us (8%)
  between operations  14.5 us (3%)
  loops' own time  8.67 us (2%)
    psum x1, waiting for transfers between devices, split_plan(): lax.psum((totals_first[0], totals_first[1], totals_first[2], totals_first...  107 us
    psum x1, blocking collectives, split_plan(): lax.psum((totals_first[0], totals_first[1], totals_first[2], totals_first...  43.4 us
    dot_general x4, matrix products, layer_parts(): upper = jnp.dot(normed_mlp, weight_up, preferred_element_type=jnp.float32)  31.6 us
    while x372, local copies, waits for them, and re-layouts  25.2 us
    convert_element_type x6, local copies, waits for them, and re-layouts, layer_backward(): d_packed = jnp.stack([d_query, d_key, d_value], axis=2).reshape(count * l...  18.7 us
    sub x4, matrix products, softmax_rows(): expo = jnp.exp(scores - highest)  17.3 us
    dot_general x4, matrix products, layer_backward(): jnp.einsum('bqhd,bkhd->bhqk', d_mixed, value, preferred_element_type=jnp....  13.8 us
    dot_general x4, matrix products, layer_backward(): jnp.einsum('bhqk,bqhd->bkhd', probs_low, d_mixed, preferred_element_type=...  12.4 us
  transfers between devices with their start and end apart: 9, of which 1 were waited for; matrix products, arithmetic and copies ran while one was open for 4% of the time, Pallas kernels for 0%

commit v1 on v0

v1 whole, which is shorter than its diff:
```python
import jax
import jax.numpy as jnp
from jax import lax
from jax.experimental import pallas as pl
from jax.experimental.pallas import tpu as pltpu
from jax.sharding import PartitionSpec as P

D = 256
FF = 1024
FRAME = 17
LP = 352
EPS = 1e-05
BIG = -(2.0**100)
BLOCKS = ((0, 112, 0, 128), (112, 240, 0, 256), (240, 304, 64, 320), (304, 352, 96, 352))
ERF = (7.97884531e-01, 3.63337968e-02, -3.28609901e-05, -5.53091310e-05, 3.97786435e-06, -1.33973644e-07, 1.81750064e-09)
F32 = jnp.float32
BF = jnp.bfloat16


def mm(a, b):
    return jnp.dot(a, b, preferred_element_type=F32)


def mm_t(a, b):
    return lax.dot_general(a, b, (((1,), (1,)), ((), ())), preferred_element_type=F32)


def tmm(a, b):
    return lax.dot_general(a, b, (((0,), (0,)), ((), ())), preferred_element_type=F32)


def norm_stats(x):
    mean = jnp.sum(x, axis=-1, keepdims=True) * (1.0 / D)
    center = x - mean
    var = jnp.sum(center * center, axis=-1, keepdims=True) * (1.0 / D)
    rstd = lax.rsqrt(var + EPS)
    return center * rstd, rstd


def norm_back(d_out, gain, xhat, rstd):
    dy = d_out * gain
    s1 = jnp.sum(dy, axis=-1, keepdims=True) * (1.0 / D)
    s2 = jnp.sum(dy * xhat, axis=-1, keepdims=True) * (1.0 / D)
    return rstd * (dy - s1 - xhat * s2)


def gain_rows(d_out, xhat):
    prod = d_out * xhat
    return jnp.sum(prod.reshape(LP // 8, 8, D), axis=0)


def gelu_pair(u):
    u2 = u * u
    p = jnp.full_like(u, ERF[-1])
    for c in ERF[-2::-1]:
        p = p * u2 + c
    cdf = 0.5 + 0.5 * jnp.tanh(u * p)
    pdf = 0.3989422804014327 * jnp.exp(-0.5 * u2)
    return u * cdf, cdf + u * pdf


def two_heads(block, lane_low):
    zero = jnp.zeros_like(block)
    return jnp.concatenate(
        [jnp.where(lane_low, block, zero), jnp.where(lane_low, zero, block)], axis=0
    )


def one_pair(stacked, n, lane_low):
    return jnp.where(lane_low, stacked[:n], stacked[n:])


def kernel(
    x_ref, cot_ref, eq_ref, ek_ref, wqkv_ref, wout_ref, wup_ref, wdown_ref, gains_ref,
    y_ref, d_ref, grads_ref,
    hid_ref, xhat1_ref, rstd1_ref, xhat2_ref, rstd2_ref, a_ref, b_ref, o_ref, qs_ref, ke_ref,
    v1_ref, p_ref, m_ref, gp_ref, h_ref, dup_ref, up_ref, do_ref, dqkv_ref, dk_ref, dv_ref,
    aqkv_ref, aout_ref, aup_ref, adown_ref, again_ref,
):
    step = pl.program_id(0)
    last = pl.num_programs(0) - 1

    @pl.when(step == 0)
    def _():
        for ref in (aqkv_ref, aout_ref, aup_ref, adown_ref, again_ref):
            ref[...] = jnp.zeros_like(ref)

    eq = eq_ref[0]
    ek = ek_ref[0]

    def low_mask(n):
        return lax.broadcasted_iota(jnp.int32, (n, 128), 1) < 64

    def forward(l, x):
        xhat, rstd = norm_stats(x)
        xhat1_ref[l] = xhat
        rstd1_ref[l] = jnp.broadcast_to(rstd, (LP, 128))
        a = (xhat * gains_ref[l, 0:1, :]).astype(BF)
        a_ref[l] = a
        for p in range(2):
            qs = (mm(a, wqkv_ref[l, :, 128 * p : 128 * p + 128])).astype(BF) * jnp.array(0.125, BF)
            for q0, q1, _, _ in BLOCKS:
                qs_ref[l, p, 2 * q0 : 2 * q1, 0:128] = two_heads(qs[q0:q1], low_mask(q1 - q0))
                qs_ref[l, p, 2 * q0 : 2 * q1, 128:256] = jnp.concatenate([eq[q0:q1], eq[q0:q1]], axis=0)
            ke_ref[l, p, :, 0:128] = mm(a, wqkv_ref[l, :, 256 + 128 * p : 384 + 128 * p]).astype(BF)
            ke_ref[l, p, :, 128:256] = ek
            v1_ref[l, p, :, 0:128] = mm(a, wqkv_ref[l, :, 512 + 128 * p : 640 + 128 * p]).astype(BF)
            v1_ref[l, p, :, 128:256] = jnp.ones((LP, 128), BF)
        for p in range(2):
            for q0, q1, k0, k1 in BLOCKS:
                n = q1 - q0
                s = mm_t(qs_ref[l, p, 2 * q0 : 2 * q1, :], ke_ref[l, p, k0:k1, :])
                e = jnp.exp(s - jnp.max(s, axis=-1, keepdims=True))
                prob = (e * (1.0 / jnp.sum(e, axis=-1, keepdims=True))).astype(BF)
                p_ref[l, p, 2 * q0 : 2 * q1, 0 : k1 - k0] = prob
                o = mm(prob, v1_ref[l, p, k0:k1, 0:128])
                o_ref[l, q0:q1, 128 * p : 128 * p + 128] = one_pair(o, n, low_mask(n)).astype(BF)
        h = x + mm(o_ref[l], wout_ref[l])
        xhat, rstd = norm_stats(h)
        xhat2_ref[l] = xhat
        rstd2_ref[l] = jnp.broadcast_to(rstd, (LP, 128))
        b = (xhat * gains_ref[l, 1:2, :]).astype(BF)
        b_ref[l] = b
        y = h
        for c in range(4):
            cols = slice(256 * c, 256 * c + 256)
            m, gp = gelu_pair(mm(b, wup_ref[l, :, cols]))
            m = m.astype(BF)
            m_ref[l, :, cols] = m
            gp_ref[l, :, cols] = gp.astype(BF)
            y = y + mm(m, wdown_ref[l, cols, :])
        return y

    def backward(l, g):
        gb = g.astype(BF)
        d_b = jnp.zeros((LP, D), F32)
        b = b_ref[l]
        for c in range(4):
            cols = slice(256 * c, 256 * c + 256)
            du = (mm_t(gb, wdown_ref[l, cols, :]) * gp_ref[l, :, cols].astype(F32)).astype(BF)
            adown_ref[l, :, cols] += tmm(gb, m_ref[l, :, cols])
            aup_ref[l, :, cols] += tmm(b, du)
            d_b = d_b + mm_t(du, wup_ref[l, :, cols])
        xhat = xhat2_ref[l]
        again_ref[l, 1] += gain_rows(d_b, xhat)
        d_h = g + norm_back(d_b, gains_ref[l, 1:2, :], xhat, rstd2_ref[l, :, 0:1])
        d_hb = d_h.astype(BF)
        o = o_ref[l]
        aout_ref[l] += tmm(o, d_hb)
        d_o = mm_t(d_hb, wout_ref[l]).astype(BF)
        prod = (-(d_o.astype(F32) * o.astype(F32))).astype(BF)
        for p in range(2):
            lanes = slice(128 * p, 128 * p + 128)
            for q0, q1, _, _ in BLOCKS:
                mask = low_mask(q1 - q0)
                do_ref[p, 2 * q0 : 2 * q1, 0:128] = two_heads(d_o[q0:q1, lanes], mask)
                do_ref[p, 2 * q0 : 2 * q1, 128:256] = two_heads(prod[q0:q1, lanes], mask)
        for p in range(2):
            dk_ref[...] = jnp.zeros_like(dk_ref)
            dv_ref[...] = jnp.zeros_like(dv_ref)
            for q0, q1, k0, k1 in BLOCKS:
                n = q1 - q0
                rows = slice(2 * q0, 2 * q1)
                dp = mm_t(do_ref[p, rows, :], v1_ref[l, p, k0:k1, :])
                prob = p_ref[l, p, rows, 0 : k1 - k0]
                ds = (prob.astype(F32) * dp).astype(BF)
                dq = mm(ds, ke_ref[l, p, k0:k1, 0:128])
                dqkv_ref[q0:q1, 128 * p : 128 * p + 128] = (one_pair(dq, n, low_mask(n)) * 0.125).astype(BF)
                dv_ref[k0:k1, :] += tmm(prob, do_ref[p, rows, 0:128])
                dk_ref[k0:k1, :] += tmm(ds, qs_ref[l, p, rows, 0:128])
            dqkv_ref[:, 256 + 128 * p : 384 + 128 * p] = dk_ref[...].astype(BF)
            dqkv_ref[:, 512 + 128 * p : 640 + 128 * p] = dv_ref[...].astype(BF)
        d_qkv = dqkv_ref[...]
        aqkv_ref[l] += tmm(a_ref[l], d_qkv)
        d_a = mm_t(d_qkv, wqkv_ref[l])
        xhat = xhat1_ref[l]
        again_ref[l, 0] += gain_rows(d_a, xhat)
        return d_h + norm_back(d_a, gains_ref[l, 0:1, :], xhat, rstd1_ref[l, :, 0:1])

    y0 = forward(0, x_ref[0].astype(F32)).astype(BF)
    y_ref[0, 0] = y0
    y1 = forward(1, y0.astype(F32)).astype(BF)
    y_ref[1, 0] = y1
    d1 = backward(1, cot_ref[0].astype(F32)).astype(BF)
    d_ref[1, 0] = d1
    d0 = backward(0, d1.astype(F32)).astype(BF)
    d_ref[0, 0] = d0

    @pl.when(step == last)
    def _():
        for l in range(2):
            for j in range(3):
                grads_ref[l, 256 * j : 256 * j + 256, :] = aqkv_ref[l, :, 256 * j : 256 * j + 256].astype(BF)
            grads_ref[l, 768:1024, :] = aout_ref[l].astype(BF)
            for j in range(4):
                cols = slice(256 * j, 256 * j + 256)
                grads_ref[l, 1024 + 256 * j : 1280 + 256 * j, :] = aup_ref[l, :, cols].astype(BF)
                grads_ref[l, 2048 + 256 * j : 2304 + 256 * j, :] = adown_ref[l, :, cols].T.astype(BF)
            row = lax.broadcasted_iota(jnp.int32, (16, D), 0)
            attn = jnp.sum(again_ref[l, 0], axis=0, keepdims=True)
            mlp = jnp.sum(again_ref[l, 1], axis=0, keepdims=True)
            grads_ref[l, 3072:3088, :] = jnp.where(row == 0, attn, jnp.where(row == 1, mlp, 0.0)).astype(BF)


def local_step(x, cot, eq, ek, wqkv, wout, wup, wdown, gains):
    rows = x.shape[0]
    tok = lambda w: pl.BlockSpec((1, LP, w), lambda i: (i, 0, 0))
    whole = lambda a: pl.BlockSpec(a.shape, lambda i: (0,) * a.ndim, pipeline_mode=pl.Buffered(1))
    out_tok = pl.BlockSpec((2, 1, LP, D), lambda i: (0, i, 0, 0))
    vm = pltpu.VMEM
    return pl.pallas_call(
        kernel,
        grid=(rows,),
        in_specs=[tok(D), tok(D), tok(128), tok(128)] + [whole(a) for a in (wqkv, wout, wup, wdown, gains)],
        out_specs=[out_tok, out_tok, pl.BlockSpec((2, 3088, D), lambda i: (0, 0, 0), pipeline_mode=pl.Buffered(1))],
        out_shape=[
            jax.ShapeDtypeStruct((2, rows, LP, D), BF),
            jax.ShapeDtypeStruct((2, rows, LP, D), BF),
            jax.ShapeDtypeStruct((2, 3088, D), BF),
        ],
        scratch_shapes=[
            vm((LP, D), F32),
            vm((2, LP, D), F32), vm((2, LP, 128), F32), vm((2, LP, D), F32), vm((2, LP, 128), F32),
            vm((2, LP, D), BF), vm((2, LP, D), BF), vm((2, LP, D), BF),
            vm((2, 2, 2 * LP, D), BF), vm((2, 2, LP, D), BF), vm((2, 2, LP, D), BF),
            vm((2, 2, 2 * LP, D), BF), vm((2, LP, FF), BF), vm((2, LP, FF), BF),
            vm((LP, D), F32), vm((LP, D), F32), vm((LP, D), F32),
            vm((2, 2 * LP, D), BF), vm((LP, 3 * D), BF), vm((LP, 128), F32), vm((LP, 128), F32),
            vm((2, D, 3 * D), F32), vm((2, D, D), F32), vm((2, D, FF), F32), vm((2, D, FF), F32), vm((2, 2, 8, D), F32),
        ],
        compiler_params=pltpu.CompilerParams(
            dimension_semantics=("arbitrary",), vmem_limit_bytes=60 * 1024 * 1024
        ),
    )(x, cot, eq, ek, wqkv, wout, wup, wdown, gains)


def codes(segments):
    rows, length = segments.shape
    seg = jnp.pad(segments, ((0, 0), (0, LP - length)), constant_values=-1)[:, :, None]
    frame = (lax.iota(jnp.int32, LP) // FRAME)[None, :, None]
    lane = lax.iota(jnp.int32, 128)[None, None, :]
    eq = jnp.where(lane < 64, frame == lane, seg == lane - 64)
    ek = jnp.where(lane < 64, frame > lane, (seg != lane - 64) & (lane < 68))
    return eq.astype(BF), jnp.where(ek, BIG, 0.0).astype(BF)


def partner(value):
    return lax.ppermute(value, "section", [(0, 1), (1, 0)])


def cross(value, count, bits):
    pairs = [(s * count + i, s * count + (i ^ (1 << bits[s]))) for s in range(2) for i in range(count)]
    return lax.ppermute(value, ("section", "dp"), pairs)


def add(a, b):
    return (a.astype(F32) + b.astype(F32)).astype(BF)


def sum_over_dp(main, extra, section):
    count = lax.axis_size("dp")
    place = lax.axis_index("dp")
    depth = count.bit_length() - 1
    orders = [(i, i) for i in range(depth)]
    if depth > 1:
        orders[0], orders[1] = (0, 1), (1, 0)
    uppers = []
    for bits in orders:
        upper = jnp.where(section == 0, place >> bits[0], place >> bits[1]) & 1
        uppers.append(upper)
        half = main.shape[0] // 2
        send = lax.dynamic_slice_in_dim(main, (1 - upper) * half, half, 0)
        got = cross(jnp.concatenate([send, extra], axis=0), count, bits)
        main = add(lax.dynamic_slice_in_dim(main, upper * half, half, 0), got[:half])
        extra = add(extra, got[half:])
    for bits, upper in zip(orders[::-1], uppers[::-1]):
        got = cross(main, count, bits)
        main = jnp.where(
            upper == 0, jnp.concatenate([main, got], axis=0), jnp.concatenate([got, main], axis=0)
        )
    return main, extra


def shards(
    layer_input, out_cotangent, segment_ids, gain_attn, weight_qkv, weight_out, gain_mlp, weight_up, weight_down
):
    section = lax.axis_index("section")
    first = section == 0
    rows, length, width = layer_input.shape
    half = rows // 2

    def both(mine):
        theirs = partner(mine)
        return jnp.concatenate([jnp.where(first, mine, theirs), jnp.where(first, theirs, mine)], axis=0)

    gains = both(jnp.stack([gain_attn, gain_mlp], axis=1)).astype(F32)
    weights = [both(w) for w in (weight_qkv, weight_out, weight_up, weight_down)]
    pad = ((0, 0), (0, LP - length), (0, 0))
    mine = lambda a: lax.dynamic_slice_in_dim(a, section * half, half, 0)
    eq, ek = codes(mine(segment_ids))
    y, d, grads = local_step(
        jnp.pad(mine(layer_input), pad), jnp.pad(mine(out_cotangent), pad), eq, ek, *weights, gains
    )

    def split(a):
        take = lambda j: lax.dynamic_index_in_dim(a, j, 0, False)
        return take(section), take(1 - section)

    keep_g, send_g = split(grads)
    keep_y, send_y = split(y[:, :, :length])
    keep_d, send_d = split(d[:, :, :length])
    total = add(keep_g, partner(send_g))
    main, extra = sum_over_dp(total[:3072], total[3072:], section)

    def whole_rows(keep, send):
        got = partner(send)
        return jnp.where(
            first, jnp.concatenate([keep, got], axis=0), jnp.concatenate([got, keep], axis=0)
        )

    activations = whole_rows(keep_y, send_y)
    input_grads = whole_rows(keep_d, send_d).astype(F32)
    main = main.astype(F32)
    extra = extra.astype(F32)
    side = lambda first_row, n: jnp.concatenate(
        [main[first_row + D * j : first_row + D * j + D] for j in range(n)], axis=1
    )
    return (
        activations[None],
        input_grads[None],
        side(0, 3)[None],
        main[768:1024][None],
        side(1024, 4)[None],
        main[2048:3072][None],
        extra[0][None],
        extra[1][None],
    )


def solution(mesh):
    placed = (
        P("dp", None, None),
        P("dp", None, None),
        P("dp", None),
        P("section", None),
        P("section", None, None),
        P("section", None, None),
        P("section", None),
        P("section", None, None),
        P("section", None, None),
    )
    return jax.shard_map(
        shards,
        mesh=mesh,
        in_specs=placed,
        out_specs=(
            P("section", "dp", None, None),
            P("section", "dp", None, None),
            P("section", None, None),
            P("section", None, None),
            P("section", None, None),
            P("section", None, None),
            P("section", None),
            P("section", None),
        ),
        check_vma=False,
    )
```

time: 483 us -> 163 us (0.34)
  matrix products: 157 us -> 0 us
  local copies, waits for them, and re-layouts: 108 us -> 19.3 us
  waiting for transfers between devices: 107 us -> 39.4 us
  Pallas kernels: 0 us -> 64.5 us
  blocking collectives: 43.4 us -> 0 us
  other arithmetic: 37.9 us -> 14.2 us
  starting transfers between devices: 2.27 us -> 23.1 us
  between operations: 14.5 us -> 0.99 us
  loops' own time: 8.67 us -> 0 us
    dot_general x68 -> x0, matrix products: 139 us -> none  [the longest x4 31.6 us: layer_parts(): upper = jnp.dot(normed_mlp, weight_up, preferred_element_type=jnp.float32)]
    psum x1 -> x0, waiting for transfers between devices: 107 us -> none  [split_plan(): lax.psum((totals_first[0], totals_first[1], totals_first[2], totals_first...]
    pallas_call x0 -> x1, Pallas kernels: none -> 64.5 us  [local_step(): pl.pallas_call(kernel, grid=(rows,), in_specs=[tok(D), tok(D), tok(128),...]
    psum x1 -> x0, blocking collectives: 43.4 us -> none  [split_plan(): lax.psum((totals_first[0], totals_first[1], totals_first[2], totals_first...]
    ppermute x8 -> x16, waiting for transfers between devices: 0.02 us -> 39.4 us  [the longest x8 36.1 us: cross(): return lax.ppermute(value, ('section', 'dp'), pairs)]
    convert_element_type x17 -> x0, local copies, waits for them, and re-layouts: 26.2 us -> none  [the longest x6 18.7 us: layer_backward(): d_packed = jnp.stack([d_query, d_key, d_value], axis=2).reshape(count * l...]
    while x372 -> x0, local copies, waits for them, and re-layouts: 25.2 us -> none
    ppermute x8 -> x16, starting transfers between devices: 2.23 us -> 23.1 us  [the longest x8 21.4 us: cross(): return lax.ppermute(value, ('section', 'dp'), pairs)]
  transfers between devices with their start and end apart: 9 -> 16, of which waited for: 1 -> 9; matrix products, arithmetic and copies ran while one was open for 4% -> 13% of each run, Pallas kernels for 0% -> 0%
where the time goes in v1:
time: 163 us; the launch traced here: 162 us
  Pallas kernels  64.5 us (40%)
  waiting for transfers between devices  39.4 us (24%)
  starting transfers between devices  23.1 us (14%)
  local copies, waits for them, and re-layouts  19.3 us (12%)
  other arithmetic  14.2 us (9%)
    pallas_call x1, Pallas kernels, local_step(): pl.pallas_call(kernel, grid=(rows,), in_specs=[tok(D), tok(D), tok(128),...  64.5 us
    ppermute x8, waiting for transfers between devices, cross(): return lax.ppermute(value, ('section', 'dp'), pairs)  36.1 us
    ppermute x8, starting transfers between devices, cross(): return lax.ppermute(value, ('section', 'dp'), pairs)  21.4 us
    unnamed x26, local copies, waits for them, and re-layouts  5.1 us
    concatenate x4, other arithmetic, both(): jnp.concatenate([jnp.where(first, mine, theirs), jnp.where(first, theirs,...  3.8 us
    squeeze x3, local copies, waits for them, and re-layouts, split(): take = lambda j: lax.dynamic_index_in_dim(a, j, 0, False)  3.76 us
    ppermute x8, waiting for transfers between devices, partner(): return lax.ppermute(value, 'section', [(0, 1), (1, 0)])  3.36 us
  transfers between devices with their start and end apart: 16, of which 9 were waited for; matrix products, arithmetic and copies ran while one was open for 13% of the time, Pallas kernels for 0%

profile of v1, /device:TPU:0, one launch (start us, length us, event | category | flops | bytes accessed | tf_op | source)
XLA Modules:
  0.0 161.5 jit_solution(15425131913042895802)
XLA Ops:
  5.1 2.5 %constant_dynamic-slice_fusion.7 = (bf16[4,340,256]{2,0,1:T(4,128)(2,1)S(1)}, bf16[4,340,256]{2,0,1:T(4,128)(2,1)S(1)}) fusion(bf16[8,340,256]{2,0,1:T(8,128)(2,1)} %param.10, s32[]{:T(128)S(6)} %select_n.191, bf16[8,340,256]{2,0,1:T(8,128)(2,1)} %param.9), kind=kLoop, calls=%fused_computation.55 | loop fusion | bytes 2785284 | tf_op jit(solution)/shard_map/dynamic_slice | solution.py:299
  12.2 1.1 pad_maximum_fusion.wup_ref
  13.4 1.1 pad_maximum_fusion.1.wdown_ref
  14.4 64.5 %shard_map.152 = (bf16[2,4,352,256]{3,2,1,0:T(8,128)(2,1)}, bf16[2,4,352,256]{3,2,1,0:T(8,128)(2,1)}, bf16[2,3088,256]{2,1,0:T(8,128)(2,1)}) custom-call(bf16[4,352,256]{2,1,0:T(8,128)(2,1)} %pad.11.x_ref, bf16[4,352,256]{2,1,0:T(8,128)(2,1)} %pad.12.cot_ref, bf16[4,352,128]{2,1,0:T(8,128)(2,1)} %select_convert_fusion.1.eq_ref, ...), custom_call_target="tpu_custom_call" | custom-call | tf_op jit(solution)/shard_map/pallas_call | solution.py:211
  78.9 1.5 dynamic-slice_bitcast_fusion
  80.6 3.3 %collective-permute-done.7 = bf16[3088,256]{1,0:T(8,128)(2,1)S(1)} collective-permute-done((bf16[3088,256]{1,0:T(8,128)(2,1)S(1)}, bf16[3088,256]{1,0:T(8,128)(2,1)S(1)}, u32[]{:S(2)}, u32[]{:S(2)}) %collective-permute-start.7) | collective-permute-done | bytes 1581088 | tf_op jit(solution)/shard_map/ppermute | solution.py:248
  83.9 1.9 %fusion = bf16[3088,256]{1,0:T(8,128)(2,1)S(1)} fusion(bf16[3088,256]{1,0:T(8,128)(2,1)S(1)} %collective-permute-done.7, bf16[2,3088,256]{2,1,0:T(8,128)(2,1)} %get-tuple-element.13, s32[]{:T(128)S(6)} %select_n.211), kind=kLoop, calls=%fused_computation.1 | loop fusion | flops 3162112 | bytes 4743172 | tf_op jit(solution)/shard_map/convert_element_type | solution.py:257
  85.9 1.0 copy-done.1
  88.6 2.6 %collective-permute-start.8 = (bf16[1552,256]{1,0:T(8,128)(2,1)}, bf16[1552,256]{1,0:T(8,128)(2,1)S(1)}, u32[]{:S(2)}, u32[]{:S(2)}) collective-permute-start(bf16[1552,256]{1,0:T(8,128)(2,1)} %pad_maximum_fusion.2), channel_id=1, source_target_pairs={{0,1},{1,0},{2,3},{3,2},{4,5},{5,4},{6,7},{7,6},{8,9},{9,8},{10,11... | collective-permute-start | bytes 2383880 | tf_op jit(solution)/shard_map/ppermute | solution.py:253
  91.2 10.3 %collective-permute-done.8 = bf16[1552,256]{1,0:T(8,128)(2,1)S(1)} collective-permute-done((bf16[1552,256]{1,0:T(8,128)(2,1)}, bf16[1552,256]{1,0:T(8,128)(2,1)S(1)}, u32[]{:S(2)}, u32[]{:S(2)}) %collective-permute-start.8) | collective-permute-done | bytes 794656 | tf_op jit(solution)/shard_map/ppermute | solution.py:253
  101.8 2.1 %collective-permute-start.9 = (bf16[784,256]{1,0:T(8,128)(2,1)S(1)}, bf16[784,256]{1,0:T(8,128)(2,1)S(1)}, u32[]{:S(2)}, u32[]{:S(2)}) collective-permute-start(bf16[784,256]{1,0:T(8,128)(2,1)S(1)} %pad_maximum_fusion.4), channel_id=1, source_target_pairs={{0,2},{1,3},{2,0},{3,1},{4,6},{5,7},{6,4},{7,5},{8,10},{9,11},{10,... | collective-permute-start | bytes 1204232 | tf_op jit(solution)/shard_map/ppermute | solution.py:253
  103.9 5.8 %collective-permute-done.9 = bf16[784,256]{1,0:T(8,128)(2,1)S(1)} collective-permute-done((bf16[784,256]{1,0:T(8,128)(2,1)S(1)}, bf16[784,256]{1,0:T(8,128)(2,1)S(1)}, u32[]{:S(2)}, u32[]{:S(2)}) %collective-permute-start.9) | collective-permute-done | bytes 401440 | tf_op jit(solution)/shard_map/ppermute | solution.py:253
  110.0 2.1 %collective-permute-start.10 = (bf16[400,256]{1,0:T(8,128)(2,1)S(1)}, bf16[400,256]{1,0:T(8,128)(2,1)S(1)}, u32[]{:S(2)}, u32[]{:S(2)}) collective-permute-start(bf16[400,256]{1,0:T(8,128)(2,1)S(1)} %pad_maximum_fusion.6), channel_id=1, source_target_pairs={{0,4},{1,5},{2,6},{3,7},{4,0},{5,1},{6,2},{7,3},{8,12},{9,13},{10,... | collective-permute-start | bytes 614408 | tf_op jit(solution)/shard_map/ppermute | solution.py:253
  112.1 3.9 %collective-permute-done.10 = bf16[400,256]{1,0:T(8,128)(2,1)S(1)} collective-permute-done((bf16[400,256]{1,0:T(8,128)(2,1)S(1)}, bf16[400,256]{1,0:T(8,128)(2,1)S(1)}, u32[]{:S(2)}, u32[]{:S(2)}) %collective-permute-start.10) | collective-permute-done | bytes 204832 | tf_op jit(solution)/shard_map/ppermute | solution.py:253
  116.1 2.9 %collective-permute-start.11 = (bf16[208,256]{1,0:T(8,128)(2,1)S(1)}, bf16[208,256]{1,0:T(8,128)(2,1)S(1)}, u32[]{:S(2)}, u32[]{:S(2)}) collective-permute-start(bf16[208,256]{1,0:T(8,128)(2,1)S(1)} %pad_maximum_fusion.7), channel_id=1, source_target_pairs={{0,8},{1,9},{2,10},{3,11},{4,12},{5,13},{6,14},{7,15},{8,0},{9,1},... | collective-permute-start | bytes 319496 | tf_op jit(solution)/shard_map/ppermute | solution.py:253
  119.1 2.7 %collective-permute-done.11 = bf16[208,256]{1,0:T(8,128)(2,1)S(1)} collective-permute-done((bf16[208,256]{1,0:T(8,128)(2,1)S(1)}, bf16[208,256]{1,0:T(8,128)(2,1)S(1)}, u32[]{:S(2)}, u32[]{:S(2)}) %collective-permute-start.11) | collective-permute-done | bytes 106528 | tf_op jit(solution)/shard_map/ppermute | solution.py:253
  121.8 3.0 %collective-permute-start.12 = (bf16[192,256]{1,0:T(8,128)(2,1)S(1)}, bf16[192,256]{1,0:T(8,128)(2,1)S(1)}, u32[]{:S(2)}, u32[]{:S(2)}) collective-permute-start(bf16[192,256]{1,0:T(8,128)(2,1)S(1)} %add_convert_fusion.3), channel_id=1, source_target_pairs={{0,8},{1,9},{2,10},{3,11},{4,12},{5,13},{6,14},{7,15},{8,0},{9,1},... | collective-permute-start | bytes 294920 | tf_op jit(solution)/shard_map/ppermute | solution.py:253
  124.9 2.8 %collective-permute-done.12 = bf16[192,256]{1,0:T(8,128)(2,1)S(1)} collective-permute-done((bf16[192,256]{1,0:T(8,128)(2,1)S(1)}, bf16[192,256]{1,0:T(8,128)(2,1)S(1)}, u32[]{:S(2)}, u32[]{:S(2)}) %collective-permute-start.12) | collective-permute-done | bytes 98336 | tf_op jit(solution)/shard_map/ppermute | solution.py:253
  127.8 5.4 %collective-permute-start.13 = (bf16[384,256]{1,0:T(8,128)(2,1)S(1)}, bf16[384,256]{1,0:T(8,128)(2,1)S(1)}, u32[]{:S(2)}, u32[]{:S(2)}) collective-permute-start(bf16[384,256]{1,0:T(8,128)(2,1)S(1)} %maximum_select_fusion.5), channel_id=1, source_target_pairs={{0,4},{1,5},{2,6},{3,7},{4,0},{5,1},{6,2},{7,3},{8,12},{9,13},{10,... | collective-permute-start | bytes 589832 | tf_op jit(solution)/shard_map/ppermute | solution.py:253
  133.4 1.1 copy.31
  134.5 2.3 %collective-permute-done.13 = bf16[384,256]{1,0:T(8,128)(2,1)S(1)} collective-permute-done((bf16[384,256]{1,0:T(8,128)(2,1)S(1)}, bf16[384,256]{1,0:T(8,128)(2,1)S(1)}, u32[]{:S(2)}, u32[]{:S(2)}) %collective-permute-start.13) | collective-permute-done | bytes 196640 | tf_op jit(solution)/shard_map/ppermute | solution.py:253
  137.0 1.6 collective-permute-start.14
  138.8 1.1 copy.29
  139.9 4.9 %collective-permute-done.14 = bf16[768,256]{1,0:T(8,128)(2,1)S(1)} collective-permute-done((bf16[768,256]{1,0:T(8,128)(2,1)S(1)}, bf16[768,256]{1,0:T(8,128)(2,1)S(1)}, u32[]{:S(2)}, u32[]{:S(2)}) %collective-permute-start.14) | collective-permute-done | bytes 393248 | tf_op jit(solution)/shard_map/ppermute | solution.py:253
  145.1 1.6 collective-permute-start.15
  146.7 1.2 copy.39
  148.2 2.4 %copy.34 = f32[1,8,340,256]{3,1,2,0:T(8,128)} copy(f32[1,8,340,256]{3,2,1,0:T(8,128)S(1)} %fusion.2) | data formatting | bytes 5570560
  150.6 1.2 copy.40
  152.0 1.4 copy.33
  154.0 3.2 %collective-permute-done.15 = bf16[1536,256]{1,0:T(8,128)(2,1)S(1)} collective-permute-done((bf16[1536,256]{1,0:T(8,128)(2,1)S(1)}, bf16[1536,256]{1,0:T(8,128)(2,1)S(1)}, u32[]{:S(2)}, u32[]{:S(2)}) %collective-permute-start.15) | collective-permute-done | bytes 786464 | tf_op jit(solution)/shard_map/ppermute | solution.py:253
  158.4 1.0 slice_bitcast_fusion
  160.4 1.1 maximum_bitcast_fusion
  (89 shorter events, 15.7 us)
Async XLA Ops:
  0.6 2.4 %copy-start = (s32[8,340]{1,0:T(8,128)S(1)}, s32[8,340]{1,0:T(8,128)}, u32[]{:S(2)}) copy-start(s32[8,340]{1,0:T(8,128)} %param.11) | copy-start | bytes 32644
  1.4 8.3 %collective-permute-start.4 = (bf16[1,2,256]{2,1,0:T(2,128)(2,1)S(1)}, bf16[1,2,256]{2,1,0:T(2,128)(2,1)S(1)}, u32[]{:S(2)}, u32[]{:S(2)}) collective-permute-start(bf16[1,2,256]{2,1,0:T(2,128)(2,1)S(1)} %pad_maximum_fusion.8), channel_id=1, source_target_pairs={{0,16},{16,0},{1,17},{17,1},{2,18},{18,2},{3,19},{19,3},{4,20},{20... | collective-permute-start | bytes 3080 | tf_op jit(solution)/shard_map/ppermute | solution.py:248
  1.9 10.2 %collective-permute-start.2 = (bf16[1,256,1024]{2,1,0:T(8,128)(2,1)}, bf16[1,256,1024]{2,1,0:T(8,128)(2,1)S(1)}, u32[]{:S(2)}, u32[]{:S(2)}) collective-permute-start(bf16[1,256,1024]{2,1,0:T(8,128)(2,1)} %param.16), channel_id=1, source_target_pairs={{0,16},{16,0},{1,17},{17,1},{2,18},{18,2},{3,19},{19,3},{4,20},{20... | collective-permute-start | bytes 1572872 | tf_op jit(solution)/shard_map/ppermute | solution.py:248
  1.9 11.3 %collective-permute-start.3 = (bf16[1,1024,256]{2,1,0:T(8,128)(2,1)}, bf16[1,1024,256]{2,1,0:T(8,128)(2,1)S(1)}, u32[]{:S(2)}, u32[]{:S(2)}) collective-permute-start(bf16[1,1024,256]{2,1,0:T(8,128)(2,1)} %param.17), channel_id=1, source_target_pairs={{0,16},{16,0},{1,17},{17,1},{2,18},{18,2},{3,19},{19,3},{4,20},{20... | collective-permute-start | bytes 1572872 | tf_op jit(solution)/shard_map/ppermute | solution.py:248
  2.4 8.7 %collective-permute-start = (bf16[1,256,768]{2,1,0:T(8,128)(2,1)}, bf16[1,256,768]{2,1,0:T(8,128)(2,1)S(1)}, u32[]{:S(2)}, u32[]{:S(2)}) collective-permute-start(bf16[1,256,768]{2,1,0:T(8,128)(2,1)} %param.13), channel_id=1, source_target_pairs={{0,16},{16,0},{1,17},{17,1},{2,18},{18,2},{3,19},{19,3},{4,20},{20... | collective-permute-start | bytes 1179656 | tf_op jit(solution)/shard_map/ppermute | solution.py:248
  2.5 7.8 %collective-permute-start.1 = (bf16[1,256,256]{2,1,0:T(8,128)(2,1)}, bf16[1,256,256]{2,1,0:T(8,128)(2,1)S(1)}, u32[]{:S(2)}, u32[]{:S(2)}) collective-permute-start(bf16[1,256,256]{2,1,0:T(8,128)(2,1)} %param.14), channel_id=1, source_target_pairs={{0,16},{16,0},{1,17},{17,1},{2,18},{18,2},{3,19},{19,3},{4,20},{20... | collective-permute-start | bytes 393224 | tf_op jit(solution)/shard_map/ppermute | solution.py:248
  7.8 1.9 %copy-start.9 = (bf16[1,256]{1,0:T(2,128)(2,1)S(1)}, bf16[1,256]{1,0:T(2,128)(2,1)}, u32[]{:S(2)}) copy-start(bf16[1,256]{1,0:T(2,128)(2,1)} %param.15) | copy-start | bytes 1540
  7.8 1.9 %copy-start.10 = (bf16[1,256]{1,0:T(2,128)(2,1)S(1)}, bf16[1,256]{1,0:T(2,128)(2,1)}, u32[]{:S(2)}) copy-start(bf16[1,256]{1,0:T(2,128)(2,1)} %param.12) | copy-start | bytes 1540
  7.8 2.5 %copy-start.8 = (bf16[1,256,256]{2,1,0:T(8,128)(2,1)S(1)}, bf16[1,256,256]{2,1,0:T(8,128)(2,1)}, u32[]{:S(2)}) copy-start(bf16[1,256,256]{2,1,0:T(8,128)(2,1)} %param.14) | copy-start | bytes 393220
  8.8 2.3 %copy-start.7 = (bf16[1,256,768]{2,1,0:T(8,128)(2,1)S(1)}, bf16[1,256,768]{2,1,0:T(8,128)(2,1)}, u32[]{:S(2)}) copy-start(bf16[1,256,768]{2,1,0:T(8,128)(2,1)} %param.13) | copy-start | bytes 1179652
  11.1 1.0 copy-start.5
  12.2 1.1 copy-start.6
  80.5 3.5 %collective-permute-start.7 = (bf16[3088,256]{1,0:T(8,128)(2,1)S(1)}, bf16[3088,256]{1,0:T(8,128)(2,1)S(1)}, u32[]{:S(2)}, u32[]{:S(2)}) collective-permute-start(bf16[3088,256]{1,0:T(8,128)(2,1)S(1)} %dynamic-slice_bitcast_fusion), channel_id=1, source_target_pairs={{0,16},{16,0},{1,17},{17,1},{2,18},{18,2},{3,19},{19,3},{4,20},{20... | collective-permute-start | bytes 4743176 | tf_op jit(solution)/shard_map/ppermute | solution.py:248
  85.8 1.1 copy-start.1
  87.0 0.7 slice-start
  88.6 12.9 %collective-permute-start.8 = (bf16[1552,256]{1,0:T(8,128)(2,1)}, bf16[1552,256]{1,0:T(8,128)(2,1)S(1)}, u32[]{:S(2)}, u32[]{:S(2)}) collective-permute-start(bf16[1552,256]{1,0:T(8,128)(2,1)} %pad_maximum_fusion.2), channel_id=1, source_target_pairs={{0,1},{1,0},{2,3},{3,2},{4,5},{5,4},{6,7},{7,6},{8,9},{9,8},{10,11... | collective-permute-start | bytes 2383880 | tf_op jit(solution)/shard_map/ppermute | solution.py:253
  91.2 10.5 %copy-start.2 = (bf16[3088,256]{1,0:T(8,128)(2,1)S(1)}, bf16[3088,256]{1,0:T(8,128)(2,1)}, u32[]{:S(2)}) copy-start(bf16[3088,256]{1,0:T(8,128)(2,1)} %copy-done.1) | copy-start | bytes 4743172
  101.8 8.0 %collective-permute-start.9 = (bf16[784,256]{1,0:T(8,128)(2,1)S(1)}, bf16[784,256]{1,0:T(8,128)(2,1)S(1)}, u32[]{:S(2)}, u32[]{:S(2)}) collective-permute-start(bf16[784,256]{1,0:T(8,128)(2,1)S(1)} %pad_maximum_fusion.4), channel_id=1, source_target_pairs={{0,2},{1,3},{2,0},{3,1},{4,6},{5,7},{6,4},{7,5},{8,10},{9,11},{10,... | collective-permute-start | bytes 1204232 | tf_op jit(solution)/shard_map/ppermute | solution.py:253
  109.9 23.3 %copy-start.4 = (bf16[2,4,352,256]{3,2,1,0:T(8,128)(2,1)S(1)}, bf16[2,4,352,256]{3,2,1,0:T(8,128)(2,1)}, u32[]{:S(2)}) copy-start(bf16[2,4,352,256]{3,2,1,0:T(8,128)(2,1)} %get-tuple-element.12) | copy-start | bytes 4325380
  110.0 6.0 %collective-permute-start.10 = (bf16[400,256]{1,0:T(8,128)(2,1)S(1)}, bf16[400,256]{1,0:T(8,128)(2,1)S(1)}, u32[]{:S(2)}, u32[]{:S(2)}) collective-permute-start(bf16[400,256]{1,0:T(8,128)(2,1)S(1)} %pad_maximum_fusion.6), channel_id=1, source_target_pairs={{0,4},{1,5},{2,6},{3,7},{4,0},{5,1},{6,2},{7,3},{8,12},{9,13},{10,... | collective-permute-start | bytes 614408 | tf_op jit(solution)/shard_map/ppermute | solution.py:253
  116.1 5.7 %collective-permute-start.11 = (bf16[208,256]{1,0:T(8,128)(2,1)S(1)}, bf16[208,256]{1,0:T(8,128)(2,1)S(1)}, u32[]{:S(2)}, u32[]{:S(2)}) collective-permute-start(bf16[208,256]{1,0:T(8,128)(2,1)S(1)} %pad_maximum_fusion.7), channel_id=1, source_target_pairs={{0,8},{1,9},{2,10},{3,11},{4,12},{5,13},{6,14},{7,15},{8,0},{9,1},... | collective-permute-start | bytes 319496 | tf_op jit(solution)/shard_map/ppermute | solution.py:253
  121.8 5.9 %collective-permute-start.12 = (bf16[192,256]{1,0:T(8,128)(2,1)S(1)}, bf16[192,256]{1,0:T(8,128)(2,1)S(1)}, u32[]{:S(2)}, u32[]{:S(2)}) collective-permute-start(bf16[192,256]{1,0:T(8,128)(2,1)S(1)} %add_convert_fusion.3), channel_id=1, source_target_pairs={{0,8},{1,9},{2,10},{3,11},{4,12},{5,13},{6,14},{7,15},{8,0},{9,1},... | collective-permute-start | bytes 294920 | tf_op jit(solution)/shard_map/ppermute | solution.py:253
  127.8 9.1 %collective-permute-start.13 = (bf16[384,256]{1,0:T(8,128)(2,1)S(1)}, bf16[384,256]{1,0:T(8,128)(2,1)S(1)}, u32[]{:S(2)}, u32[]{:S(2)}) collective-permute-start(bf16[384,256]{1,0:T(8,128)(2,1)S(1)} %maximum_select_fusion.5), channel_id=1, source_target_pairs={{0,4},{1,5},{2,6},{3,7},{4,0},{5,1},{6,2},{7,3},{8,12},{9,13},{10,... | collective-permute-start | bytes 589832 | tf_op jit(solution)/shard_map/ppermute | solution.py:253
  133.4 5.2 %copy-start.3 = (bf16[2,4,352,256]{3,2,1,0:T(8,128)(2,1)S(1)}, bf16[2,4,352,256]{3,2,1,0:T(8,128)(2,1)}, u32[]{:S(2)}) copy-start(bf16[2,4,352,256]{3,2,1,0:T(8,128)(2,1)} %get-tuple-element.11) | copy-start | bytes 4325380
  134.5 12.2 %collective-permute-start.6 = (bf16[4,340,256]{2,0,1:T(4,128)(2,1)}, bf16[4,340,256]{2,0,1:T(4,128)(2,1)}, u32[]{:S(2)}, u32[]{:S(2)}) collective-permute-start(bf16[4,340,256]{2,0,1:T(4,128)(2,1)} %copy.31), channel_id=1, source_target_pairs={{0,16},{16,0},{1,17},{17,1},{2,18},{18,2},{3,19},{19,3},{4,20},{20... | collective-permute-start | bytes 2088968 | tf_op jit(solution)/shard_map/ppermute | solution.py:248
  137.0 7.8 %collective-permute-start.14 = (bf16[768,256]{1,0:T(8,128)(2,1)S(1)}, bf16[768,256]{1,0:T(8,128)(2,1)S(1)}, u32[]{:S(2)}, u32[]{:S(2)}) collective-permute-start(bf16[768,256]{1,0:T(8,128)(2,1)S(1)} %maximum_select_fusion.4), channel_id=1, source_target_pairs={{0,2},{1,3},{2,0},{3,1},{4,6},{5,7},{6,4},{7,5},{8,10},{9,11},{10,... | collective-permute-start | bytes 1179656 | tf_op jit(solution)/shard_map/ppermute | solution.py:253
  139.9 10.7 %collective-permute-start.5 = (bf16[4,340,256]{2,0,1:T(4,128)(2,1)}, bf16[4,340,256]{2,0,1:T(4,128)(2,1)}, u32[]{:S(2)}, u32[]{:S(2)}) collective-permute-start(bf16[4,340,256]{2,0,1:T(4,128)(2,1)} %copy.29), channel_id=1, source_target_pairs={{0,16},{16,0},{1,17},{17,1},{2,18},{18,2},{3,19},{19,3},{4,20},{20... | collective-permute-start | bytes 2088968 | tf_op jit(solution)/shard_map/ppermute | solution.py:248
  145.1 12.1 %collective-permute-start.15 = (bf16[1536,256]{1,0:T(8,128)(2,1)S(1)}, bf16[1536,256]{1,0:T(8,128)(2,1)S(1)}, u32[]{:S(2)}, u32[]{:S(2)}) collective-permute-start(bf16[1536,256]{1,0:T(8,128)(2,1)S(1)} %maximum_select_fusion.3), channel_id=1, source_target_pairs={{0,1},{1,0},{2,3},{3,2},{4,5},{5,4},{6,7},{7,6},{8,9},{9,8},{10,11... | collective-permute-start | bytes 2359304 | tf_op jit(solution)/shard_map/ppermute | solution.py:253

commit v2 on v1

v2 whole, which is shorter than its diff:
```python
import jax
import jax.numpy as jnp
from jax import lax
from jax.experimental import pallas as pl
from jax.experimental.pallas import tpu as pltpu
from jax.sharding import PartitionSpec as P

D = 256
FF = 1024
FRAME = 17
LP = 352
EPS = 1e-05
BIG = -(2.0**100)
BLOCKS = ((0, 112, 0, 128), (112, 240, 0, 256), (240, 304, 64, 320), (304, 352, 96, 352))
ERF = (7.97852379e-01, 3.64383569e-02, -1.13746830e-04, -3.20493527e-05, 1.18025665e-06)
TWO = 2
F32 = jnp.float32
BF = jnp.bfloat16


def mm(a, b):
    return jnp.dot(a, b, preferred_element_type=F32)


def mm_t(a, b):
    return lax.dot_general(a, b, (((1,), (1,)), ((), ())), preferred_element_type=F32)


def tmm(a, b):
    return lax.dot_general(a, b, (((0,), (0,)), ((), ())), preferred_element_type=F32)


def norm_stats(x):
    mean = jnp.sum(x, axis=-1, keepdims=True) * (1.0 / D)
    center = x - mean
    var = jnp.sum(center * center, axis=-1, keepdims=True) * (1.0 / D)
    rstd = lax.rsqrt(var + EPS)
    return center * rstd, rstd


def norm_back(d_out, gain, xhat, rstd):
    dy = d_out * gain
    s1 = jnp.sum(dy, axis=-1, keepdims=True) * (1.0 / D)
    s2 = jnp.sum(dy * xhat, axis=-1, keepdims=True) * (1.0 / D)
    return rstd * (dy - s1 - xhat * s2)


def gain_rows(d_out, xhat):
    prod = d_out * xhat
    return jnp.sum(prod.reshape(prod.shape[0] // 8, 8, D), axis=0)


def gelu_pair(u):
    u2 = u * u
    p = jnp.full_like(u, ERF[-1])
    for c in ERF[-2::-1]:
        p = p * u2 + c
    cdf = 0.5 + 0.5 * jnp.tanh(u * p)
    pdf = jnp.exp2(u2 * -0.7213475204444817 - 1.3257480647361593)
    return u * cdf, cdf + u * pdf


def two_heads(block, lane_low):
    zero = jnp.zeros_like(block)
    return jnp.concatenate(
        [jnp.where(lane_low, block, zero), jnp.where(lane_low, zero, block)], axis=0
    )


def one_pair(stacked, n, lane_low):
    return jnp.where(lane_low, stacked[:n], stacked[n:])


def low_mask(n):
    return lax.broadcasted_iota(jnp.int32, (n, 128), 1) < 64


def merged(*lists):
    tagged = [((i + 0.5) / len(units), j, unit) for j, units in enumerate(lists) for i, unit in enumerate(units)]
    for _, _, unit in sorted(tagged, key=lambda t: t[:2]):
        unit()


def wide(column):
    return jnp.concatenate([column, column], axis=1)


PARTS = ((0, 176), (176, 352))
PAIRS = ((0, slice(0, 128)), (1, slice(128, 256)))


def kernel(
    sec_ref, x_ref, cot_ref, seg_ref, gmine_ref, gother_ref,
    wqkv_mine, wout_mine, wup_mine, wdown_mine, wqkv_other, wout_other, wup_other, wdown_other,
    yk_ref, ys_ref, dk_out_ref, ds_out_ref, pk_ref, qk_ref, psend_ref, qsend_ref,
    wqkv_ref, wout_ref, wup_ref, wdown_ref, wsem, gains_ref, eq_ref, ek_ref, ybuf_ref, dbuf_ref,
    res_ref, xhat1_ref, rstd1_ref, xhat2_ref, rstd2_ref, a_ref, b_ref, o_ref, qs_ref, k_ref, v_ref,
    p_ref, m_ref, gp_ref, gb_ref, du_ref, dh_ref, dhb_ref, do_ref, dqkv_ref, dk_ref, dv_ref,
    left_ref, aqkv_ref, aout_ref, aup_ref, adown_ref, again_ref,
):
    step = pl.program_id(0)
    last = pl.num_programs(0) - 1
    sec = sec_ref[0]
    first = sec == 0
    length = x_ref.shape[1]

    @pl.when(step == 0)
    def _():
        copies = []
        for mine, other, held in (
            (wqkv_mine, wqkv_other, wqkv_ref), (wout_mine, wout_other, wout_ref),
            (wup_mine, wup_other, wup_ref), (wdown_mine, wdown_other, wdown_ref),
        ):
            copies.append(pltpu.make_async_copy(mine.at[0], held.at[sec], wsem.at[len(copies)]))
            copies.append(pltpu.make_async_copy(other.at[0], held.at[1 - sec], wsem.at[len(copies)]))
        for copy in copies:
            copy.start()
        gains_ref[0] = jnp.where(first, gmine_ref[...], gother_ref[...])
        gains_ref[1] = jnp.where(first, gother_ref[...], gmine_ref[...])
        for ref in (aqkv_ref, aout_ref, aup_ref, adown_ref, again_ref):
            ref[...] = jnp.zeros_like(ref)
        for copy in copies:
            copy.wait()

    parts = ((0, 176), (176, length))

    def load(r):
        def tokens(lo, hi):
            res_ref[r, lo:hi, :] = x_ref[r, lo:hi, :].astype(F32)
            gb_ref[1, LP * r + lo : LP * r + hi, :] = cot_ref[r, lo:hi, :]

        def visibility():
            seg = jnp.broadcast_to(seg_ref[r], (128, seg_ref.shape[2])).astype(F32).T[:LP]
            lane = lax.broadcasted_iota(jnp.int32, (LP, 128), 1)
            token = lax.broadcasted_iota(jnp.int32, (LP, 128), 0)
            same = seg == (lane - 64).astype(F32)
            start = FRAME * lane
            here = jnp.logical_and(token >= start, token < start + FRAME)
            later = token >= start + FRAME
            other = jnp.logical_and(jnp.logical_not(same), lane < 68)
            eq_ref[r] = jnp.where(lane < 64, jnp.where(here, 1.0, 0.0), jnp.where(same, 1.0, 0.0)).astype(BF)
            ek_ref[r] = jnp.where(lane < 64, jnp.where(later, BIG, 0.0), jnp.where(other, BIG, 0.0)).astype(BF)

        res_ref[r, LP - 16 : LP, :] = jnp.zeros((16, D), F32)
        gb_ref[1, LP * r + LP - 16 : LP * r + LP, :] = jnp.zeros((16, D), BF)
        return [lambda lo=lo, hi=hi: tokens(lo, hi) for lo, hi in parts] + [visibility]

    ones = jnp.ones((LP, 128), BF)

    def attn_forward(r, l):
        base = LP * r
        units = []

        def norm(lo, hi):
            xhat, rstd = norm_stats(res_ref[r, lo:hi, :])
            xhat1_ref[l, r, lo:hi, :] = xhat
            rstd1_ref[l, r, lo:hi, :] = jnp.broadcast_to(rstd, (hi - lo, 128))
            a_ref[l, base + lo : base + hi, :] = (xhat * gains_ref[l, 0:1, :]).astype(BF)

        def query():
            q = mm(a_ref[l, base : base + LP, :], wqkv_ref[l, :, 0:256]).astype(BF) * jnp.array(0.125, BF)
            for p in range(2):
                for q0, q1, _, _ in BLOCKS:
                    qs_ref[l, r, p, 2 * q0 : 2 * q1, :] = two_heads(q[q0:q1, 128 * p : 128 * p + 128], low_mask(q1 - q0))

        def key():
            k_ref[l, r] = mm(a_ref[l, base : base + LP, :], wqkv_ref[l, :, 256:512]).astype(BF)

        def value():
            v_ref[l, r] = mm(a_ref[l, base : base + LP, :], wqkv_ref[l, :, 512:768]).astype(BF)

        held = {}

        def scores(q0, q1, k0, k1):
            eq = eq_ref[r, q0:q1, :]
            eq = jnp.concatenate([eq, eq], axis=0)
            ek = ek_ref[r, k0:k1, :]
            held[q0] = [
                mm_t(
                    jnp.concatenate([qs_ref[l, r, p, 2 * q0 : 2 * q1, :], eq], axis=1),
                    jnp.concatenate([k_ref[l, r, k0:k1, lanes], ek], axis=1),
                )
                for p, lanes in PAIRS
            ]

        def mix(q0, q1, k0, k1):
            n = q1 - q0
            probs = []
            for p, _ in PAIRS:
                s = held[q0][p]
                e = jnp.exp(s - jnp.max(s, axis=-1, keepdims=True))
                prob = (e * (1.0 / jnp.sum(e, axis=-1, keepdims=True))).astype(BF)
                p_ref[l, r, p, 2 * q0 : 2 * q1, 0 : k1 - k0] = prob
                probs.append(prob)
            for p, lanes in PAIRS:
                o = mm(probs[p], v_ref[l, r, k0:k1, lanes])
                o_ref[l, base + q0 : base + q1, lanes] = one_pair(o, n, low_mask(n)).astype(BF)

        def out(lo, hi):
            h = res_ref[r, lo:hi, :] + mm(o_ref[l, base + lo : base + hi, :], wout_ref[l])
            res_ref[r, lo:hi, :] = h
            xhat, rstd = norm_stats(h)
            xhat2_ref[l, r, lo:hi, :] = xhat
            rstd2_ref[l, r, lo:hi, :] = jnp.broadcast_to(rstd, (hi - lo, 128))
            b_ref[l, base + lo : base + hi, :] = (xhat * gains_ref[l, 1:2, :]).astype(BF)

        units += [lambda lo=lo, hi=hi: norm(lo, hi) for lo, hi in PARTS]
        units += [query, key, value]
        first = [lambda b=b: scores(*b) for b in BLOCKS]
        second = [lambda b=b: mix(*b) for b in BLOCKS]
        units += [first[0], first[1], second[0], first[2], second[1], first[3], second[2], second[3]]
        units += [lambda lo=lo, hi=hi: out(lo, hi) for lo, hi in PARTS]
        return units

    def mlp_forward(r, l):
        base = LP * r

        def chunk(c, lo, hi):
            rows = slice(base + lo, base + hi)
            ups = [mm(b_ref[l, rows, :], wup_ref[l, :, 256 * j : 256 * j + 256]) for j in (c, c + 1)]
            for j, u in zip((c, c + 1), ups):
                m, gp = gelu_pair(u)
                m_ref[l, rows, 256 * j : 256 * j + 256] = m.astype(BF)
                gp_ref[l, r, lo:hi, 256 * j : 256 * j + 256] = gp.astype(BF)

        def down(lo, hi):
            y = res_ref[r, lo:hi, :] + mm(m_ref[l, base + lo : base + hi, :], wdown_ref[l])
            y = y.astype(BF)
            if l == 0:
                ybuf_ref[r, lo:hi, :] = y
                res_ref[r, lo:hi, :] = y.astype(F32)
            else:
                end = min(hi, length)
                y0, y1 = ybuf_ref[r, lo:hi, :][: end - lo], y[: end - lo]
                yk_ref[r, lo:end, :] = jnp.where(first, y0, y1)
                ys_ref[r, lo:end, :] = jnp.where(first, y1, y0)

        return [f for lo, hi in PARTS for f in (
            lambda lo=lo, hi=hi: chunk(0, lo, hi), lambda lo=lo, hi=hi: chunk(2, lo, hi), lambda lo=lo, hi=hi: down(lo, hi))]

    def mlp_backward(r, l):
        base = LP * r

        def chunk(c, lo, hi):
            rows = slice(base + lo, base + hi)
            dms = [mm_t(gb_ref[l, rows, :], wdown_ref[l, 256 * j : 256 * j + 256, :]) for j in (c, c + 1)]
            for j, dm in zip((c, c + 1), dms):
                cols = slice(256 * j, 256 * j + 256)
                du_ref[l, rows, cols] = (dm * gp_ref[l, r, lo:hi, cols].astype(F32)).astype(BF)

        def back(lo, hi):
            rows = slice(base + lo, base + hi)
            d_b = mm_t(du_ref[l, rows, :], wup_ref[l])
            xhat = xhat2_ref[l, r, lo:hi, :]
            again_ref[l, 1] += gain_rows(d_b, xhat)
            d_h = gb_ref[l, rows, :].astype(F32) + norm_back(d_b, gains_ref[l, 1:2, :], xhat, wide(rstd2_ref[l, r, lo:hi, :]))
            dh_ref[r, lo:hi, :] = d_h
            dhb_ref[l, rows, :] = d_h.astype(BF)

        return (
            [lambda c=c, lo=lo, hi=hi: chunk(c, lo, hi) for c in (0, 2) for lo, hi in PARTS]
            + [lambda lo=lo, hi=hi: back(lo, hi) for lo, hi in PARTS]
        )

    def attn_backward(r, l):
        base = LP * r

        def out():
            d_o = mm_t(dhb_ref[l, base : base + LP, :], wout_ref[l]).astype(BF)
            prod = (-(d_o.astype(F32) * o_ref[l, base : base + LP, :].astype(F32))).astype(BF)
            for p in range(2):
                lanes = slice(128 * p, 128 * p + 128)
                for q0, q1, _, _ in BLOCKS:
                    mask = low_mask(q1 - q0)
                    do_ref[r, p, 2 * q0 : 2 * q1, 0:128] = two_heads(d_o[q0:q1, lanes], mask)
                    do_ref[r, p, 2 * q0 : 2 * q1, 128:256] = two_heads(prod[q0:q1, lanes], mask)
            dk_ref[r] = jnp.zeros((LP, D), F32)
            dv_ref[r] = jnp.zeros((LP, D), F32)

        held = {}

        def probs(q0, q1, k0, k1):
            rows = slice(2 * q0, 2 * q1)
            held[q0] = [
                mm_t(do_ref[r, p, rows, :], jnp.concatenate([v_ref[l, r, k0:k1, lanes], ones[k0:k1]], axis=1))
                for p, lanes in PAIRS
            ]

        def values(q0, q1, k0, k1):
            rows = slice(2 * q0, 2 * q1)
            for p, lanes in PAIRS:
                dv_ref[r, k0:k1, lanes] += tmm(p_ref[l, r, p, rows, 0 : k1 - k0], do_ref[r, p, rows, 0:128])

        def queries(q0, q1, k0, k1):
            n = q1 - q0
            rows = slice(2 * q0, 2 * q1)
            ds = [(p_ref[l, r, p, rows, 0 : k1 - k0].astype(F32) * held[q0][p]).astype(BF) for p, _ in PAIRS]
            for p, lanes in PAIRS:
                dq = mm(ds[p], k_ref[l, r, k0:k1, lanes])
                dqkv_ref[l, base + q0 : base + q1, lanes] = (one_pair(dq, n, low_mask(n)) * 0.125).astype(BF)
            for p, lanes in PAIRS:
                dk_ref[r, k0:k1, lanes] += tmm(ds[p], qs_ref[l, r, p, rows, :])

        def finish(lo, hi):
            rows = slice(base + lo, base + hi)
            dqkv_ref[l, rows, 256:512] = dk_ref[r, lo:hi, :].astype(BF)
            dqkv_ref[l, rows, 512:768] = dv_ref[r, lo:hi, :].astype(BF)
            d_a = mm_t(dqkv_ref[l, rows, :], wqkv_ref[l])
            xhat = xhat1_ref[l, r, lo:hi, :]
            again_ref[l, 0] += gain_rows(d_a, xhat)
            d_x = dh_ref[r, lo:hi, :] + norm_back(d_a, gains_ref[l, 0:1, :], xhat, wide(rstd1_ref[l, r, lo:hi, :]))
            if l:
                dbuf_ref[r, lo:hi, :] = d_x
                gb_ref[0, rows, :] = d_x.astype(BF)
            else:
                end = min(hi, length)
                d0, d1 = d_x[: end - lo], dbuf_ref[r, lo:hi, :][: end - lo]
                dk_out_ref[r, lo:end, :] = jnp.where(first, d0, d1)
                ds_out_ref[r, lo:end, :] = jnp.where(first, d1, d0).astype(BF)

        order = [(probs, 0), (probs, 1), (values, 0), (queries, 0), (probs, 2), (values, 1), (queries, 1)]
        order += [(probs, 3), (values, 2), (queries, 2), (values, 3), (queries, 3)]
        return (
            [out]
            + [lambda f=f, b=BLOCKS[i]: f(*b) for f, i in order]
            + [lambda lo=lo, hi=hi: finish(lo, hi) for lo, hi in PARTS]
        )

    def turn(j, ref, l):
        left_ref[j] = ref[l].T

    def mlp_weights(l):
        def down(c):
            for j in (c, c + 1):
                cols = slice(256 * j, 256 * j + 256)
                adown_ref[l, :, cols] += mm(left_ref[0], m_ref[l, :, cols])

        def up(c):
            for j in (c, c + 1):
                cols = slice(256 * j, 256 * j + 256)
                aup_ref[l, :, cols] += mm(left_ref[1], du_ref[l, :, cols])

        return [
            lambda: turn(0, gb_ref, l), lambda: turn(1, b_ref, l),
            lambda: down(0), lambda: down(2), lambda: up(0), lambda: up(2),
        ]

    def attn_weights(l):
        def out_and_query():
            aout_ref[l] += mm(left_ref[2], dhb_ref[l])
            aqkv_ref[l, :, 0:256] += mm(left_ref[3], dqkv_ref[l, :, 0:256])

        def key_and_value():
            for j in (1, 2):
                cols = slice(256 * j, 256 * j + 256)
                aqkv_ref[l, :, cols] += mm(left_ref[3], dqkv_ref[l, :, cols])

        return [lambda: turn(2, o_ref, l), lambda: turn(3, a_ref, l), out_and_query, key_and_value]

    merged(load(0) + attn_forward(0, 0))
    merged(mlp_forward(0, 0), load(1) + attn_forward(1, 0))
    merged(attn_forward(0, 1), mlp_forward(1, 0))
    merged(mlp_forward(0, 1), attn_forward(1, 1))
    merged(mlp_backward(0, 1), mlp_forward(1, 1))
    merged(attn_backward(0, 1), mlp_backward(1, 1))
    merged(mlp_backward(0, 0), attn_backward(1, 1), mlp_weights(1))
    merged(attn_backward(0, 0), mlp_backward(1, 0), attn_weights(1))
    merged(attn_backward(1, 0), mlp_weights(0))
    merged(attn_weights(0))

    @pl.when(step == last)
    def _():
        for l, p_out, q_out in ((sec, pk_ref, qk_ref), (1 - sec, psend_ref, qsend_ref)):
            for j in range(3):
                p_out[256 * j : 256 * j + 256, :] = aqkv_ref[l, :, 256 * j : 256 * j + 256].astype(BF)
            p_out[768:1024, :] = aout_ref[l].astype(BF)
            for j in range(2):
                p_out[1024 + 256 * j : 1280 + 256 * j, :] = aup_ref[l, :, 256 * j : 256 * j + 256].astype(BF)
                q_out[256 * j : 256 * j + 256, :] = aup_ref[l, :, 512 + 256 * j : 768 + 256 * j].astype(BF)
            for j in range(4):
                q_out[512 + 256 * j : 768 + 256 * j, :] = adown_ref[l, :, 256 * j : 256 * j + 256].astype(BF).T
            row = lax.broadcasted_iota(jnp.int32, (16, D), 0)
            attn = jnp.sum(again_ref[l, 0], axis=0, keepdims=True)
            mlp = jnp.sum(again_ref[l, 1], axis=0, keepdims=True)
            p_out[1536:1552, :] = jnp.where(row == 0, attn, jnp.where(row == 1, mlp, 0.0)).astype(BF)


def local_step(section, x, cot, segments, gains, other_gains, mine, other):
    rows, length, _ = x.shape
    steps = rows // 2 // TWO
    place = lambda i, sec: (sec[0] * steps + i, 0, 0)
    tok = lambda w: pl.BlockSpec((TWO, length, w), place)
    row_out = pl.BlockSpec((TWO, length, D), lambda i, sec: (i, 0, 0))
    whole = lambda shape: pl.BlockSpec(shape, lambda i, sec: (0,) * len(shape), pipeline_mode=pl.Buffered(1))
    hbm = pl.BlockSpec(memory_space=pl.ANY)
    vm = pltpu.VMEM
    flat = lambda w: vm((2, TWO * LP, w), BF)
    shape = jax.ShapeDtypeStruct
    return pl.pallas_call(
        kernel,
        grid_spec=pltpu.PrefetchScalarGridSpec(
            num_scalar_prefetch=1,
            grid=(steps,),
            in_specs=[tok(D), tok(D), pl.BlockSpec((TWO, 1, segments.shape[2]), place), whole((2, D)), whole((2, D))] + [hbm] * 8,
            out_specs=[tok(D), row_out, tok(D), row_out, whole((1552, D)), whole((1536, D)), whole((1552, D)), whole((1536, D))],
            scratch_shapes=[
                vm((2, D, 3 * D), BF), vm((2, D, D), BF), vm((2, D, FF), BF), vm((2, FF, D), BF), pltpu.SemaphoreType.DMA((8,)),
                vm((2, 2, D), F32), vm((TWO, LP, 128), BF), vm((TWO, LP, 128), BF), vm((TWO, LP, D), BF), vm((TWO, LP, D), F32),
                vm((TWO, LP, D), F32),
                vm((2, TWO, LP, D), F32), vm((2, TWO, LP, 128), F32), vm((2, TWO, LP, D), F32), vm((2, TWO, LP, 128), F32),
                flat(D), flat(D), flat(D),
                vm((2, TWO, 2, 2 * LP, 128), BF), vm((2, TWO, LP, D), BF), vm((2, TWO, LP, D), BF),
                vm((2, TWO, 2, 2 * LP, D), BF), flat(FF), vm((2, TWO, LP, FF), BF),
                flat(D), flat(FF), vm((TWO, LP, D), F32), flat(D),
                vm((TWO, 2, 2 * LP, D), BF), flat(3 * D), vm((TWO, LP, D), F32), vm((TWO, LP, D), F32),
                vm((4, D, TWO * LP), BF), vm((2, D, 3 * D), F32), vm((2, D, D), F32), vm((2, D, FF), F32), vm((2, D, FF), F32),
                vm((2, 2, 8, D), F32),
            ],
        ),
        out_shape=[
            shape((rows, length, D), BF), shape((rows // 2, length, D), BF),
            shape((rows, length, D), F32), shape((rows // 2, length, D), BF),
            shape((1552, D), BF), shape((1536, D), BF), shape((1552, D), BF), shape((1536, D), BF),
        ],
        compiler_params=pltpu.CompilerParams(
            dimension_semantics=("arbitrary",), vmem_limit_bytes=60 * 1024 * 1024
        ),
    )(section, x, cot, segments, gains, other_gains, *mine, *other)


def partner(value):
    return lax.ppermute(value, "section", [(0, 1), (1, 0)])


def cross(value, count, bits):
    pairs = [(s * count + i, s * count + (i ^ (1 << bits[s]))) for s in range(2) for i in range(count)]
    return lax.ppermute(value, ("section", "dp"), pairs)


def add(a, b):
    return (a.astype(F32) + b.astype(F32)).astype(BF)


def sum_over_dp(parts, tail, section):
    count = lax.axis_size("dp")
    place = lax.axis_index("dp")
    depth = count.bit_length() - 1
    orders = [list(range(depth)), list(range(depth))]
    if depth > 2:
        orders[1][1], orders[1][2] = 2, 1
    swap = {0: 1, 1: 0} if depth > 1 else {}
    orders = [[(b, swap.get(b, b)) for b in order] for order in orders]
    sizes = [tail, 0]
    current = list(parts)
    uppers = [[], []]
    for stage in range(depth):
        got = []
        for part in range(2):
            bits = orders[part][stage]
            upper = jnp.where(section == 0, place >> bits[0], place >> bits[1]) & 1
            uppers[part].append(upper)
            value = current[part]
            main = value.shape[0] - sizes[part]
            send = lax.dynamic_slice_in_dim(value, (1 - upper) * (main // 2), main // 2, 0)
            if sizes[part]:
                send = jnp.concatenate([send, value[main:]], axis=0)
            got.append(cross(send, count, bits))
        for part in range(2):
            value = current[part]
            main = value.shape[0] - sizes[part]
            keep = lax.dynamic_slice_in_dim(value, uppers[part][stage] * (main // 2), main // 2, 0)
            if sizes[part]:
                keep = jnp.concatenate([keep, value[main:]], axis=0)
            current[part] = add(keep, got[part])
    rest = current[0][current[0].shape[0] - tail :]
    current[0] = current[0][: current[0].shape[0] - tail]
    halves = []
    for stage in reversed(range(depth)):
        got = [cross(current[part], count, orders[part][stage]) for part in range(2)]
        for part in range(2):
            low = uppers[part][stage] == 0
            pair = (jnp.where(low, current[part], got[part]), jnp.where(low, got[part], current[part]))
            if stage == 0:
                halves.append(pair)
            else:
                current[part] = jnp.concatenate(pair, axis=0)
    return halves, rest


def shards(
    layer_input, out_cotangent, segment_ids, gain_attn, weight_qkv, weight_out, gain_mlp, weight_up, weight_down
):
    section = lax.axis_index("section")
    rows, length, _ = layer_input.shape
    half = rows // 2
    gains = jnp.concatenate([gain_attn, gain_mlp], axis=0)
    mine = (weight_qkv, weight_out, weight_up, weight_down)
    other = tuple(partner(w) for w in mine)
    other_gains = partner(gains)
    segments = jnp.pad(segment_ids, ((0, 0), (0, 384 - length)), constant_values=-1)[:, None, :]
    acts, acts_send, grads, grads_send, first, second, first_send, second_send = local_step(
        section[None].astype(jnp.int32), layer_input, out_cotangent, segments,
        gains.astype(F32), other_gains.astype(F32), mine, other,
    )
    got = partner(first_send), partner(second_send)
    parts = add(first, got[0]), add(second, got[1])
    ((qkv, out_up), (up_down, down)), rest = sum_over_dp(parts, 16, section)
    there = (1 - section) * half
    activations = lax.dynamic_update_slice_in_dim(acts, partner(acts_send), there, 0)
    input_grads = lax.dynamic_update_slice_in_dim(grads, partner(grads_send).astype(F32), there, 0)
    side = lambda *blocks: jnp.concatenate(blocks, axis=1).astype(F32)
    return (
        activations[None],
        input_grads[None],
        side(qkv[0:256], qkv[256:512], qkv[512:768])[None],
        out_up[0:256].astype(F32)[None],
        side(out_up[256:512], out_up[512:768], up_down[0:256], up_down[256:512])[None],
        jnp.concatenate([up_down[512:768], down], axis=0).astype(F32)[None],
        rest[0].astype(F32)[None],
        rest[1].astype(F32)[None],
    )


def solution(mesh):
    placed = (
        P("dp", None, None),
        P("dp", None, None),
        P("dp", None),
        P("section", None),
        P("section", None, None),
        P("section", None, None),
        P("section", None),
        P("section", None, None),
        P("section", None, None),
    )
    return jax.shard_map(
        shards,
        mesh=mesh,
        in_specs=placed,
        out_specs=(
            P("section", "dp", None, None),
            P("section", "dp", None, None),
            P("section", None, None),
            P("section", None, None),
            P("section", None, None),
            P("section", None, None),
            P("section", None),
            P("section", None),
        ),
        check_vma=False,
    )
```

time: 163 us -> 120 us (0.74)
  Pallas kernels: 64.5 us -> 43.2 us
  waiting for transfers between devices: 39.4 us -> 20.6 us
  starting transfers between devices: 23.1 us -> 31.3 us
  other arithmetic: 14.2 us -> 9.2 us
  local copies, waits for them, and re-layouts: 19.3 us -> 14.5 us
    pallas_call x1, Pallas kernels: 64.5 us -> 43.2 us  [local_step(): pl.pallas_call(kernel, grid_spec=pltpu.PrefetchScalarGridSpec(num_scalar_...]
    ppermute x8 -> x16, waiting for transfers between devices: 36.1 us -> 19.7 us  [cross(): return lax.ppermute(value, ('section', 'dp'), pairs)]
    ppermute x8 -> x16, starting transfers between devices: 21.4 us -> 28.7 us  [cross(): return lax.ppermute(value, ('section', 'dp'), pairs)]
    unnamed x26 -> x24, local copies, waits for them, and re-layouts: 5.1 us -> 9.7 us
    pallas_call x0 -> x2, local copies, waits for them, and re-layouts: none -> 3.82 us  [local_step(): pl.pallas_call(kernel, grid_spec=pltpu.PrefetchScalarGridSpec(num_scalar_...]
    squeeze x3 -> x0, local copies, waits for them, and re-layouts: 3.76 us -> none  [split(): take = lambda j: lax.dynamic_index_in_dim(a, j, 0, False)]
    concatenate x8 -> x12, other arithmetic: 4.79 us -> 1.04 us  [the longest x1 0.74 us: shards(): side = lambda *blocks: jnp.concatenate(blocks, axis=1).astype(F32)]
    dynamic_slice x8, local copies, waits for them, and re-layouts: 2.82 us -> 0.23 us  [the longest x4 0.14 us: sum_over_dp(): lax.dynamic_slice_in_dim(value, uppers[part][stage] * (main // 2), main /...]
  transfers between devices with their start and end apart: 16 -> 25, of which waited for: 9 -> 15; matrix products, arithmetic and copies ran while one was open for 13% -> 14% of each run, Pallas kernels for 0% -> 0%
where the time goes in v2:
time: 120 us
  Pallas kernels  43.2 us (36%)
  starting transfers between devices  31.3 us (26%)
  waiting for transfers between devices  20.6 us (17%)
  local copies, waits for them, and re-layouts  14.5 us (12%)
  other arithmetic  9.2 us (8%)
    pallas_call x1, Pallas kernels, local_step(): pl.pallas_call(kernel, grid_spec=pltpu.PrefetchScalarGridSpec(num_scalar_...  43.2 us
    ppermute x16, starting transfers between devices, cross(): return lax.ppermute(value, ('section', 'dp'), pairs)  28.7 us
    ppermute x16, waiting for transfers between devices, cross(): return lax.ppermute(value, ('section', 'dp'), pairs)  19.7 us
    unnamed x24, local copies, waits for them, and re-layouts  9.7 us
    pallas_call x2, local copies, waits for them, and re-layouts, local_step(): pl.pallas_call(kernel, grid_spec=pltpu.PrefetchScalarGridSpec(num_scalar_...  3.82 us
    ppermute x9, starting transfers between devices, partner(): return lax.ppermute(value, 'section', [(0, 1), (1, 0)])  2.62 us
  transfers between devices with their start and end apart: 25, of which 15 were waited for; matrix products, arithmetic and copies ran while one was open for 14% of the time, Pallas kernels for 0%

profile of v2, /device:TPU:0, one launch (start us, length us, event | category | flops | bytes accessed | tf_op | source)
XLA Modules:
  0.0 119.9 jit_solution(16892039869080532649)
XLA Ops:
  1.8 1.3 %fusion.1 = (f32[2,256]{1,0:T(2,128)}, bf16[2,256]{1,0:T(2,128)(2,1)S(1)}) fusion(bf16[1,256]{1,0:T(2,128)(2,1)} %param.15, bf16[1,256]{1,0:T(2,128)(2,1)} %param.12), kind=kLoop, calls=%fused_computation.70 | loop fusion | flops 2560 | bytes 4096 | tf_op jit(solution)/shard_map/convert_element_type | solution.py:503
  3.5 2.7 %copy.21.x_ref = bf16[8,340,256]{2,1,0:T(8,128)(2,1)} copy(bf16[8,340,256]{2,0,1:T(8,128)(2,1)} %param.9) | data formatting | bytes 2785280 | tf_op args[0]
  6.2 1.4 %copy.22.cot_ref = bf16[8,340,256]{2,1,0:T(8,128)(2,1)} copy(bf16[8,340,256]{2,0,1:T(8,128)(2,1)S(1)} %copy-done.2) | data formatting | bytes 2785280 | tf_op args[1]
  10.0 43.2 %shard_map.152 = (bf16[8,340,256]{2,1,0:T(8,128)(2,1)}, bf16[4,340,256]{2,1,0:T(8,128)(2,1)}, f32[8,340,256]{2,1,0:T(8,128)}, bf16[4,340,256]{2,1,0:T(8,128)(2,1...) custom-call(s32[1]{0:T(128)} %bitcast.sec_ref, ...), custom_call_target="tpu_custom_call" | custom-call | tf_op jit(solution)/shard_map/pallas_call | solution.py:399
  53.3 2.4 %copy.25 = bf16[4,340,256]{2,0,1:T(4,128)(2,1)} copy(bf16[4,340,256]{2,1,0:T(8,128)(2,1)} %get-tuple-element.19) | data formatting | bytes 1392640 | tf_op jit(solution)/shard_map/pallas_call | solution.py:399
  56.2 1.4 %copy.23 = bf16[4,340,256]{2,0,1:T(4,128)(2,1)S(1)} copy(bf16[4,340,256]{2,1,0:T(8,128)(2,1)} %get-tuple-element.17) | data formatting | bytes 1392640 | tf_op jit(solution)/shard_map/pallas_call | solution.py:399
  59.3 1.4 %add_convert_fusion.1 = bf16[1536,256]{1,0:T(8,128)(2,1)S(1)} fusion(bf16[1536,256]{1,0:T(8,128)(2,1)} %collective-permute-done.16, bf16[1536,256]{1,0:T(8,128)(2,1)S(1)} %copy-done.4), kind=kLoop, calls=%fused_computation.1 | loop fusion | flops 1572864 | bytes 2359296 | tf_op jit(solution)/shard_map/convert_element_type | solution.py:441
  60.7 2.7 %collective-permute-start.17 = (bf16[768,256]{1,0:T(8,128)(2,1)S(1)}, bf16[768,256]{1,0:T(8,128)(2,1)S(1)}, u32[]{:S(2)}, u32[]{:S(2)}) collective-permute-start(bf16[768,256]{1,0:T(8,128)(2,1)S(1)} %constant_dynamic-slice_fusion.3), channel_id=1, source_target_pairs={{0,1},{1,0},{2,3},{3,2},{4,5},{5,4},{6,7},{7,6},{8,9},{9,8},{10,11... | collective-permute-start | bytes 1179656 | tf_op jit(solution)/shard_map/ppermute | solution.py:437
  65.2 1.4 %copy.27 = bf16[1,8,340,256]{3,1,2,0:T(8,128)(2,1)} copy(bf16[1,8,340,256]{3,2,1,0:T(8,128)(2,1)S(1)} %bitcast_dynamic-update-slice_fusion) | data formatting | bytes 2785280
  66.5 2.4 %copy.28 = f32[1,8,340,256]{3,1,2,0:T(8,128)} copy(f32[1,8,340,256]{3,2,1,0:T(8,128)S(1)} %convert_dynamic-update-slice_fusion) | data formatting | bytes 5570560
  69.3 2.2 %collective-permute-start.18 = (bf16[384,256]{1,0:T(8,128)(2,1)S(1)}, bf16[384,256]{1,0:T(8,128)(2,1)S(1)}, u32[]{:S(2)}, u32[]{:S(2)}) collective-permute-start(bf16[384,256]{1,0:T(8,128)(2,1)S(1)} %constant_dynamic-slice_fusion.2), channel_id=1, source_target_pairs={{0,4},{1,5},{2,6},{3,7},{4,0},{5,1},{6,2},{7,3},{8,12},{9,13},{10,... | collective-permute-start | bytes 589832 | tf_op jit(solution)/shard_map/ppermute | solution.py:437
  71.5 2.0 %collective-permute-done.8 = bf16[784,256]{1,0:T(8,128)(2,1)S(1)} collective-permute-done((bf16[784,256]{1,0:T(8,128)(2,1)S(1)}, bf16[784,256]{1,0:T(8,128)(2,1)S(1)}, u32[]{:S(2)}, u32[]{:S(2)}) %collective-permute-start.8) | collective-permute-done | bytes 401440 | tf_op jit(solution)/shard_map/ppermute | solution.py:437
  73.7 2.1 %collective-permute-start.9 = (bf16[400,256]{1,0:T(8,128)(2,1)S(1)}, bf16[400,256]{1,0:T(8,128)(2,1)S(1)}, u32[]{:S(2)}, u32[]{:S(2)}) collective-permute-start(bf16[400,256]{1,0:T(8,128)(2,1)S(1)} %pad_maximum_fusion.4), channel_id=1, source_target_pairs={{0,2},{1,3},{2,0},{3,1},{4,6},{5,7},{6,4},{7,5},{8,10},{9,11},{10,... | collective-permute-start | bytes 614408 | tf_op jit(solution)/shard_map/ppermute | solution.py:437
  76.2 1.7 %collective-permute-start.19 = (bf16[192,256]{1,0:T(8,128)(2,1)S(1)}, bf16[192,256]{1,0:T(8,128)(2,1)S(1)}, u32[]{:S(2)}, u32[]{:S(2)}) collective-permute-start(bf16[192,256]{1,0:T(8,128)(2,1)S(1)} %constant_dynamic-slice_fusion.1), channel_id=1, source_target_pairs={{0,2},{1,3},{2,0},{3,1},{4,6},{5,7},{6,4},{7,5},{8,10},{9,11},{10,... | collective-permute-start | bytes 294920 | tf_op jit(solution)/shard_map/ppermute | solution.py:437
  77.9 1.6 %collective-permute-done.9 = bf16[400,256]{1,0:T(8,128)(2,1)S(1)} collective-permute-done((bf16[400,256]{1,0:T(8,128)(2,1)S(1)}, bf16[400,256]{1,0:T(8,128)(2,1)S(1)}, u32[]{:S(2)}, u32[]{:S(2)}) %collective-permute-start.9) | collective-permute-done | bytes 204832 | tf_op jit(solution)/shard_map/ppermute | solution.py:437
  79.6 2.1 %collective-permute-start.10 = (bf16[208,256]{1,0:T(8,128)(2,1)S(1)}, bf16[208,256]{1,0:T(8,128)(2,1)S(1)}, u32[]{:S(2)}, u32[]{:S(2)}) collective-permute-start(bf16[208,256]{1,0:T(8,128)(2,1)S(1)} %pad_maximum_fusion.8), channel_id=1, source_target_pairs={{0,4},{1,5},{2,6},{3,7},{4,0},{5,1},{6,2},{7,3},{8,12},{9,13},{10,... | collective-permute-start | bytes 319496 | tf_op jit(solution)/shard_map/ppermute | solution.py:437
  81.8 2.7 %collective-permute-start.20 = (bf16[96,256]{1,0:T(8,128)(2,1)S(1)}, bf16[96,256]{1,0:T(8,128)(2,1)S(1)}, u32[]{:S(2)}, u32[]{:S(2)}) collective-permute-start(bf16[96,256]{1,0:T(8,128)(2,1)S(1)} %constant_dynamic-slice_fusion), channel_id=1, source_target_pairs={{0,8},{1,9},{2,10},{3,11},{4,12},{5,13},{6,14},{7,15},{8,0},{9,1},... | collective-permute-start | bytes 147464 | tf_op jit(solution)/shard_map/ppermute | solution.py:437
  85.1 2.6 %collective-permute-start.11 = (bf16[112,256]{1,0:T(8,128)(2,1)S(1)}, bf16[112,256]{1,0:T(8,128)(2,1)S(1)}, u32[]{:S(2)}, u32[]{:S(2)}) collective-permute-start(bf16[112,256]{1,0:T(8,128)(2,1)S(1)} %pad_maximum_fusion.12), channel_id=1, source_target_pairs={{0,8},{1,9},{2,10},{3,11},{4,12},{5,13},{6,14},{7,15},{8,0},{9,1},... | collective-permute-start | bytes 172040 | tf_op jit(solution)/shard_map/ppermute | solution.py:437
  88.6 1.4 %collective-permute-start.21 = (bf16[96,256]{1,0:T(8,128)(2,1)S(1)}, bf16[96,256]{1,0:T(8,128)(2,1)S(1)}, u32[]{:S(2)}, u32[]{:S(2)}) collective-permute-start(bf16[96,256]{1,0:T(8,128)(2,1)S(1)} %add_convert_fusion.9), channel_id=1, source_target_pairs={{0,8},{1,9},{2,10},{3,11},{4,12},{5,13},{6,14},{7,15},{8,0},{9,1},... | collective-permute-start | bytes 147464 | tf_op jit(solution)/shard_map/ppermute | solution.py:437
  90.6 2.2 %collective-permute-start.12 = (bf16[96,256]{1,0:T(8,128)(2,1)S(1)}, bf16[96,256]{1,0:T(8,128)(2,1)S(1)}, u32[]{:S(2)}, u32[]{:S(2)}) collective-permute-start(bf16[96,256]{1,0:T(8,128)(2,1)S(1)} %slice.75), channel_id=1, source_target_pairs={{0,8},{1,9},{2,10},{3,11},{4,12},{5,13},{6,14},{7,15},{8,0},{9,1},... | collective-permute-start | bytes 147464 | tf_op jit(solution)/shard_map/ppermute | solution.py:437
  92.8 1.4 %collective-permute-done.21 = bf16[96,256]{1,0:T(8,128)(2,1)S(1)} collective-permute-done((bf16[96,256]{1,0:T(8,128)(2,1)S(1)}, bf16[96,256]{1,0:T(8,128)(2,1)S(1)}, u32[]{:S(2)}, u32[]{:S(2)}) %collective-permute-start.21) | collective-permute-done | bytes 49184 | tf_op jit(solution)/shard_map/ppermute | solution.py:437
  94.3 1.6 %collective-permute-start.22 = (bf16[192,256]{1,0:T(8,128)(2,1)S(1)}, bf16[192,256]{1,0:T(8,128)(2,1)S(1)}, u32[]{:S(2)}, u32[]{:S(2)}) collective-permute-start(bf16[192,256]{1,0:T(8,128)(2,1)S(1)} %pad_maximum_fusion.11), channel_id=1, source_target_pairs={{0,2},{1,3},{2,0},{3,1},{4,6},{5,7},{6,4},{7,5},{8,10},{9,11},{10,... | collective-permute-start | bytes 294920 | tf_op jit(solution)/shard_map/ppermute | solution.py:437
  95.9 1.5 %collective-permute-start.13 = (bf16[192,256]{1,0:T(8,128)(2,1)S(1)}, bf16[192,256]{1,0:T(8,128)(2,1)S(1)}, u32[]{:S(2)}, u32[]{:S(2)}) collective-permute-start(bf16[192,256]{1,0:T(8,128)(2,1)S(1)} %pad_maximum_fusion.10), channel_id=1, source_target_pairs={{0,4},{1,5},{2,6},{3,7},{4,0},{5,1},{6,2},{7,3},{8,12},{9,13},{10,... | collective-permute-start | bytes 294920 | tf_op jit(solution)/shard_map/ppermute | solution.py:437
  97.4 1.6 %collective-permute-done.22 = bf16[192,256]{1,0:T(8,128)(2,1)S(1)} collective-permute-done((bf16[192,256]{1,0:T(8,128)(2,1)S(1)}, bf16[192,256]{1,0:T(8,128)(2,1)S(1)}, u32[]{:S(2)}, u32[]{:S(2)}) %collective-permute-start.22) | collective-permute-done | bytes 98336 | tf_op jit(solution)/shard_map/ppermute | solution.py:437
  99.8 1.2 collective-permute-done.13
  101.0 1.6 %collective-permute-start.14 = (bf16[384,256]{1,0:T(8,128)(2,1)S(1)}, bf16[384,256]{1,0:T(8,128)(2,1)S(1)}, u32[]{:S(2)}, u32[]{:S(2)}) collective-permute-start(bf16[384,256]{1,0:T(8,128)(2,1)S(1)} %pad_maximum_fusion.6), channel_id=1, source_target_pairs={{0,2},{1,3},{2,0},{3,1},{4,6},{5,7},{6,4},{7,5},{8,10},{9,11},{10,... | collective-permute-start | bytes 589832 | tf_op jit(solution)/shard_map/ppermute | solution.py:437
  102.6 2.2 %collective-permute-done.23 = bf16[384,256]{1,0:T(8,128)(2,1)S(1)} collective-permute-done((bf16[384,256]{1,0:T(8,128)(2,1)S(1)}, bf16[384,256]{1,0:T(8,128)(2,1)S(1)}, u32[]{:S(2)}, u32[]{:S(2)}) %collective-permute-start.23) | collective-permute-done | bytes 196640 | tf_op jit(solution)/shard_map/ppermute | solution.py:437
  104.9 1.6 %collective-permute-start.24 = (bf16[768,256]{1,0:T(8,128)(2,1)S(1)}, bf16[768,256]{1,0:T(8,128)(2,1)S(1)}, u32[]{:S(2)}, u32[]{:S(2)}) collective-permute-start(bf16[768,256]{1,0:T(8,128)(2,1)S(1)} %pad_maximum_fusion.3), channel_id=1, source_target_pairs={{0,1},{1,0},{2,3},{3,2},{4,5},{5,4},{6,7},{7,6},{8,9},{9,8},{10,11... | collective-permute-start | bytes 1179656 | tf_op jit(solution)/shard_map/ppermute | solution.py:437
  107.0 1.9 %collective-permute-done.14 = bf16[384,256]{1,0:T(8,128)(2,1)S(1)} collective-permute-done((bf16[384,256]{1,0:T(8,128)(2,1)S(1)}, bf16[384,256]{1,0:T(8,128)(2,1)S(1)}, u32[]{:S(2)}, u32[]{:S(2)}) %collective-permute-start.14) | collective-permute-done | bytes 196640 | tf_op jit(solution)/shard_map/ppermute | solution.py:437
  109.0 1.6 %collective-permute-start.15 = (bf16[768,256]{1,0:T(8,128)(2,1)S(1)}, bf16[768,256]{1,0:T(8,128)(2,1)S(1)}, u32[]{:S(2)}, u32[]{:S(2)}) collective-permute-start(bf16[768,256]{1,0:T(8,128)(2,1)S(1)} %pad_maximum_fusion.2), channel_id=1, source_target_pairs={{0,1},{1,0},{2,3},{3,2},{4,5},{5,4},{6,7},{7,6},{8,9},{9,8},{10,11... | collective-permute-start | bytes 1179656 | tf_op jit(solution)/shard_map/ppermute | solution.py:437
  110.6 2.2 %collective-permute-done.24 = bf16[768,256]{1,0:T(8,128)(2,1)S(1)} collective-permute-done((bf16[768,256]{1,0:T(8,128)(2,1)S(1)}, bf16[768,256]{1,0:T(8,128)(2,1)S(1)}, u32[]{:S(2)}, u32[]{:S(2)}) %collective-permute-start.24) | collective-permute-done | bytes 393248 | tf_op jit(solution)/shard_map/ppermute | solution.py:437
  114.0 3.0 %collective-permute-done.15 = bf16[768,256]{1,0:T(8,128)(2,1)S(1)} collective-permute-done((bf16[768,256]{1,0:T(8,128)(2,1)S(1)}, bf16[768,256]{1,0:T(8,128)(2,1)S(1)}, u32[]{:S(2)}, u32[]{:S(2)}) %collective-permute-start.15) | collective-permute-done | bytes 393248 | tf_op jit(solution)/shard_map/ppermute | solution.py:437
  (99 shorter events, 16.7 us)
Async XLA Ops:
  0.6 5.6 %copy-start.2 = (bf16[8,340,256]{2,0,1:T(8,128)(2,1)S(1)}, bf16[8,340,256]{2,0,1:T(8,128)(2,1)}, u32[]{:S(2)}) copy-start(bf16[8,340,256]{2,0,1:T(8,128)(2,1)} %param.10) | copy-start | bytes 4177924
  0.6 8.2 %collective-permute-start.3 = (bf16[1,256,1024]{2,1,0:T(8,128)(2,1)}, bf16[1,256,1024]{2,1,0:T(8,128)(2,1)S(1)}, u32[]{:S(2)}, u32[]{:S(2)}) collective-permute-start(bf16[1,256,1024]{2,1,0:T(8,128)(2,1)} %wup_mine.1), channel_id=1, source_target_pairs={{0,16},{16,0},{1,17},{17,1},{2,18},{18,2},{3,19},{19,3},{4,20},{20... | collective-permute-start | bytes 1572872 | tf_op jit(solution)/shard_map/ppermute | solution.py:432
  1.2 7.7 %collective-permute-start.4 = (bf16[1,1024,256]{2,1,0:T(8,128)(2,1)}, bf16[1,1024,256]{2,1,0:T(8,128)(2,1)S(1)}, u32[]{:S(2)}, u32[]{:S(2)}) collective-permute-start(bf16[1,1024,256]{2,1,0:T(8,128)(2,1)} %wdown_mine.1), channel_id=1, source_target_pairs={{0,16},{16,0},{1,17},{17,1},{2,18},{18,2},{3,19},{19,3},{4,20},{20... | collective-permute-start | bytes 1572872 | tf_op jit(solution)/shard_map/ppermute | solution.py:432
  1.2 7.6 %collective-permute-start.1 = (bf16[1,256,768]{2,1,0:T(8,128)(2,1)}, bf16[1,256,768]{2,1,0:T(8,128)(2,1)S(1)}, u32[]{:S(2)}, u32[]{:S(2)}) collective-permute-start(bf16[1,256,768]{2,1,0:T(8,128)(2,1)} %wqkv_mine.1), channel_id=1, source_target_pairs={{0,16},{16,0},{1,17},{17,1},{2,18},{18,2},{3,19},{19,3},{4,20},{20... | collective-permute-start | bytes 1179656 | tf_op jit(solution)/shard_map/ppermute | solution.py:432
  1.7 7.1 %collective-permute-start.2 = (bf16[1,256,256]{2,1,0:T(8,128)(2,1)}, bf16[1,256,256]{2,1,0:T(8,128)(2,1)S(1)}, u32[]{:S(2)}, u32[]{:S(2)}) collective-permute-start(bf16[1,256,256]{2,1,0:T(8,128)(2,1)} %wout_mine.1), channel_id=1, source_target_pairs={{0,16},{16,0},{1,17},{17,1},{2,18},{18,2},{3,19},{19,3},{4,20},{20... | collective-permute-start | bytes 393224 | tf_op jit(solution)/shard_map/ppermute | solution.py:432
  3.1 5.2 %collective-permute-start = (bf16[2,256]{1,0:T(2,128)(2,1)S(1)}, bf16[2,256]{1,0:T(2,128)(2,1)S(1)}, u32[]{:S(2)}, u32[]{:S(2)}) collective-permute-start(bf16[2,256]{1,0:T(2,128)(2,1)S(1)} %get-tuple-element.41), channel_id=1, source_target_pairs={{0,16},{16,0},{1,17},{17,1},{2,18},{18,2},{3,19},{19,3},{4,20},{20... | collective-permute-start | bytes 3080 | tf_op jit(solution)/shard_map/ppermute | solution.py:432
  6.2 1.4 %copy-start.9 = (s32[8,340]{1,0:T(8,128)S(1)}, s32[8,340]{1,0:T(8,128)}, u32[]{:S(2)}) copy-start(s32[8,340]{1,0:T(8,128)} %param.11) | copy-start | bytes 32644
  8.9 1.1 copy-start.6
  53.3 4.9 %copy-start = (f32[8,340,256]{2,1,0:T(8,128)S(1)}, f32[8,340,256]{2,1,0:T(8,128)}, u32[]{:S(2)}) copy-start(f32[8,340,256]{2,1,0:T(8,128)} %get-tuple-element.18) | copy-start | bytes 8355844
  55.6 2.6 %collective-permute-start.6 = (bf16[4,340,256]{2,0,1:T(4,128)(2,1)}, bf16[4,340,256]{2,0,1:T(4,128)(2,1)S(1)}, u32[]{:S(2)}, u32[]{:S(2)}) collective-permute-start(bf16[4,340,256]{2,0,1:T(4,128)(2,1)} %copy.25), channel_id=1, source_target_pairs={{0,16},{16,0},{1,17},{17,1},{2,18},{18,2},{3,19},{19,3},{4,20},{20... | collective-permute-start | bytes 2088968 | tf_op jit(solution)/shard_map/ppermute | solution.py:432
  55.7 3.5 %collective-permute-start.16 = (bf16[1536,256]{1,0:T(8,128)(2,1)}, bf16[1536,256]{1,0:T(8,128)(2,1)}, u32[]{:S(2)}, u32[]{:S(2)}) collective-permute-start(bf16[1536,256]{1,0:T(8,128)(2,1)} %get-tuple-element.23), channel_id=1, source_target_pairs={{0,16},{16,0},{1,17},{17,1},{2,18},{18,2},{3,19},{19,3},{4,20},{20... | collective-permute-start | bytes 2359304 | tf_op jit(solution)/shard_map/ppermute | solution.py:432
  56.1 3.1 %copy-start.4 = (bf16[1536,256]{1,0:T(8,128)(2,1)S(1)}, bf16[1536,256]{1,0:T(8,128)(2,1)}, u32[]{:S(2)}) copy-start(bf16[1536,256]{1,0:T(8,128)(2,1)} %get-tuple-element.22) | copy-start | bytes 2359300
  57.6 6.8 %collective-permute-start.5 = (bf16[4,340,256]{2,0,1:T(4,128)(2,1)S(1)}, bf16[4,340,256]{2,0,1:T(4,128)(2,1)S(1)}, u32[]{:S(2)}, u32[]{:S(2)}) collective-permute-start(bf16[4,340,256]{2,0,1:T(4,128)(2,1)S(1)} %copy.23), channel_id=1, source_target_pairs={{0,16},{16,0},{1,17},{17,1},{2,18},{18,2},{3,19},{19,3},{4,20},{20... | collective-permute-start | bytes 2088968 | tf_op jit(solution)/shard_map/ppermute | solution.py:432
  57.7 5.7 %collective-permute-start.7 = (bf16[1552,256]{1,0:T(8,128)(2,1)}, bf16[1552,256]{1,0:T(8,128)(2,1)S(1)}, u32[]{:S(2)}, u32[]{:S(2)}) collective-permute-start(bf16[1552,256]{1,0:T(8,128)(2,1)} %get-tuple-element.21), channel_id=1, source_target_pairs={{0,16},{16,0},{1,17},{17,1},{2,18},{18,2},{3,19},{19,3},{4,20},{20... | collective-permute-start | bytes 2383880 | tf_op jit(solution)/shard_map/ppermute | solution.py:432
  59.3 4.1 %copy-start.3 = (bf16[1552,256]{1,0:T(8,128)(2,1)S(1)}, bf16[1552,256]{1,0:T(8,128)(2,1)}, u32[]{:S(2)}) copy-start(bf16[1552,256]{1,0:T(8,128)(2,1)} %get-tuple-element.20) | copy-start | bytes 2383876
  60.7 8.4 %collective-permute-start.17 = (bf16[768,256]{1,0:T(8,128)(2,1)S(1)}, bf16[768,256]{1,0:T(8,128)(2,1)S(1)}, u32[]{:S(2)}, u32[]{:S(2)}) collective-permute-start(bf16[768,256]{1,0:T(8,128)(2,1)S(1)} %constant_dynamic-slice_fusion.3), channel_id=1, source_target_pairs={{0,1},{1,0},{2,3},{3,2},{4,5},{5,4},{6,7},{7,6},{8,9},{9,8},{10,11... | collective-permute-start | bytes 1179656 | tf_op jit(solution)/shard_map/ppermute | solution.py:437
  63.7 1.4 %copy-start.1 = (bf16[8,340,256]{2,1,0:T(8,128)(2,1)S(1)}, bf16[8,340,256]{2,1,0:T(8,128)(2,1)}, u32[]{:S(2)}) copy-start(bf16[8,340,256]{2,1,0:T(8,128)(2,1)} %get-tuple-element.16) | copy-start | bytes 4177924
  63.8 9.6 %collective-permute-start.8 = (bf16[784,256]{1,0:T(8,128)(2,1)S(1)}, bf16[784,256]{1,0:T(8,128)(2,1)S(1)}, u32[]{:S(2)}, u32[]{:S(2)}) collective-permute-start(bf16[784,256]{1,0:T(8,128)(2,1)S(1)} %pad_maximum_fusion), channel_id=1, source_target_pairs={{0,1},{1,0},{2,3},{3,2},{4,5},{5,4},{6,7},{7,6},{8,9},{9,8},{10,11... | collective-permute-start | bytes 1204232 | tf_op jit(solution)/shard_map/ppermute | solution.py:437
  69.3 6.8 %collective-permute-start.18 = (bf16[384,256]{1,0:T(8,128)(2,1)S(1)}, bf16[384,256]{1,0:T(8,128)(2,1)S(1)}, u32[]{:S(2)}, u32[]{:S(2)}) collective-permute-start(bf16[384,256]{1,0:T(8,128)(2,1)S(1)} %constant_dynamic-slice_fusion.2), channel_id=1, source_target_pairs={{0,4},{1,5},{2,6},{3,7},{4,0},{5,1},{6,2},{7,3},{8,12},{9,13},{10,... | collective-permute-start | bytes 589832 | tf_op jit(solution)/shard_map/ppermute | solution.py:437
  73.7 5.9 %collective-permute-start.9 = (bf16[400,256]{1,0:T(8,128)(2,1)S(1)}, bf16[400,256]{1,0:T(8,128)(2,1)S(1)}, u32[]{:S(2)}, u32[]{:S(2)}) collective-permute-start(bf16[400,256]{1,0:T(8,128)(2,1)S(1)} %pad_maximum_fusion.4), channel_id=1, source_target_pairs={{0,2},{1,3},{2,0},{3,1},{4,6},{5,7},{6,4},{7,5},{8,10},{9,11},{10,... | collective-permute-start | bytes 614408 | tf_op jit(solution)/shard_map/ppermute | solution.py:437
  76.2 5.6 %collective-permute-start.19 = (bf16[192,256]{1,0:T(8,128)(2,1)S(1)}, bf16[192,256]{1,0:T(8,128)(2,1)S(1)}, u32[]{:S(2)}, u32[]{:S(2)}) collective-permute-start(bf16[192,256]{1,0:T(8,128)(2,1)S(1)} %constant_dynamic-slice_fusion.1), channel_id=1, source_target_pairs={{0,2},{1,3},{2,0},{3,1},{4,6},{5,7},{6,4},{7,5},{8,10},{9,11},{10,... | collective-permute-start | bytes 294920 | tf_op jit(solution)/shard_map/ppermute | solution.py:437
  79.6 5.4 %collective-permute-start.10 = (bf16[208,256]{1,0:T(8,128)(2,1)S(1)}, bf16[208,256]{1,0:T(8,128)(2,1)S(1)}, u32[]{:S(2)}, u32[]{:S(2)}) collective-permute-start(bf16[208,256]{1,0:T(8,128)(2,1)S(1)} %pad_maximum_fusion.8), channel_id=1, source_target_pairs={{0,4},{1,5},{2,6},{3,7},{4,0},{5,1},{6,2},{7,3},{8,12},{9,13},{10,... | collective-permute-start | bytes 319496 | tf_op jit(solution)/shard_map/ppermute | solution.py:437
  81.8 6.7 %collective-permute-start.20 = (bf16[96,256]{1,0:T(8,128)(2,1)S(1)}, bf16[96,256]{1,0:T(8,128)(2,1)S(1)}, u32[]{:S(2)}, u32[]{:S(2)}) collective-permute-start(bf16[96,256]{1,0:T(8,128)(2,1)S(1)} %constant_dynamic-slice_fusion), channel_id=1, source_target_pairs={{0,8},{1,9},{2,10},{3,11},{4,12},{5,13},{6,14},{7,15},{8,0},{9,1},... | collective-permute-start | bytes 147464 | tf_op jit(solution)/shard_map/ppermute | solution.py:437
  85.1 5.5 %collective-permute-start.11 = (bf16[112,256]{1,0:T(8,128)(2,1)S(1)}, bf16[112,256]{1,0:T(8,128)(2,1)S(1)}, u32[]{:S(2)}, u32[]{:S(2)}) collective-permute-start(bf16[112,256]{1,0:T(8,128)(2,1)S(1)} %pad_maximum_fusion.12), channel_id=1, source_target_pairs={{0,8},{1,9},{2,10},{3,11},{4,12},{5,13},{6,14},{7,15},{8,0},{9,1},... | collective-permute-start | bytes 172040 | tf_op jit(solution)/shard_map/ppermute | solution.py:437
  88.6 5.7 %collective-permute-start.21 = (bf16[96,256]{1,0:T(8,128)(2,1)S(1)}, bf16[96,256]{1,0:T(8,128)(2,1)S(1)}, u32[]{:S(2)}, u32[]{:S(2)}) collective-permute-start(bf16[96,256]{1,0:T(8,128)(2,1)S(1)} %add_convert_fusion.9), channel_id=1, source_target_pairs={{0,8},{1,9},{2,10},{3,11},{4,12},{5,13},{6,14},{7,15},{8,0},{9,1},... | collective-permute-start | bytes 147464 | tf_op jit(solution)/shard_map/ppermute | solution.py:437
  90.6 5.3 %collective-permute-start.12 = (bf16[96,256]{1,0:T(8,128)(2,1)S(1)}, bf16[96,256]{1,0:T(8,128)(2,1)S(1)}, u32[]{:S(2)}, u32[]{:S(2)}) collective-permute-start(bf16[96,256]{1,0:T(8,128)(2,1)S(1)} %slice.75), channel_id=1, source_target_pairs={{0,8},{1,9},{2,10},{3,11},{4,12},{5,13},{6,14},{7,15},{8,0},{9,1},... | collective-permute-start | bytes 147464 | tf_op jit(solution)/shard_map/ppermute | solution.py:437
  94.3 4.7 %collective-permute-start.22 = (bf16[192,256]{1,0:T(8,128)(2,1)S(1)}, bf16[192,256]{1,0:T(8,128)(2,1)S(1)}, u32[]{:S(2)}, u32[]{:S(2)}) collective-permute-start(bf16[192,256]{1,0:T(8,128)(2,1)S(1)} %pad_maximum_fusion.11), channel_id=1, source_target_pairs={{0,2},{1,3},{2,0},{3,1},{4,6},{5,7},{6,4},{7,5},{8,10},{9,11},{10,... | collective-permute-start | bytes 294920 | tf_op jit(solution)/shard_map/ppermute | solution.py:437
  95.9 5.0 %collective-permute-start.13 = (bf16[192,256]{1,0:T(8,128)(2,1)S(1)}, bf16[192,256]{1,0:T(8,128)(2,1)S(1)}, u32[]{:S(2)}, u32[]{:S(2)}) collective-permute-start(bf16[192,256]{1,0:T(8,128)(2,1)S(1)} %pad_maximum_fusion.10), channel_id=1, source_target_pairs={{0,4},{1,5},{2,6},{3,7},{4,0},{5,1},{6,2},{7,3},{8,12},{9,13},{10,... | collective-permute-start | bytes 294920 | tf_op jit(solution)/shard_map/ppermute | solution.py:437
  99.1 5.7 %collective-permute-start.23 = (bf16[384,256]{1,0:T(8,128)(2,1)S(1)}, bf16[384,256]{1,0:T(8,128)(2,1)S(1)}, u32[]{:S(2)}, u32[]{:S(2)}) collective-permute-start(bf16[384,256]{1,0:T(8,128)(2,1)S(1)} %pad_maximum_fusion.7), channel_id=1, source_target_pairs={{0,4},{1,5},{2,6},{3,7},{4,0},{5,1},{6,2},{7,3},{8,12},{9,13},{10,... | collective-permute-start | bytes 589832 | tf_op jit(solution)/shard_map/ppermute | solution.py:437
  101.0 7.9 %collective-permute-start.14 = (bf16[384,256]{1,0:T(8,128)(2,1)S(1)}, bf16[384,256]{1,0:T(8,128)(2,1)S(1)}, u32[]{:S(2)}, u32[]{:S(2)}) collective-permute-start(bf16[384,256]{1,0:T(8,128)(2,1)S(1)} %pad_maximum_fusion.6), channel_id=1, source_target_pairs={{0,2},{1,3},{2,0},{3,1},{4,6},{5,7},{6,4},{7,5},{8,10},{9,11},{10,... | collective-permute-start | bytes 589832 | tf_op jit(solution)/shard_map/ppermute | solution.py:437
  104.9 7.8 %collective-permute-start.24 = (bf16[768,256]{1,0:T(8,128)(2,1)S(1)}, bf16[768,256]{1,0:T(8,128)(2,1)S(1)}, u32[]{:S(2)}, u32[]{:S(2)}) collective-permute-start(bf16[768,256]{1,0:T(8,128)(2,1)S(1)} %pad_maximum_fusion.3), channel_id=1, source_target_pairs={{0,1},{1,0},{2,3},{3,2},{4,5},{5,4},{6,7},{7,6},{8,9},{9,8},{10,11... | collective-permute-start | bytes 1179656 | tf_op jit(solution)/shard_map/ppermute | solution.py:437
  109.0 8.0 %collective-permute-start.15 = (bf16[768,256]{1,0:T(8,128)(2,1)S(1)}, bf16[768,256]{1,0:T(8,128)(2,1)S(1)}, u32[]{:S(2)}, u32[]{:S(2)}) collective-permute-start(bf16[768,256]{1,0:T(8,128)(2,1)S(1)} %pad_maximum_fusion.2), channel_id=1, source_target_pairs={{0,1},{1,0},{2,3},{3,2},{4,5},{5,4},{6,7},{7,6},{8,9},{9,8},{10,11... | collective-permute-start | bytes 1179656 | tf_op jit(solution)/shard_map/ppermute | solution.py:437
  (3 other events, 2.4 us)

commit v3 on v2

--- a/solution.py
+++ b/solution.py
@@ -67,8 +67,19 @@
     )
 
 
-def one_pair(stacked, n, lane_low):
-    return jnp.where(lane_low, stacked[:n], stacked[n:])
+def pair_rows(p, q0, q1):
+    return slice(4 * q0 + 2 * p * (q1 - q0), 4 * q0 + 2 * (p + 1) * (q1 - q0))
+
+
+def one_row(stacked, n):
+    mask = low_mask(n)
+    return jnp.concatenate(
+        [
+            jnp.where(mask, stacked[:n, 0:128], stacked[n : 2 * n, 0:128]),
+            jnp.where(mask, stacked[2 * n : 3 * n, 128:256], stacked[3 * n :, 128:256]),
+        ],
+        axis=1,
+    )
 
 
 def low_mask(n):
@@ -86,51 +97,74 @@
 
 
 PARTS = ((0, 176), (176, 352))
+WHOLE = ((0, LP),)
 PAIRS = ((0, slice(0, 128)), (1, slice(128, 256)))
 
 
 def kernel(
-    sec_ref, x_ref, cot_ref, seg_ref, gmine_ref, gother_ref,
+    sec_ref, seg_ref, attn_mine, mlp_mine, attn_other, mlp_other, x_hbm, cot_hbm,
     wqkv_mine, wout_mine, wup_mine, wdown_mine, wqkv_other, wout_other, wup_other, wdown_other,
     yk_ref, ys_ref, dk_out_ref, ds_out_ref, pk_ref, qk_ref, psend_ref, qsend_ref,
-    wqkv_ref, wout_ref, wup_ref, wdown_ref, wsem, gains_ref, eq_ref, ek_ref, ybuf_ref, dbuf_ref,
+    wqkv_ref, wout_ref, wup_ref, wdown_ref, wsem, insem, xin_ref, cin_ref, wide_ref, xrow_ref, crow_ref, seg_pad_ref, gains_ref, eq_ref, ek_ref, ybuf_ref, dbuf_ref,
     res_ref, xhat1_ref, rstd1_ref, xhat2_ref, rstd2_ref, a_ref, b_ref, o_ref, qs_ref, k_ref, v_ref,
-    p_ref, m_ref, gp_ref, gb_ref, du_ref, dh_ref, dhb_ref, do_ref, dqkv_ref, dk_ref, dv_ref,
+    p_ref, m_ref, gp_ref, gb_ref, du_ref, dh_ref, dhb_ref, do_ref, prod_ref, dqkv_ref, dk_ref, dv_ref,
     left_ref, aqkv_ref, aout_ref, aup_ref, adown_ref, again_ref,
 ):
     step = pl.program_id(0)
     last = pl.num_programs(0) - 1
     sec = sec_ref[0]
     first = sec == 0
-    length = x_ref.shape[1]
+    length = x_hbm.shape[0]
+    loads = [
+        pltpu.make_async_copy(x_hbm, xin_ref, insem.at[0]),
+        pltpu.make_async_copy(cot_hbm, cin_ref, insem.at[1]),
+    ]
+
+    def spread(tokens_ref, rows_ref):
+        count = tokens_ref.shape[1]
+        for p in range(2):
+            wide_ref[p] = tokens_ref[:, :, 128 * p : 128 * p + 128].astype(F32).reshape(length * count, 128)
+        for r in range(count // 2):
+            rows_ref[r, LP - 16 : LP, :] = jnp.zeros((16, D), BF)
+            for p in range(2):
+                row = wide_ref[p, pl.ds(sec * (count // 2) + r, length, stride=count), :]
+                rows_ref[r, 0:length, 128 * p : 128 * p + 128] = row.astype(BF)
+
+
+    copies = []
+    for mine, other, held in (
+        (wqkv_mine, wqkv_other, wqkv_ref), (wout_mine, wout_other, wout_ref),
+        (wup_mine, wup_other, wup_ref), (wdown_mine, wdown_other, wdown_ref),
+    ):
+        copies.append(pltpu.make_async_copy(mine.at[0], held.at[sec], wsem.at[len(copies)]))
+        copies.append(pltpu.make_async_copy(other.at[0], held.at[1 - sec], wsem.at[len(copies)]))
 
     @pl.when(step == 0)
     def _():
-        copies = []
-        for mine, other, held in (
-            (wqkv_mine, wqkv_other, wqkv_ref), (wout_mine, wout_other, wout_ref),
-            (wup_mine, wup_other, wup_ref), (wdown_mine, wdown_other, wdown_ref),
-        ):
-            copies.append(pltpu.make_async_copy(mine.at[0], held.at[sec], wsem.at[len(copies)]))
-            copies.append(pltpu.make_async_copy(other.at[0], held.at[1 - sec], wsem.at[len(copies)]))
+        loads[0].start()
         for copy in copies:
             copy.start()
-        gains_ref[0] = jnp.where(first, gmine_ref[...], gother_ref[...])
-        gains_ref[1] = jnp.where(first, gother_ref[...], gmine_ref[...])
-        for ref in (aqkv_ref, aout_ref, aup_ref, adown_ref, again_ref):
+        loads[1].start()
+        for n, (mine, other) in enumerate(((attn_mine, attn_other), (mlp_mine, mlp_other))):
+            mine, other = mine[...].astype(F32), other[...].astype(F32)
+            gains_ref[0, n : n + 1, :] = jnp.where(first, mine, other)
+            gains_ref[1, n : n + 1, :] = jnp.where(first, other, mine)
+        seg_pad_ref[...] = jnp.full(seg_pad_ref.shape, -1, jnp.int32)
+        seg_pad_ref[:, 0:length] = seg_ref[...]
+        for ref in (qs_ref, do_ref, aqkv_ref, aout_ref, aup_ref, adown_ref, again_ref):
             ref[...] = jnp.zeros_like(ref)
-        for copy in copies:
+        loads[0].wait()
+        spread(xin_ref, xrow_ref)
+        for copy in copies[:4]:
             copy.wait()
-
-    parts = ((0, 176), (176, length))
 
     def load(r):
         def tokens(lo, hi):
-            res_ref[r, lo:hi, :] = x_ref[r, lo:hi, :].astype(F32)
-            gb_ref[1, LP * r + lo : LP * r + hi, :] = cot_ref[r, lo:hi, :]
+            res_ref[r, lo:hi, :] = xrow_ref[TWO * step + r, lo:hi, :].astype(F32)
 
         def visibility():
-            seg = jnp.broadcast_to(seg_ref[r], (128, seg_ref.shape[2])).astype(F32).T[:LP]
+            row = sec * (seg_ref.shape[0] // 2) + TWO * step + r
+            seg = jnp.broadcast_to(seg_pad_ref[pl.ds(row, 1), :], (128, seg_pad_ref.shape[1])).astype(F32).T[:LP]
             lane = lax.broadcasted_iota(jnp.int32, (LP, 128), 1)
             token = lax.broadcasted_iota(jnp.int32, (LP, 128), 0)
             same = seg == (lane - 64).astype(F32)
@@ -141,9 +175,7 @@
             eq_ref[r] = jnp.where(lane < 64, jnp.where(here, 1.0, 0.0), jnp.where(same, 1.0, 0.0)).astype(BF)
             ek_ref[r] = jnp.where(lane < 64, jnp.where(later, BIG, 0.0), jnp.where(other, BIG, 0.0)).astype(BF)
 
-        res_ref[r, LP - 16 : LP, :] = jnp.zeros((16, D), F32)
-        gb_ref[1, LP * r + LP - 16 : LP * r + LP, :] = jnp.zeros((16, D), BF)
-        return [lambda lo=lo, hi=hi: tokens(lo, hi) for lo, hi in parts] + [visibility]
+        return [lambda lo=lo, hi=hi: tokens(lo, hi) for lo, hi in PARTS] + [visibility]
 
     ones = jnp.ones((LP, 128), BF)
 
@@ -159,9 +191,9 @@
 
         def query():
             q = mm(a_ref[l, base : base + LP, :], wqkv_ref[l, :, 0:256]).astype(BF) * jnp.array(0.125, BF)
-            for p in range(2):
+            for p, lanes in PAIRS:
                 for q0, q1, _, _ in BLOCKS:
-                    qs_ref[l, r, p, 2 * q0 : 2 * q1, :] = two_heads(q[q0:q1, 128 * p : 128 * p + 128], low_mask(q1 - q0))
+                    qs_ref[l, r, pair_rows(p, q0, q1), lanes] = two_heads(q[q0:q1, lanes], low_mask(q1 - q0))
 
         def key():
             k_ref[l, r] = mm(a_ref[l, base : base + LP, :], wqkv_ref[l, :, 256:512]).astype(BF)
@@ -177,7 +209,7 @@
             ek = ek_ref[r, k0:k1, :]
             held[q0] = [
                 mm_t(
-                    jnp.concatenate([qs_ref[l, r, p, 2 * q0 : 2 * q1, :], eq], axis=1),
+                    jnp.concatenate([qs_ref[l, r, pair_rows(p, q0, q1), lanes], eq], axis=1),
                     jnp.concatenate([k_ref[l, r, k0:k1, lanes], ek], axis=1),
                 )
                 for p, lanes in PAIRS
@@ -190,11 +222,10 @@
                 s = held[q0][p]
                 e = jnp.exp(s - jnp.max(s, axis=-1, keepdims=True))
                 prob = (e * (1.0 / jnp.sum(e, axis=-1, keepdims=True))).astype(BF)
-                p_ref[l, r, p, 2 * q0 : 2 * q1, 0 : k1 - k0] = prob
+                p_ref[l, r, pair_rows(p, q0, q1), 0 : k1 - k0] = prob
                 probs.append(prob)
-            for p, lanes in PAIRS:
-                o = mm(probs[p], v_ref[l, r, k0:k1, lanes])
-                o_ref[l, base + q0 : base + q1, lanes] = one_pair(o, n, low_mask(n)).astype(BF)
+            o = mm(jnp.concatenate(probs, axis=0), v_ref[l, r, k0:k1, :])
+            o_ref[l, base + q0 : base + q1, :] = one_row(o, n).astype(BF)
 
         def out(lo, hi):
             h = res_ref[r, lo:hi, :] + mm(o_ref[l, base + lo : base + hi, :], wout_ref[l])
@@ -209,7 +240,7 @@
         first = [lambda b=b: scores(*b) for b in BLOCKS]
         second = [lambda b=b: mix(*b) for b in BLOCKS]
         units += [first[0], first[1], second[0], first[2], second[1], first[3], second[2], second[3]]
-        units += [lambda lo=lo, hi=hi: out(lo, hi) for lo, hi in PARTS]
+        units += [lambda lo=lo, hi=hi: out(lo, hi) for lo, hi in WHOLE]
         return units
 
     def mlp_forward(r, l):
@@ -235,8 +266,7 @@
                 yk_ref[r, lo:end, :] = jnp.where(first, y0, y1)
                 ys_ref[r, lo:end, :] = jnp.where(first, y1, y0)
 
-        return [f for lo, hi in PARTS for f in (
-            lambda lo=lo, hi=hi: chunk(0, lo, hi), lambda lo=lo, hi=hi: chunk(2, lo, hi), lambda lo=lo, hi=hi: down(lo, hi))]
+        return [lambda: chunk(0, 0, LP), lambda: chunk(2, 0, LP), lambda: down(0, LP)]
 
     def mlp_backward(r, l):
         base = LP * r
@@ -258,8 +288,8 @@
             dhb_ref[l, rows, :] = d_h.astype(BF)
 
         return (
-            [lambda c=c, lo=lo, hi=hi: chunk(c, lo, hi) for c in (0, 2) for lo, hi in PARTS]
-            + [lambda lo=lo, hi=hi: back(lo, hi) for lo, hi in PARTS]
+            [lambda c=c, lo=lo, hi=hi: chunk(c, lo, hi) for c in (0, 2) for lo, hi in WHOLE]
+            + [lambda lo=lo, hi=hi: back(lo, hi) for lo, hi in WHOLE]
         )
 
     def attn_backward(r, l):
@@ -268,38 +298,43 @@
         def out():
             d_o = mm_t(dhb_ref[l, base : base + LP, :], wout_ref[l]).astype(BF)
             prod = (-(d_o.astype(F32) * o_ref[l, base : base + LP, :].astype(F32))).astype(BF)
-            for p in range(2):
-                lanes = slice(128 * p, 128 * p + 128)
+            for p, lanes in PAIRS:
                 for q0, q1, _, _ in BLOCKS:
                     mask = low_mask(q1 - q0)
-                    do_ref[r, p, 2 * q0 : 2 * q1, 0:128] = two_heads(d_o[q0:q1, lanes], mask)
-                    do_ref[r, p, 2 * q0 : 2 * q1, 128:256] = two_heads(prod[q0:q1, lanes], mask)
+                    do_ref[r, pair_rows(p, q0, q1), lanes] = two_heads(d_o[q0:q1, lanes], mask)
+                    prod_ref[r, pair_rows(p, q0, q1), :] = two_heads(prod[q0:q1, lanes], mask)
             dk_ref[r] = jnp.zeros((LP, D), F32)
             dv_ref[r] = jnp.zeros((LP, D), F32)
 
         held = {}
 
         def probs(q0, q1, k0, k1):
-            rows = slice(2 * q0, 2 * q1)
             held[q0] = [
-                mm_t(do_ref[r, p, rows, :], jnp.concatenate([v_ref[l, r, k0:k1, lanes], ones[k0:k1]], axis=1))
+                mm_t(
+                    jnp.concatenate(
+                        [do_ref[r, pair_rows(p, q0, q1), lanes], prod_ref[r, pair_rows(p, q0, q1), :]], axis=1
+                    ),
+                    jnp.concatenate([v_ref[l, r, k0:k1, lanes], ones[k0:k1]], axis=1),
+                )
                 for p, lanes in PAIRS
             ]
 
         def values(q0, q1, k0, k1):
-            rows = slice(2 * q0, 2 * q1)
-            for p, lanes in PAIRS:
-                dv_ref[r, k0:k1, lanes] += tmm(p_ref[l, r, p, rows, 0 : k1 - k0], do_ref[r, p, rows, 0:128])
+            rows = slice(4 * q0, 4 * q1)
+            dv_ref[r, k0:k1, :] += tmm(p_ref[l, r, rows, 0 : k1 - k0], do_ref[r, rows, :])
 
         def queries(q0, q1, k0, k1):
             n = q1 - q0
-            rows = slice(2 * q0, 2 * q1)
-            ds = [(p_ref[l, r, p, rows, 0 : k1 - k0].astype(F32) * held[q0][p]).astype(BF) for p, _ in PAIRS]
-            for p, lanes in PAIRS:
-                dq = mm(ds[p], k_ref[l, r, k0:k1, lanes])
-                dqkv_ref[l, base + q0 : base + q1, lanes] = (one_pair(dq, n, low_mask(n)) * 0.125).astype(BF)
-            for p, lanes in PAIRS:
-                dk_ref[r, k0:k1, lanes] += tmm(ds[p], qs_ref[l, r, p, rows, :])
+            ds = jnp.concatenate(
+                [
+                    (p_ref[l, r, pair_rows(p, q0, q1), 0 : k1 - k0].astype(F32) * held[q0][p]).astype(BF)
+                    for p, _ in PAIRS
+                ],
+                axis=0,
+            )
+            dq = mm(ds, k_ref[l, r, k0:k1, :])
+            dqkv_ref[l, base + q0 : base + q1, 0:256] = (one_row(dq, n) * 0.125).astype(BF)
+            dk_ref[r, k0:k1, :] += tmm(ds, qs_ref[l, r, 4 * q0 : 4 * q1, :])
 
         def finish(lo, hi):
             rows = slice(base + lo, base + hi)
@@ -323,7 +358,7 @@
         return (
             [out]
             + [lambda f=f, b=BLOCKS[i]: f(*b) for f, i in order]
-            + [lambda lo=lo, hi=hi: finish(lo, hi) for lo, hi in PARTS]
+            + [lambda lo=lo, hi=hi: finish(lo, hi) for lo, hi in WHOLE]
         )
 
     def turn(j, ref, l):
@@ -357,15 +392,27 @@
 
         return [lambda: turn(2, o_ref, l), lambda: turn(3, a_ref, l), out_and_query, key_and_value]
 
-    merged(load(0) + attn_forward(0, 0))
-    merged(mlp_forward(0, 0), load(1) + attn_forward(1, 0))
-    merged(attn_forward(0, 1), mlp_forward(1, 0))
-    merged(mlp_forward(0, 1), attn_forward(1, 1))
-    merged(mlp_backward(0, 1), mlp_forward(1, 1))
-    merged(attn_backward(0, 1), mlp_backward(1, 1))
-    merged(mlp_backward(0, 0), attn_backward(1, 1), mlp_weights(1))
-    merged(attn_backward(0, 0), mlp_backward(1, 0), attn_weights(1))
-    merged(attn_backward(1, 0), mlp_weights(0))
+    merged(load(0) + attn_forward(0, 0), load(1) + attn_forward(1, 0))
+
+    @pl.when(step == 0)
+    def _():
+        for copy in copies[4:]:
+            copy.wait()
+        loads[1].wait()
+        spread(cin_ref, crow_ref)
+
+    merged(mlp_forward(0, 0), mlp_forward(1, 0))
+    merged(attn_forward(0, 1), attn_forward(1, 1))
+    merged(mlp_forward(0, 1), mlp_forward(1, 1))
+    for r in range(TWO):
+        gb_ref[1, LP * r : LP * r + LP, :] = crow_ref[TWO * step + r]
+    merged(mlp_backward(0, 1), mlp_backward(1, 1))
+    merged(mlp_weights(1))
+    merged(attn_backward(0, 1), attn_backward(1, 1))
+    merged(attn_weights(1))
+    merged(mlp_backward(0, 0), mlp_backward(1, 0))
+    merged(mlp_weights(0))
+    merged(attn_backward(0, 0), attn_backward(1, 0))
     merged(attn_weights(0))
 
     @pl.when(step == last)
@@ -386,10 +433,8 @@
 
 
 def local_step(section, x, cot, segments, gains, other_gains, mine, other):
-    rows, length, _ = x.shape
+    length, rows, _ = x.shape
     steps = rows // 2 // TWO
-    place = lambda i, sec: (sec[0] * steps + i, 0, 0)
-    tok = lambda w: pl.BlockSpec((TWO, length, w), place)
     row_out = pl.BlockSpec((TWO, length, D), lambda i, sec: (i, 0, 0))
     whole = lambda shape: pl.BlockSpec(shape, lambda i, sec: (0,) * len(shape), pipeline_mode=pl.Buffered(1))
     hbm = pl.BlockSpec(memory_space=pl.ANY)
@@ -401,31 +446,32 @@
         grid_spec=pltpu.PrefetchScalarGridSpec(
             num_scalar_prefetch=1,
             grid=(steps,),
-            in_specs=[tok(D), tok(D), pl.BlockSpec((TWO, 1, segments.shape[2]), place), whole((2, D)), whole((2, D))] + [hbm] * 8,
-            out_specs=[tok(D), row_out, tok(D), row_out, whole((1552, D)), whole((1536, D)), whole((1552, D)), whole((1536, D))],
+            in_specs=[whole(segments.shape)] + [whole((1, D))] * 4 + [hbm] * 10,
+            out_specs=[row_out, row_out, row_out, row_out, whole((1552, D)), whole((1536, D)), whole((1552, D)), whole((1536, D))],
             scratch_shapes=[
-                vm((2, D, 3 * D), BF), vm((2, D, D), BF), vm((2, D, FF), BF), vm((2, FF, D), BF), pltpu.SemaphoreType.DMA((8,)),
+                vm((2, D, 3 * D), BF), vm((2, D, D), BF), vm((2, D, FF), BF), vm((2, FF, D), BF), pltpu.SemaphoreType.DMA((8,)), pltpu.SemaphoreType.DMA((2,)), vm(x.shape, BF), vm(x.shape, BF),
+                vm((2, length * rows, 128), F32), vm((rows // 2, LP, D), BF), vm((rows // 2, LP, D), BF), vm((rows, 384), jnp.int32),
                 vm((2, 2, D), F32), vm((TWO, LP, 128), BF), vm((TWO, LP, 128), BF), vm((TWO, LP, D), BF), vm((TWO, LP, D), F32),
                 vm((TWO, LP, D), F32),
                 vm((2, TWO, LP, D), F32), vm((2, TWO, LP, 128), F32), vm((2, TWO, LP, D), F32), vm((2, TWO, LP, 128), F32),
                 flat(D), flat(D), flat(D),
-                vm((2, TWO, 2, 2 * LP, 128), BF), vm((2, TWO, LP, D), BF), vm((2, TWO, LP, D), BF),
-                vm((2, TWO, 2, 2 * LP, D), BF), flat(FF), vm((2, TWO, LP, FF), BF),
+                vm((2, TWO, 4 * LP, D), BF), vm((2, TWO, LP, D), BF), vm((2, TWO, LP, D), BF),
+                vm((2, TWO, 4 * LP, D), BF), flat(FF), vm((2, TWO, LP, FF), BF),
                 flat(D), flat(FF), vm((TWO, LP, D), F32), flat(D),
-                vm((TWO, 2, 2 * LP, D), BF), flat(3 * D), vm((TWO, LP, D), F32), vm((TWO, LP, D), F32),
+                vm((TWO, 4 * LP, D), BF), vm((TWO, 4 * LP, 128), BF), flat(3 * D), vm((TWO, LP, D), F32), vm((TWO, LP, D), F32),
                 vm((4, D, TWO * LP), BF), vm((2, D, 3 * D), F32), vm((2, D, D), F32), vm((2, D, FF), F32), vm((2, D, FF), F32),
                 vm((2, 2, 8, D), F32),
             ],
         ),
         out_shape=[
-            shape((rows, length, D), BF), shape((rows // 2, length, D), BF),
-            shape((rows, length, D), F32), shape((rows // 2, length, D), BF),
+            shape((rows // 2, length, D), BF), shape((rows // 2, length, D), BF),
+            shape((rows // 2, length, D), F32), shape((rows // 2, length, D), BF),
             shape((1552, D), BF), shape((1536, D), BF), shape((1552, D), BF), shape((1536, D), BF),
         ],
         compiler_params=pltpu.CompilerParams(
             dimension_semantics=("arbitrary",), vmem_limit_bytes=60 * 1024 * 1024
         ),
-    )(section, x, cot, segments, gains, other_gains, *mine, *other)
+    )(section, segments, *gains, *other_gains, x, cot, *mine, *other)
 
 
 def partner(value):
@@ -491,23 +537,24 @@
     layer_input, out_cotangent, segment_ids, gain_attn, weight_qkv, weight_out, gain_mlp, weight_up, weight_down
 ):
     section = lax.axis_index("section")
-    rows, length, _ = layer_input.shape
-    half = rows // 2
-    gains = jnp.concatenate([gain_attn, gain_mlp], axis=0)
+    gains = (gain_attn, gain_mlp)
     mine = (weight_qkv, weight_out, weight_up, weight_down)
     other = tuple(partner(w) for w in mine)
-    other_gains = partner(gains)
-    segments = jnp.pad(segment_ids, ((0, 0), (0, 384 - length)), constant_values=-1)[:, None, :]
+    other_gains = tuple(partner(g) for g in gains)
     acts, acts_send, grads, grads_send, first, second, first_send, second_send = local_step(
-        section[None].astype(jnp.int32), layer_input, out_cotangent, segments,
-        gains.astype(F32), other_gains.astype(F32), mine, other,
+        section[None].astype(jnp.int32), layer_input.swapaxes(0, 1), out_cotangent.swapaxes(0, 1), segment_ids,
+        gains, other_gains, mine, other,
     )
     got = partner(first_send), partner(second_send)
     parts = add(first, got[0]), add(second, got[1])
+    low = section == 0
+
+    def whole_rows(keep, got):
+        return jnp.concatenate([jnp.where(low, keep, got), jnp.where(low, got, keep)], axis=0)
+
+    activations = whole_rows(acts, partner(acts_send))
+    input_grads = whole_rows(grads, partner(grads_send).astype(F32))
     ((qkv, out_up), (up_down, down)), rest = sum_over_dp(parts, 16, section)
-    there = (1 - section) * half
-    activations = lax.dynamic_update_slice_in_dim(acts, partner(acts_send), there, 0)
-    input_grads = lax.dynamic_update_slice_in_dim(grads, partner(grads_send).astype(F32), there, 0)
     side = lambda *blocks: jnp.concatenate(blocks, axis=1).astype(F32)
     return (
         activations[None],

time: 120 us -> 115 us (0.958)
  local copies, waits for them, and re-layouts: 14.5 us -> 6.86 us
  waiting for transfers between devices: 20.6 us -> 25.8 us
  other arithmetic: 9.2 us -> 6.63 us
  Pallas kernels: 43.2 us -> 41.4 us
  starting transfers between devices: 31.3 us -> 33.1 us
    ppermute x9 -> x10, waiting for transfers between devices: 0.96 us -> 6.93 us  [partner(): return lax.ppermute(value, 'section', [(0, 1), (1, 0)])]
    unnamed x24, local copies, waits for them, and re-layouts: 9.7 us -> 4.84 us
    pallas_call x2, local copies, waits for them, and re-layouts: 3.82 us -> 1.75 us  [local_step(): pl.pallas_call(kernel, grid_spec=pltpu.PrefetchScalarGridSpec(num_scalar_...]
    convert_element_type x2 -> x0, other arithmetic: 1.89 us -> none  [the longest x1 1.3 us: shards(): gains.astype(F32)]
    pallas_call x1, Pallas kernels: 43.2 us -> 41.4 us  [local_step(): pl.pallas_call(kernel, grid_spec=pltpu.PrefetchScalarGridSpec(num_scalar_...]
    ppermute x16, starting transfers between devices: 28.7 us -> 30 us  [cross(): return lax.ppermute(value, ('section', 'dp'), pairs)]
    convert_element_type x10, other arithmetic: 2.13 us -> 0.85 us  [add(): return (a.astype(F32) + b.astype(F32)).astype(BF)]
    ppermute x9 -> x10, starting transfers between devices: 2.62 us -> 3.06 us  [partner(): return lax.ppermute(value, 'section', [(0, 1), (1, 0)])]
  transfers between devices with their start and end apart: 25 -> 26, of which waited for: 15 -> 19; matrix products, arithmetic and copies ran while one was open for 14% -> 7% of each run, Pallas kernels for 0% -> 0%
where the time goes in v3:
time: 115 us
  Pallas kernels  41.4 us (36%)
  starting transfers between devices  33.1 us (29%)
  waiting for transfers between devices  25.8 us (22%)
  local copies, waits for them, and re-layouts  6.86 us (6%)
  other arithmetic  6.63 us (6%)
    pallas_call x1, Pallas kernels, local_step(): pl.pallas_call(kernel, grid_spec=pltpu.PrefetchScalarGridSpec(num_scalar_...  41.4 us
    ppermute x16, starting transfers between devices, cross(): return lax.ppermute(value, ('section', 'dp'), pairs)  30 us
    ppermute x16, waiting for transfers between devices, cross(): return lax.ppermute(value, ('section', 'dp'), pairs)  18.9 us
    ppermute x10, waiting for transfers between devices, partner(): return lax.ppermute(value, 'section', [(0, 1), (1, 0)])  6.93 us
    unnamed x24, local copies, waits for them, and re-layouts  4.84 us
    ppermute x10, starting transfers between devices, partner(): return lax.ppermute(value, 'section', [(0, 1), (1, 0)])  3.06 us
  transfers between devices with their start and end apart: 26, of which 19 were waited for; matrix products, arithmetic and copies ran while one was open for 7% of the time, Pallas kernels for 0%

profile of v3, /device:TPU:0, one launch (start us, length us, event | category | flops | bytes accessed | tf_op | source)
XLA Modules:
  0.0 114.8 jit_solution(7696552372850124709)
XLA Ops:
  2.2 2.2 %collective-permute-done.attn_other = bf16[1,256]{1,0:T(2,128)(2,1)S(1)} collective-permute-done((bf16[1,256]{1,0:T(2,128)(2,1)}, bf16[1,256]{1,0:T(2,128)(2,1)S(1)}, u32[]{:S(2)}, u32[]{:S(2)}) %collective-permute-start) | collective-permute-done | bytes 544 | tf_op jit(solution)/shard_map/ppermute | solution.py:478
  4.8 1.0 collective-permute-done.1.mlp_other
  6.9 41.4 %shard_map.152 = (bf16[4,340,256]{2,1,0:T(8,128)(2,1)}, bf16[4,340,256]{2,1,0:T(8,128)(2,1)}, f32[4,340,256]{2,1,0:T(8,128)}, bf16[4,340,256]{2,1,0:T(8,128)(2,1...) custom-call(s32[1]{0:T(128)} %bitcast.sec_ref, ...), custom_call_target="tpu_custom_call" | custom-call | tf_op jit(solution)/shard_map/pallas_call | solution.py:444
  48.3 1.5 %copy.19 = bf16[4,340,256]{2,0,1:T(4,128)(2,1)S(1)} copy(bf16[4,340,256]{2,1,0:T(8,128)(2,1)} %get-tuple-element.17) | data formatting | bytes 1392640 | tf_op jit(solution)/shard_map/pallas_call | solution.py:444
  52.2 1.8 %collective-permute-done.7 = bf16[4,340,256]{2,0,1:T(4,128)(2,1)S(1)} collective-permute-done((bf16[4,340,256]{2,0,1:T(4,128)(2,1)S(1)}, bf16[4,340,256]{2,0,1:T(4,128)(2,1)S(1)}, u32[]{:S(2)}, u32[]{:S(2)}) %collective-permute-start.7) | collective-permute-done | bytes 696352 | tf_op jit(solution)/shard_map/ppermute | solution.py:478
  55.8 2.9 %collective-permute-start.18 = (bf16[768,256]{1,0:T(8,128)(2,1)S(1)}, bf16[768,256]{1,0:T(8,128)(2,1)S(1)}, u32[]{:S(2)}, u32[]{:S(2)}) collective-permute-start(bf16[768,256]{1,0:T(8,128)(2,1)S(1)} %constant_dynamic-slice_fusion.3), channel_id=1, source_target_pairs={{0,1},{1,0},{2,3},{3,2},{4,5},{5,4},{6,7},{7,6},{8,9},{9,8},{10,11... | collective-permute-start | bytes 1179656 | tf_op jit(solution)/shard_map/ppermute | solution.py:483
  60.0 1.4 %copy.24 = bf16[1,8,340,256]{3,1,2,0:T(8,128)(2,1)} copy(bf16[1,8,340,256]{3,2,1,0:T(8,128)(2,1)S(1)} %maximum_bitcast_fusion.1) | data formatting | bytes 2785280
  61.4 2.4 %copy.25 = f32[1,8,340,256]{3,1,2,0:T(8,128)} copy(f32[1,8,340,256]{3,2,1,0:T(8,128)S(1)} %maximum_bitcast_fusion) | data formatting | bytes 5570560
  64.5 2.2 %collective-permute-start.19 = (bf16[384,256]{1,0:T(8,128)(2,1)S(1)}, bf16[384,256]{1,0:T(8,128)(2,1)S(1)}, u32[]{:S(2)}, u32[]{:S(2)}) collective-permute-start(bf16[384,256]{1,0:T(8,128)(2,1)S(1)} %constant_dynamic-slice_fusion.2), channel_id=1, source_target_pairs={{0,4},{1,5},{2,6},{3,7},{4,0},{5,1},{6,2},{7,3},{8,12},{9,13},{10,... | collective-permute-start | bytes 589832 | tf_op jit(solution)/shard_map/ppermute | solution.py:483
  66.7 2.0 %collective-permute-done.9 = bf16[784,256]{1,0:T(8,128)(2,1)S(1)} collective-permute-done((bf16[784,256]{1,0:T(8,128)(2,1)S(1)}, bf16[784,256]{1,0:T(8,128)(2,1)S(1)}, u32[]{:S(2)}, u32[]{:S(2)}) %collective-permute-start.9) | collective-permute-done | bytes 401440 | tf_op jit(solution)/shard_map/ppermute | solution.py:483
  68.9 2.1 %collective-permute-start.10 = (bf16[400,256]{1,0:T(8,128)(2,1)S(1)}, bf16[400,256]{1,0:T(8,128)(2,1)S(1)}, u32[]{:S(2)}, u32[]{:S(2)}) collective-permute-start(bf16[400,256]{1,0:T(8,128)(2,1)S(1)} %pad_maximum_fusion.4), channel_id=1, source_target_pairs={{0,2},{1,3},{2,0},{3,1},{4,6},{5,7},{6,4},{7,5},{8,10},{9,11},{10,... | collective-permute-start | bytes 614408 | tf_op jit(solution)/shard_map/ppermute | solution.py:483
  71.2 1.8 %collective-permute-start.20 = (bf16[192,256]{1,0:T(8,128)(2,1)S(1)}, bf16[192,256]{1,0:T(8,128)(2,1)S(1)}, u32[]{:S(2)}, u32[]{:S(2)}) collective-permute-start(bf16[192,256]{1,0:T(8,128)(2,1)S(1)} %constant_dynamic-slice_fusion.1), channel_id=1, source_target_pairs={{0,2},{1,3},{2,0},{3,1},{4,6},{5,7},{6,4},{7,5},{8,10},{9,11},{10,... | collective-permute-start | bytes 294920 | tf_op jit(solution)/shard_map/ppermute | solution.py:483
  73.0 1.8 %collective-permute-done.10 = bf16[400,256]{1,0:T(8,128)(2,1)S(1)} collective-permute-done((bf16[400,256]{1,0:T(8,128)(2,1)S(1)}, bf16[400,256]{1,0:T(8,128)(2,1)S(1)}, u32[]{:S(2)}, u32[]{:S(2)}) %collective-permute-start.10) | collective-permute-done | bytes 204832 | tf_op jit(solution)/shard_map/ppermute | solution.py:483
  74.9 2.1 %collective-permute-start.11 = (bf16[208,256]{1,0:T(8,128)(2,1)S(1)}, bf16[208,256]{1,0:T(8,128)(2,1)S(1)}, u32[]{:S(2)}, u32[]{:S(2)}) collective-permute-start(bf16[208,256]{1,0:T(8,128)(2,1)S(1)} %pad_maximum_fusion.8), channel_id=1, source_target_pairs={{0,4},{1,5},{2,6},{3,7},{4,0},{5,1},{6,2},{7,3},{8,12},{9,13},{10,... | collective-permute-start | bytes 319496 | tf_op jit(solution)/shard_map/ppermute | solution.py:483
  77.1 2.7 %collective-permute-start.21 = (bf16[96,256]{1,0:T(8,128)(2,1)S(1)}, bf16[96,256]{1,0:T(8,128)(2,1)S(1)}, u32[]{:S(2)}, u32[]{:S(2)}) collective-permute-start(bf16[96,256]{1,0:T(8,128)(2,1)S(1)} %constant_dynamic-slice_fusion), channel_id=1, source_target_pairs={{0,8},{1,9},{2,10},{3,11},{4,12},{5,13},{6,14},{7,15},{8,0},{9,1},... | collective-permute-start | bytes 147464 | tf_op jit(solution)/shard_map/ppermute | solution.py:483
  80.3 2.6 %collective-permute-start.12 = (bf16[112,256]{1,0:T(8,128)(2,1)S(1)}, bf16[112,256]{1,0:T(8,128)(2,1)S(1)}, u32[]{:S(2)}, u32[]{:S(2)}) collective-permute-start(bf16[112,256]{1,0:T(8,128)(2,1)S(1)} %pad_maximum_fusion.12), channel_id=1, source_target_pairs={{0,8},{1,9},{2,10},{3,11},{4,12},{5,13},{6,14},{7,15},{8,0},{9,1},... | collective-permute-start | bytes 172040 | tf_op jit(solution)/shard_map/ppermute | solution.py:483
  83.6 1.4 %collective-permute-start.22 = (bf16[96,256]{1,0:T(8,128)(2,1)S(1)}, bf16[96,256]{1,0:T(8,128)(2,1)S(1)}, u32[]{:S(2)}, u32[]{:S(2)}) collective-permute-start(bf16[96,256]{1,0:T(8,128)(2,1)S(1)} %add_convert_fusion.9), channel_id=1, source_target_pairs={{0,8},{1,9},{2,10},{3,11},{4,12},{5,13},{6,14},{7,15},{8,0},{9,1},... | collective-permute-start | bytes 147464 | tf_op jit(solution)/shard_map/ppermute | solution.py:483
  85.7 2.4 %collective-permute-start.13 = (bf16[96,256]{1,0:T(8,128)(2,1)S(1)}, bf16[96,256]{1,0:T(8,128)(2,1)S(1)}, u32[]{:S(2)}, u32[]{:S(2)}) collective-permute-start(bf16[96,256]{1,0:T(8,128)(2,1)S(1)} %slice.75), channel_id=1, source_target_pairs={{0,8},{1,9},{2,10},{3,11},{4,12},{5,13},{6,14},{7,15},{8,0},{9,1},... | collective-permute-start | bytes 147464 | tf_op jit(solution)/shard_map/ppermute | solution.py:483
  88.1 1.0 collective-permute-done.22
  89.2 1.1 collective-permute-start.23
  90.9 2.0 %collective-permute-start.14 = (bf16[192,256]{1,0:T(8,128)(2,1)S(1)}, bf16[192,256]{1,0:T(8,128)(2,1)S(1)}, u32[]{:S(2)}, u32[]{:S(2)}) collective-permute-start(bf16[192,256]{1,0:T(8,128)(2,1)S(1)} %pad_maximum_fusion.10), channel_id=1, source_target_pairs={{0,4},{1,5},{2,6},{3,7},{4,0},{5,1},{6,2},{7,3},{8,12},{9,13},{10,... | collective-permute-start | bytes 294920 | tf_op jit(solution)/shard_map/ppermute | solution.py:483
  92.8 1.0 collective-permute-done.23
  93.9 1.6 %collective-permute-start.24 = (bf16[384,256]{1,0:T(8,128)(2,1)S(1)}, bf16[384,256]{1,0:T(8,128)(2,1)S(1)}, u32[]{:S(2)}, u32[]{:S(2)}) collective-permute-start(bf16[384,256]{1,0:T(8,128)(2,1)S(1)} %pad_maximum_fusion.7), channel_id=1, source_target_pairs={{0,4},{1,5},{2,6},{3,7},{4,0},{5,1},{6,2},{7,3},{8,12},{9,13},{10,... | collective-permute-start | bytes 589832 | tf_op jit(solution)/shard_map/ppermute | solution.py:483
  95.6 1.7 %collective-permute-start.15 = (bf16[384,256]{1,0:T(8,128)(2,1)S(1)}, bf16[384,256]{1,0:T(8,128)(2,1)S(1)}, u32[]{:S(2)}, u32[]{:S(2)}) collective-permute-start(bf16[384,256]{1,0:T(8,128)(2,1)S(1)} %pad_maximum_fusion.6), channel_id=1, source_target_pairs={{0,2},{1,3},{2,0},{3,1},{4,6},{5,7},{6,4},{7,5},{8,10},{9,11},{10,... | collective-permute-start | bytes 589832 | tf_op jit(solution)/shard_map/ppermute | solution.py:483
  97.3 2.4 %collective-permute-done.24 = bf16[384,256]{1,0:T(8,128)(2,1)S(1)} collective-permute-done((bf16[384,256]{1,0:T(8,128)(2,1)S(1)}, bf16[384,256]{1,0:T(8,128)(2,1)S(1)}, u32[]{:S(2)}, u32[]{:S(2)}) %collective-permute-start.24) | collective-permute-done | bytes 196640 | tf_op jit(solution)/shard_map/ppermute | solution.py:483
  99.8 1.1 collective-permute-start.25
  101.4 2.1 %collective-permute-done.15 = bf16[384,256]{1,0:T(8,128)(2,1)S(1)} collective-permute-done((bf16[384,256]{1,0:T(8,128)(2,1)S(1)}, bf16[384,256]{1,0:T(8,128)(2,1)S(1)}, u32[]{:S(2)}, u32[]{:S(2)}) %collective-permute-start.15) | collective-permute-done | bytes 196640 | tf_op jit(solution)/shard_map/ppermute | solution.py:483
  103.6 1.6 %collective-permute-start.16 = (bf16[768,256]{1,0:T(8,128)(2,1)S(1)}, bf16[768,256]{1,0:T(8,128)(2,1)S(1)}, u32[]{:S(2)}, u32[]{:S(2)}) collective-permute-start(bf16[768,256]{1,0:T(8,128)(2,1)S(1)} %pad_maximum_fusion.2), channel_id=1, source_target_pairs={{0,1},{1,0},{2,3},{3,2},{4,5},{5,4},{6,7},{7,6},{8,9},{9,8},{10,11... | collective-permute-start | bytes 1179656 | tf_op jit(solution)/shard_map/ppermute | solution.py:483
  105.3 2.4 %collective-permute-done.25 = bf16[768,256]{1,0:T(8,128)(2,1)S(1)} collective-permute-done((bf16[768,256]{1,0:T(8,128)(2,1)S(1)}, bf16[768,256]{1,0:T(8,128)(2,1)S(1)}, u32[]{:S(2)}, u32[]{:S(2)}) %collective-permute-start.25) | collective-permute-done | bytes 393248 | tf_op jit(solution)/shard_map/ppermute | solution.py:483
  107.8 1.0 maximum_convert_fusion.1
  108.8 3.0 %collective-permute-done.16 = bf16[768,256]{1,0:T(8,128)(2,1)S(1)} collective-permute-done((bf16[768,256]{1,0:T(8,128)(2,1)S(1)}, bf16[768,256]{1,0:T(8,128)(2,1)S(1)}, u32[]{:S(2)}, u32[]{:S(2)}) %collective-permute-start.16) | collective-permute-done | bytes 393248 | tf_op jit(solution)/shard_map/ppermute | solution.py:483
  113.7 1.1 maximum_convert_fusion
  (98 shorter events, 15.0 us)
Async XLA Ops:
  0.6 5.2 %collective-permute-start.4 = (bf16[1,256,1024]{2,1,0:T(8,128)(2,1)}, bf16[1,256,1024]{2,1,0:T(8,128)(2,1)S(1)}, u32[]{:S(2)}, u32[]{:S(2)}) collective-permute-start(bf16[1,256,1024]{2,1,0:T(8,128)(2,1)} %wup_mine.1), channel_id=1, source_target_pairs={{0,16},{16,0},{1,17},{17,1},{2,18},{18,2},{3,19},{19,3},{4,20},{20... | collective-permute-start | bytes 1572872 | tf_op jit(solution)/shard_map/ppermute | solution.py:478
  1.2 4.7 %collective-permute-start.5 = (bf16[1,1024,256]{2,1,0:T(8,128)(2,1)}, bf16[1,1024,256]{2,1,0:T(8,128)(2,1)S(1)}, u32[]{:S(2)}, u32[]{:S(2)}) collective-permute-start(bf16[1,1024,256]{2,1,0:T(8,128)(2,1)} %wdown_mine.1), channel_id=1, source_target_pairs={{0,16},{16,0},{1,17},{17,1},{2,18},{18,2},{3,19},{19,3},{4,20},{20... | collective-permute-start | bytes 1572872 | tf_op jit(solution)/shard_map/ppermute | solution.py:478
  1.2 4.6 %collective-permute-start.2 = (bf16[1,256,768]{2,1,0:T(8,128)(2,1)}, bf16[1,256,768]{2,1,0:T(8,128)(2,1)S(1)}, u32[]{:S(2)}, u32[]{:S(2)}) collective-permute-start(bf16[1,256,768]{2,1,0:T(8,128)(2,1)} %wqkv_mine.1), channel_id=1, source_target_pairs={{0,16},{16,0},{1,17},{17,1},{2,18},{18,2},{3,19},{19,3},{4,20},{20... | collective-permute-start | bytes 1179656 | tf_op jit(solution)/shard_map/ppermute | solution.py:478
  1.7 4.1 %collective-permute-start.3 = (bf16[1,256,256]{2,1,0:T(8,128)(2,1)}, bf16[1,256,256]{2,1,0:T(8,128)(2,1)S(1)}, u32[]{:S(2)}, u32[]{:S(2)}) collective-permute-start(bf16[1,256,256]{2,1,0:T(8,128)(2,1)} %wout_mine.1), channel_id=1, source_target_pairs={{0,16},{16,0},{1,17},{17,1},{2,18},{18,2},{3,19},{19,3},{4,20},{20... | collective-permute-start | bytes 393224 | tf_op jit(solution)/shard_map/ppermute | solution.py:478
  1.7 2.7 %collective-permute-start = (bf16[1,256]{1,0:T(2,128)(2,1)}, bf16[1,256]{1,0:T(2,128)(2,1)S(1)}, u32[]{:S(2)}, u32[]{:S(2)}) collective-permute-start(bf16[1,256]{1,0:T(2,128)(2,1)} %attn_mine.1), channel_id=1, source_target_pairs={{0,16},{16,0},{1,17},{17,1},{2,18},{18,2},{3,19},{19,3},{4,20},{20... | collective-permute-start | bytes 1544 | tf_op jit(solution)/shard_map/ppermute | solution.py:478
  4.4 1.5 %copy-start.9 = (bf16[1,256]{1,0:T(2,128)(2,1)}, bf16[1,256]{1,0:T(2,128)(2,1)S(1)}, u32[]{:S(2)}) copy-start(bf16[1,256]{1,0:T(2,128)(2,1)S(1)} %collective-permute-done.attn_other) | copy-start | bytes 1540
  4.4 1.4 %collective-permute-start.1 = (bf16[1,256]{1,0:T(2,128)(2,1)}, bf16[1,256]{1,0:T(2,128)(2,1)S(1)}, u32[]{:S(2)}, u32[]{:S(2)}) collective-permute-start(bf16[1,256]{1,0:T(2,128)(2,1)} %mlp_mine.1), channel_id=1, source_target_pairs={{0,16},{16,0},{1,17},{17,1},{2,18},{18,2},{3,19},{19,3},{4,20},{20... | collective-permute-start | bytes 1544 | tf_op jit(solution)/shard_map/ppermute | solution.py:478
  48.3 1.9 %copy-start.3 = (bf16[4,340,256]{2,1,0:T(8,128)(2,1)S(1)}, bf16[4,340,256]{2,1,0:T(8,128)(2,1)}, u32[]{:S(2)}) copy-start(bf16[4,340,256]{2,1,0:T(8,128)(2,1)} %get-tuple-element.19) | copy-start | bytes 2088964
  48.3 3.7 %copy-start.4 = (bf16[4,340,256]{2,1,0:T(8,128)(2,1)S(1)}, bf16[4,340,256]{2,1,0:T(8,128)(2,1)}, u32[]{:S(2)}) copy-start(bf16[4,340,256]{2,1,0:T(8,128)(2,1)} %get-tuple-element.16) | copy-start | bytes 2088964
  49.8 2.2 %collective-permute-start.6 = (bf16[4,340,256]{2,0,1:T(4,128)(2,1)S(1)}, bf16[4,340,256]{2,0,1:T(4,128)(2,1)S(1)}, u32[]{:S(2)}, u32[]{:S(2)}) collective-permute-start(bf16[4,340,256]{2,0,1:T(4,128)(2,1)S(1)} %copy.19), channel_id=1, source_target_pairs={{0,16},{16,0},{1,17},{17,1},{2,18},{18,2},{3,19},{19,3},{4,20},{20... | collective-permute-start | bytes 2088968 | tf_op jit(solution)/shard_map/ppermute | solution.py:478
  50.5 3.5 %collective-permute-start.7 = (bf16[4,340,256]{2,0,1:T(4,128)(2,1)S(1)}, bf16[4,340,256]{2,0,1:T(4,128)(2,1)S(1)}, u32[]{:S(2)}, u32[]{:S(2)}) collective-permute-start(bf16[4,340,256]{2,0,1:T(4,128)(2,1)S(1)} %copy.22), channel_id=1, source_target_pairs={{0,16},{16,0},{1,17},{17,1},{2,18},{18,2},{3,19},{19,3},{4,20},{20... | collective-permute-start | bytes 2088968 | tf_op jit(solution)/shard_map/ppermute | solution.py:478
  50.7 3.3 %copy-start = (f32[4,340,256]{2,1,0:T(8,128)S(1)}, f32[4,340,256]{2,1,0:T(8,128)}, u32[]{:S(2)}) copy-start(f32[4,340,256]{2,1,0:T(8,128)} %get-tuple-element.18) | copy-start | bytes 4177924
  50.7 7.9 %collective-permute-start.8 = (bf16[1552,256]{1,0:T(8,128)(2,1)}, bf16[1552,256]{1,0:T(8,128)(2,1)S(1)}, u32[]{:S(2)}, u32[]{:S(2)}) collective-permute-start(bf16[1552,256]{1,0:T(8,128)(2,1)} %get-tuple-element.21), channel_id=1, source_target_pairs={{0,16},{16,0},{1,17},{17,1},{2,18},{18,2},{3,19},{19,3},{4,20},{20... | collective-permute-start | bytes 2383880 | tf_op jit(solution)/shard_map/ppermute | solution.py:478
  51.1 4.4 %collective-permute-start.17 = (bf16[1536,256]{1,0:T(8,128)(2,1)}, bf16[1536,256]{1,0:T(8,128)(2,1)S(1)}, u32[]{:S(2)}, u32[]{:S(2)}) collective-permute-start(bf16[1536,256]{1,0:T(8,128)(2,1)} %get-tuple-element.23), channel_id=1, source_target_pairs={{0,16},{16,0},{1,17},{17,1},{2,18},{18,2},{3,19},{19,3},{4,20},{20... | collective-permute-start | bytes 2359304 | tf_op jit(solution)/shard_map/ppermute | solution.py:478
  54.3 1.2 %copy-start.2 = (bf16[1536,256]{1,0:T(8,128)(2,1)S(1)}, bf16[1536,256]{1,0:T(8,128)(2,1)}, u32[]{:S(2)}) copy-start(bf16[1536,256]{1,0:T(8,128)(2,1)} %get-tuple-element.22) | copy-start | bytes 2359300
  55.5 3.1 %copy-start.1 = (bf16[1552,256]{1,0:T(8,128)(2,1)S(1)}, bf16[1552,256]{1,0:T(8,128)(2,1)}, u32[]{:S(2)}) copy-start(bf16[1552,256]{1,0:T(8,128)(2,1)} %get-tuple-element.20) | copy-start | bytes 2383876
  55.8 8.6 %collective-permute-start.18 = (bf16[768,256]{1,0:T(8,128)(2,1)S(1)}, bf16[768,256]{1,0:T(8,128)(2,1)S(1)}, u32[]{:S(2)}, u32[]{:S(2)}) collective-permute-start(bf16[768,256]{1,0:T(8,128)(2,1)S(1)} %constant_dynamic-slice_fusion.3), channel_id=1, source_target_pairs={{0,1},{1,0},{2,3},{3,2},{4,5},{5,4},{6,7},{7,6},{8,9},{9,8},{10,11... | collective-permute-start | bytes 1179656 | tf_op jit(solution)/shard_map/ppermute | solution.py:483
  59.0 9.7 %collective-permute-start.9 = (bf16[784,256]{1,0:T(8,128)(2,1)S(1)}, bf16[784,256]{1,0:T(8,128)(2,1)S(1)}, u32[]{:S(2)}, u32[]{:S(2)}) collective-permute-start(bf16[784,256]{1,0:T(8,128)(2,1)S(1)} %pad_maximum_fusion), channel_id=1, source_target_pairs={{0,1},{1,0},{2,3},{3,2},{4,5},{5,4},{6,7},{7,6},{8,9},{9,8},{10,11... | collective-permute-start | bytes 1204232 | tf_op jit(solution)/shard_map/ppermute | solution.py:483
  64.5 6.6 %collective-permute-start.19 = (bf16[384,256]{1,0:T(8,128)(2,1)S(1)}, bf16[384,256]{1,0:T(8,128)(2,1)S(1)}, u32[]{:S(2)}, u32[]{:S(2)}) collective-permute-start(bf16[384,256]{1,0:T(8,128)(2,1)S(1)} %constant_dynamic-slice_fusion.2), channel_id=1, source_target_pairs={{0,4},{1,5},{2,6},{3,7},{4,0},{5,1},{6,2},{7,3},{8,12},{9,13},{10,... | collective-permute-start | bytes 589832 | tf_op jit(solution)/shard_map/ppermute | solution.py:483
  68.9 5.9 %collective-permute-start.10 = (bf16[400,256]{1,0:T(8,128)(2,1)S(1)}, bf16[400,256]{1,0:T(8,128)(2,1)S(1)}, u32[]{:S(2)}, u32[]{:S(2)}) collective-permute-start(bf16[400,256]{1,0:T(8,128)(2,1)S(1)} %pad_maximum_fusion.4), channel_id=1, source_target_pairs={{0,2},{1,3},{2,0},{3,1},{4,6},{5,7},{6,4},{7,5},{8,10},{9,11},{10,... | collective-permute-start | bytes 614408 | tf_op jit(solution)/shard_map/ppermute | solution.py:483
  71.2 5.8 %collective-permute-start.20 = (bf16[192,256]{1,0:T(8,128)(2,1)S(1)}, bf16[192,256]{1,0:T(8,128)(2,1)S(1)}, u32[]{:S(2)}, u32[]{:S(2)}) collective-permute-start(bf16[192,256]{1,0:T(8,128)(2,1)S(1)} %constant_dynamic-slice_fusion.1), channel_id=1, source_target_pairs={{0,2},{1,3},{2,0},{3,1},{4,6},{5,7},{6,4},{7,5},{8,10},{9,11},{10,... | collective-permute-start | bytes 294920 | tf_op jit(solution)/shard_map/ppermute | solution.py:483
  74.9 5.3 %collective-permute-start.11 = (bf16[208,256]{1,0:T(8,128)(2,1)S(1)}, bf16[208,256]{1,0:T(8,128)(2,1)S(1)}, u32[]{:S(2)}, u32[]{:S(2)}) collective-permute-start(bf16[208,256]{1,0:T(8,128)(2,1)S(1)} %pad_maximum_fusion.8), channel_id=1, source_target_pairs={{0,4},{1,5},{2,6},{3,7},{4,0},{5,1},{6,2},{7,3},{8,12},{9,13},{10,... | collective-permute-start | bytes 319496 | tf_op jit(solution)/shard_map/ppermute | solution.py:483
  77.1 6.5 %collective-permute-start.21 = (bf16[96,256]{1,0:T(8,128)(2,1)S(1)}, bf16[96,256]{1,0:T(8,128)(2,1)S(1)}, u32[]{:S(2)}, u32[]{:S(2)}) collective-permute-start(bf16[96,256]{1,0:T(8,128)(2,1)S(1)} %constant_dynamic-slice_fusion), channel_id=1, source_target_pairs={{0,8},{1,9},{2,10},{3,11},{4,12},{5,13},{6,14},{7,15},{8,0},{9,1},... | collective-permute-start | bytes 147464 | tf_op jit(solution)/shard_map/ppermute | solution.py:483
  80.3 5.4 %collective-permute-start.12 = (bf16[112,256]{1,0:T(8,128)(2,1)S(1)}, bf16[112,256]{1,0:T(8,128)(2,1)S(1)}, u32[]{:S(2)}, u32[]{:S(2)}) collective-permute-start(bf16[112,256]{1,0:T(8,128)(2,1)S(1)} %pad_maximum_fusion.12), channel_id=1, source_target_pairs={{0,8},{1,9},{2,10},{3,11},{4,12},{5,13},{6,14},{7,15},{8,0},{9,1},... | collective-permute-start | bytes 172040 | tf_op jit(solution)/shard_map/ppermute | solution.py:483
  83.6 5.6 %collective-permute-start.22 = (bf16[96,256]{1,0:T(8,128)(2,1)S(1)}, bf16[96,256]{1,0:T(8,128)(2,1)S(1)}, u32[]{:S(2)}, u32[]{:S(2)}) collective-permute-start(bf16[96,256]{1,0:T(8,128)(2,1)S(1)} %add_convert_fusion.9), channel_id=1, source_target_pairs={{0,8},{1,9},{2,10},{3,11},{4,12},{5,13},{6,14},{7,15},{8,0},{9,1},... | collective-permute-start | bytes 147464 | tf_op jit(solution)/shard_map/ppermute | solution.py:483
  85.7 5.2 %collective-permute-start.13 = (bf16[96,256]{1,0:T(8,128)(2,1)S(1)}, bf16[96,256]{1,0:T(8,128)(2,1)S(1)}, u32[]{:S(2)}, u32[]{:S(2)}) collective-permute-start(bf16[96,256]{1,0:T(8,128)(2,1)S(1)} %slice.75), channel_id=1, source_target_pairs={{0,8},{1,9},{2,10},{3,11},{4,12},{5,13},{6,14},{7,15},{8,0},{9,1},... | collective-permute-start | bytes 147464 | tf_op jit(solution)/shard_map/ppermute | solution.py:483
  89.2 4.7 %collective-permute-start.23 = (bf16[192,256]{1,0:T(8,128)(2,1)S(1)}, bf16[192,256]{1,0:T(8,128)(2,1)S(1)}, u32[]{:S(2)}, u32[]{:S(2)}) collective-permute-start(bf16[192,256]{1,0:T(8,128)(2,1)S(1)} %pad_maximum_fusion.11), channel_id=1, source_target_pairs={{0,2},{1,3},{2,0},{3,1},{4,6},{5,7},{6,4},{7,5},{8,10},{9,11},{10,... | collective-permute-start | bytes 294920 | tf_op jit(solution)/shard_map/ppermute | solution.py:483
  90.9 4.7 %collective-permute-start.14 = (bf16[192,256]{1,0:T(8,128)(2,1)S(1)}, bf16[192,256]{1,0:T(8,128)(2,1)S(1)}, u32[]{:S(2)}, u32[]{:S(2)}) collective-permute-start(bf16[192,256]{1,0:T(8,128)(2,1)S(1)} %pad_maximum_fusion.10), channel_id=1, source_target_pairs={{0,4},{1,5},{2,6},{3,7},{4,0},{5,1},{6,2},{7,3},{8,12},{9,13},{10,... | collective-permute-start | bytes 294920 | tf_op jit(solution)/shard_map/ppermute | solution.py:483
  93.9 5.7 %collective-permute-start.24 = (bf16[384,256]{1,0:T(8,128)(2,1)S(1)}, bf16[384,256]{1,0:T(8,128)(2,1)S(1)}, u32[]{:S(2)}, u32[]{:S(2)}) collective-permute-start(bf16[384,256]{1,0:T(8,128)(2,1)S(1)} %pad_maximum_fusion.7), channel_id=1, source_target_pairs={{0,4},{1,5},{2,6},{3,7},{4,0},{5,1},{6,2},{7,3},{8,12},{9,13},{10,... | collective-permute-start | bytes 589832 | tf_op jit(solution)/shard_map/ppermute | solution.py:483
  95.6 7.9 %collective-permute-start.15 = (bf16[384,256]{1,0:T(8,128)(2,1)S(1)}, bf16[384,256]{1,0:T(8,128)(2,1)S(1)}, u32[]{:S(2)}, u32[]{:S(2)}) collective-permute-start(bf16[384,256]{1,0:T(8,128)(2,1)S(1)} %pad_maximum_fusion.6), channel_id=1, source_target_pairs={{0,2},{1,3},{2,0},{3,1},{4,6},{5,7},{6,4},{7,5},{8,10},{9,11},{10,... | collective-permute-start | bytes 589832 | tf_op jit(solution)/shard_map/ppermute | solution.py:483
  99.8 7.8 %collective-permute-start.25 = (bf16[768,256]{1,0:T(8,128)(2,1)S(1)}, bf16[768,256]{1,0:T(8,128)(2,1)S(1)}, u32[]{:S(2)}, u32[]{:S(2)}) collective-permute-start(bf16[768,256]{1,0:T(8,128)(2,1)S(1)} %pad_maximum_fusion.3), channel_id=1, source_target_pairs={{0,1},{1,0},{2,3},{3,2},{4,5},{5,4},{6,7},{7,6},{8,9},{9,8},{10,11... | collective-permute-start | bytes 1179656 | tf_op jit(solution)/shard_map/ppermute | solution.py:483
  103.6 8.2 %collective-permute-start.16 = (bf16[768,256]{1,0:T(8,128)(2,1)S(1)}, bf16[768,256]{1,0:T(8,128)(2,1)S(1)}, u32[]{:S(2)}, u32[]{:S(2)}) collective-permute-start(bf16[768,256]{1,0:T(8,128)(2,1)S(1)} %pad_maximum_fusion.2), channel_id=1, source_target_pairs={{0,1},{1,0},{2,3},{3,2},{4,5},{5,4},{6,7},{7,6},{8,9},{9,8},{10,11... | collective-permute-start | bytes 1179656 | tf_op jit(solution)/shard_map/ppermute | solution.py:483
  (5 other events, 4.0 us)

commit v4 on v3

--- a/solution.py
+++ b/solution.py
@@ -12,8 +12,9 @@
 EPS = 1e-05
 BIG = -(2.0**100)
 BLOCKS = ((0, 112, 0, 128), (112, 240, 0, 256), (240, 304, 64, 320), (304, 352, 96, 352))
-ERF = (7.97852379e-01, 3.64383569e-02, -1.13746830e-04, -3.20493527e-05, 1.18025665e-06)
+ODDS = (-2.296875, -0.10888671875, 0.00135040283203125, -1.1146068572998047e-05)
 TWO = 2
+HALF = 1536
 F32 = jnp.float32
 BF = jnp.bfloat16
 
@@ -51,12 +52,13 @@
 
 
 def gelu_pair(u):
+    low = lambda value: jnp.array(value, BF)
+    u = u.astype(BF)
     u2 = u * u
-    p = jnp.full_like(u, ERF[-1])
-    for c in ERF[-2::-1]:
-        p = p * u2 + c
-    cdf = 0.5 + 0.5 * jnp.tanh(u * p)
-    pdf = jnp.exp2(u2 * -0.7213475204444817 - 1.3257480647361593)
+    x = jnp.minimum(u2, low(25.0))
+    p = ((x * low(ODDS[3]) + low(ODDS[2])) * x + low(ODDS[1])) * x + low(ODDS[0])
+    cdf = pl.reciprocal(low(1.0) + jnp.exp2(u * p), approx=True)
+    pdf = jnp.exp2(u2 * low(-0.7213475204444817) - low(1.3257480647361593))
     return u * cdf, cdf + u * pdf
 
 
@@ -102,10 +104,10 @@
 
 
 def kernel(
-    sec_ref, seg_ref, attn_mine, mlp_mine, attn_other, mlp_other, x_hbm, cot_hbm,
+    sec_ref, x_ref, cot_ref, eq_ref, ek_ref, gains_mine, gains_other,
     wqkv_mine, wout_mine, wup_mine, wdown_mine, wqkv_other, wout_other, wup_other, wdown_other,
-    yk_ref, ys_ref, dk_out_ref, ds_out_ref, pk_ref, qk_ref, psend_ref, qsend_ref,
-    wqkv_ref, wout_ref, wup_ref, wdown_ref, wsem, insem, xin_ref, cin_ref, wide_ref, xrow_ref, crow_ref, seg_pad_ref, gains_ref, eq_ref, ek_ref, ybuf_ref, dbuf_ref,
+    yk_ref, ys_ref, dk_out_ref, ds_out_ref, pkeep_hbm, qkeep_hbm, psend_hbm, qsend_hbm,
+    wqkv_ref, wout_ref, wup_ref, wdown_ref, wsem, outsem, grads_ref, gains_ref, ybuf_ref, dbuf_ref,
     res_ref, xhat1_ref, rstd1_ref, xhat2_ref, rstd2_ref, a_ref, b_ref, o_ref, qs_ref, k_ref, v_ref,
     p_ref, m_ref, gp_ref, gb_ref, du_ref, dh_ref, dhb_ref, do_ref, prod_ref, dqkv_ref, dk_ref, dv_ref,
     left_ref, aqkv_ref, aout_ref, aup_ref, adown_ref, again_ref,
@@ -114,22 +116,7 @@
     last = pl.num_programs(0) - 1
     sec = sec_ref[0]
     first = sec == 0
-    length = x_hbm.shape[0]
-    loads = [
-        pltpu.make_async_copy(x_hbm, xin_ref, insem.at[0]),
-        pltpu.make_async_copy(cot_hbm, cin_ref, insem.at[1]),
-    ]
-
-    def spread(tokens_ref, rows_ref):
-        count = tokens_ref.shape[1]
-        for p in range(2):
-            wide_ref[p] = tokens_ref[:, :, 128 * p : 128 * p + 128].astype(F32).reshape(length * count, 128)
-        for r in range(count // 2):
-            rows_ref[r, LP - 16 : LP, :] = jnp.zeros((16, D), BF)
-            for p in range(2):
-                row = wide_ref[p, pl.ds(sec * (count // 2) + r, length, stride=count), :]
-                rows_ref[r, 0:length, 128 * p : 128 * p + 128] = row.astype(BF)
-
+    length = yk_ref.shape[1]
 
     copies = []
     for mine, other, held in (
@@ -141,41 +128,21 @@
 
     @pl.when(step == 0)
     def _():
-        loads[0].start()
         for copy in copies:
             copy.start()
-        loads[1].start()
-        for n, (mine, other) in enumerate(((attn_mine, attn_other), (mlp_mine, mlp_other))):
-            mine, other = mine[...].astype(F32), other[...].astype(F32)
-            gains_ref[0, n : n + 1, :] = jnp.where(first, mine, other)
-            gains_ref[1, n : n + 1, :] = jnp.where(first, other, mine)
-        seg_pad_ref[...] = jnp.full(seg_pad_ref.shape, -1, jnp.int32)
-        seg_pad_ref[:, 0:length] = seg_ref[...]
+        mine, other = gains_mine[...].astype(F32), gains_other[...].astype(F32)
+        gains_ref[0] = jnp.where(first, mine, other)
+        gains_ref[1] = jnp.where(first, other, mine)
         for ref in (qs_ref, do_ref, aqkv_ref, aout_ref, aup_ref, adown_ref, again_ref):
             ref[...] = jnp.zeros_like(ref)
-        loads[0].wait()
-        spread(xin_ref, xrow_ref)
         for copy in copies[:4]:
             copy.wait()
 
     def load(r):
         def tokens(lo, hi):
-            res_ref[r, lo:hi, :] = xrow_ref[TWO * step + r, lo:hi, :].astype(F32)
-
-        def visibility():
-            row = sec * (seg_ref.shape[0] // 2) + TWO * step + r
-            seg = jnp.broadcast_to(seg_pad_ref[pl.ds(row, 1), :], (128, seg_pad_ref.shape[1])).astype(F32).T[:LP]
-            lane = lax.broadcasted_iota(jnp.int32, (LP, 128), 1)
-            token = lax.broadcasted_iota(jnp.int32, (LP, 128), 0)
-            same = seg == (lane - 64).astype(F32)
-            start = FRAME * lane
-            here = jnp.logical_and(token >= start, token < start + FRAME)
-            later = token >= start + FRAME
-            other = jnp.logical_and(jnp.logical_not(same), lane < 68)
-            eq_ref[r] = jnp.where(lane < 64, jnp.where(here, 1.0, 0.0), jnp.where(same, 1.0, 0.0)).astype(BF)
-            ek_ref[r] = jnp.where(lane < 64, jnp.where(later, BIG, 0.0), jnp.where(other, BIG, 0.0)).astype(BF)
-
-        return [lambda lo=lo, hi=hi: tokens(lo, hi) for lo, hi in PARTS] + [visibility]
+            res_ref[r, lo:hi, :] = x_ref[r, lo:hi, :].astype(F32)
+
+        return [lambda lo=lo, hi=hi: tokens(lo, hi) for lo, hi in PARTS]
 
     ones = jnp.ones((LP, 128), BF)
 
@@ -398,14 +365,12 @@
     def _():
         for copy in copies[4:]:
             copy.wait()
-        loads[1].wait()
-        spread(cin_ref, crow_ref)
 
     merged(mlp_forward(0, 0), mlp_forward(1, 0))
     merged(attn_forward(0, 1), attn_forward(1, 1))
     merged(mlp_forward(0, 1), mlp_forward(1, 1))
     for r in range(TWO):
-        gb_ref[1, LP * r : LP * r + LP, :] = crow_ref[TWO * step + r]
+        gb_ref[1, LP * r : LP * r + LP, :] = cot_ref[r]
     merged(mlp_backward(0, 1), mlp_backward(1, 1))
     merged(mlp_weights(1))
     merged(attn_backward(0, 1), attn_backward(1, 1))
@@ -417,24 +382,85 @@
 
     @pl.when(step == last)
     def _():
-        for l, p_out, q_out in ((sec, pk_ref, qk_ref), (1 - sec, psend_ref, qsend_ref)):
+        copies = []
+
+        def hand(n, lo, rows, out):
+            copies.append(pltpu.make_async_copy(grads_ref.at[n, pl.ds(lo, rows)], out, outsem.at[len(copies)]))
+            copies[-1].start()
+
+        for n, l, p_out, q_out in ((0, 1 - sec, psend_hbm, qsend_hbm), (1, sec, pkeep_hbm, qkeep_hbm)):
             for j in range(3):
-                p_out[256 * j : 256 * j + 256, :] = aqkv_ref[l, :, 256 * j : 256 * j + 256].astype(BF)
-            p_out[768:1024, :] = aout_ref[l].astype(BF)
+                grads_ref[n, 256 * j : 256 * j + 256, :] = aqkv_ref[l, :, 256 * j : 256 * j + 256].astype(BF)
+            grads_ref[n, 768:1024, :] = aout_ref[l].astype(BF)
             for j in range(2):
-                p_out[1024 + 256 * j : 1280 + 256 * j, :] = aup_ref[l, :, 256 * j : 256 * j + 256].astype(BF)
-                q_out[256 * j : 256 * j + 256, :] = aup_ref[l, :, 512 + 256 * j : 768 + 256 * j].astype(BF)
-            for j in range(4):
-                q_out[512 + 256 * j : 768 + 256 * j, :] = adown_ref[l, :, 256 * j : 256 * j + 256].astype(BF).T
+                grads_ref[n, 1024 + 256 * j : 1280 + 256 * j, :] = aup_ref[l, :, 256 * j : 256 * j + 256].astype(BF)
             row = lax.broadcasted_iota(jnp.int32, (16, D), 0)
             attn = jnp.sum(again_ref[l, 0], axis=0, keepdims=True)
             mlp = jnp.sum(again_ref[l, 1], axis=0, keepdims=True)
-            p_out[1536:1552, :] = jnp.where(row == 0, attn, jnp.where(row == 1, mlp, 0.0)).astype(BF)
-
-
-def local_step(section, x, cot, segments, gains, other_gains, mine, other):
+            grads_ref[n, HALF : HALF + 16, :] = jnp.where(row == 0, attn, jnp.where(row == 1, mlp, 0.0)).astype(BF)
+            hand(n, 0, HALF + 16, p_out)
+            for j in range(2):
+                grads_ref[n, 1552 + 256 * j : 1808 + 256 * j, :] = aup_ref[l, :, 512 + 256 * j : 768 + 256 * j].astype(BF)
+            for j in range(4):
+                grads_ref[n, 2064 + 256 * j : 2320 + 256 * j, :] = adown_ref[l, :, 256 * j : 256 * j + 256].astype(BF).T
+            hand(n, HALF + 16, HALF, q_out)
+        for copy in copies:
+            copy.wait()
+
+
+def spread(sec_ref, seg_ref, x_hbm, cot_hbm, x_out, cot_out, eq_ref, ek_ref, x_ref, cot_ref, wide_ref, seg_pad_ref, sem):
+    length, count, _ = x_ref.shape
+    begin = sec_ref[0] * (count // 2)
+    copies = [pltpu.make_async_copy(x_hbm, x_ref, sem.at[0]), pltpu.make_async_copy(cot_hbm, cot_ref, sem.at[1])]
+    for copy in copies:
+        copy.start()
+    seg_pad_ref[...] = jnp.full(seg_pad_ref.shape, -1, jnp.int32)
+    seg_pad_ref[:, 0:length] = seg_ref[...]
+    lane = lax.broadcasted_iota(jnp.int32, (LP, 128), 1)
+    token = lax.broadcasted_iota(jnp.int32, (LP, 128), 0)
+    here = jnp.logical_and(token >= FRAME * lane, token < FRAME * lane + FRAME)
+    later = token >= FRAME * lane + FRAME
+    for r in range(count // 2):
+        seg = jnp.broadcast_to(seg_pad_ref[pl.ds(begin + r, 1), :], (128, seg_pad_ref.shape[1])).astype(F32).T[:LP]
+        same = seg == (lane - 64).astype(F32)
+        other = jnp.logical_and(jnp.logical_not(same), lane < 68)
+        eq_ref[r] = jnp.where(lane < 64, jnp.where(here, 1.0, 0.0), jnp.where(same, 1.0, 0.0)).astype(BF)
+        ek_ref[r] = jnp.where(lane < 64, jnp.where(later, BIG, 0.0), jnp.where(other, BIG, 0.0)).astype(BF)
+    for copy, taken, out in ((copies[0], x_ref, x_out), (copies[1], cot_ref, cot_out)):
+        copy.wait()
+        for p in range(2):
+            wide_ref[p] = taken[:, :, 128 * p : 128 * p + 128].astype(F32).reshape(length * count, 128)
+        for r in range(count // 2):
+            out[r, LP - 16 : LP, :] = jnp.zeros((16, D), BF)
+            for p in range(2):
+                row = wide_ref[p, pl.ds(begin + r, length, stride=count), :]
+                out[r, 0:length, 128 * p : 128 * p + 128] = row.astype(BF)
+
+
+def prepare(section, x, cot, segments):
     length, rows, _ = x.shape
-    steps = rows // 2 // TWO
+    hbm = pl.BlockSpec(memory_space=pl.ANY)
+    vmem = pl.BlockSpec(memory_space=pltpu.VMEM)
+    vm = pltpu.VMEM
+    tokens = jax.ShapeDtypeStruct((rows // 2, LP, D), BF)
+    columns = jax.ShapeDtypeStruct((rows // 2, LP, 128), BF)
+    return pl.pallas_call(
+        spread,
+        in_specs=[pl.BlockSpec(memory_space=pltpu.SMEM), vmem, hbm, hbm],
+        out_specs=[vmem] * 4,
+        out_shape=[tokens, tokens, columns, columns],
+        scratch_shapes=[
+            vm(x.shape, BF), vm(x.shape, BF), vm((2, length * rows, 128), F32), vm((rows, 384), jnp.int32),
+            pltpu.SemaphoreType.DMA((2,)),
+        ],
+        compiler_params=pltpu.CompilerParams(vmem_limit_bytes=60 * 1024 * 1024),
+    )(section, segments, x, cot)
+
+
+def local_step(section, rows_in, length, gains, other_gains, mine, other):
+    count = rows_in[0].shape[0]
+    steps = count // TWO
+    tok = lambda w: pl.BlockSpec((TWO, LP, w), lambda i, sec: (i, 0, 0))
     row_out = pl.BlockSpec((TWO, length, D), lambda i, sec: (i, 0, 0))
     whole = lambda shape: pl.BlockSpec(shape, lambda i, sec: (0,) * len(shape), pipeline_mode=pl.Buffered(1))
     hbm = pl.BlockSpec(memory_space=pl.ANY)
@@ -446,12 +472,11 @@
         grid_spec=pltpu.PrefetchScalarGridSpec(
             num_scalar_prefetch=1,
             grid=(steps,),
-            in_specs=[whole(segments.shape)] + [whole((1, D))] * 4 + [hbm] * 10,
-            out_specs=[row_out, row_out, row_out, row_out, whole((1552, D)), whole((1536, D)), whole((1552, D)), whole((1536, D))],
+            in_specs=[tok(D), tok(D), tok(128), tok(128)] + [whole((2, D))] * 2 + [hbm] * 8,
+            out_specs=[row_out, row_out, row_out, row_out, hbm, hbm, hbm, hbm],
             scratch_shapes=[
-                vm((2, D, 3 * D), BF), vm((2, D, D), BF), vm((2, D, FF), BF), vm((2, FF, D), BF), pltpu.SemaphoreType.DMA((8,)), pltpu.SemaphoreType.DMA((2,)), vm(x.shape, BF), vm(x.shape, BF),
-                vm((2, length * rows, 128), F32), vm((rows // 2, LP, D), BF), vm((rows // 2, LP, D), BF), vm((rows, 384), jnp.int32),
-                vm((2, 2, D), F32), vm((TWO, LP, 128), BF), vm((TWO, LP, 128), BF), vm((TWO, LP, D), BF), vm((TWO, LP, D), F32),
+                vm((2, D, 3 * D), BF), vm((2, D, D), BF), vm((2, D, FF), BF), vm((2, FF, D), BF), pltpu.SemaphoreType.DMA((8,)), pltpu.SemaphoreType.DMA((4,)), vm((2, 3088, D), BF),
+                vm((2, 2, D), F32), vm((TWO, LP, D), BF), vm((TWO, LP, D), F32),
                 vm((TWO, LP, D), F32),
                 vm((2, TWO, LP, D), F32), vm((2, TWO, LP, 128), F32), vm((2, TWO, LP, D), F32), vm((2, TWO, LP, 128), F32),
                 flat(D), flat(D), flat(D),
@@ -464,14 +489,14 @@
             ],
         ),
         out_shape=[
-            shape((rows // 2, length, D), BF), shape((rows // 2, length, D), BF),
-            shape((rows // 2, length, D), F32), shape((rows // 2, length, D), BF),
-            shape((1552, D), BF), shape((1536, D), BF), shape((1552, D), BF), shape((1536, D), BF),
+            shape((count, length, D), BF), shape((count, length, D), BF),
+            shape((count, length, D), F32), shape((count, length, D), BF),
+            shape((HALF + 16, D), BF), shape((HALF, D), BF), shape((HALF + 16, D), BF), shape((HALF, D), BF),
         ],
         compiler_params=pltpu.CompilerParams(
             dimension_semantics=("arbitrary",), vmem_limit_bytes=60 * 1024 * 1024
         ),
-    )(section, segments, *gains, *other_gains, x, cot, *mine, *other)
+    )(section, *rows_in, gains, other_gains, *mine, *other)
 
 
 def partner(value):
@@ -487,7 +512,11 @@
     return (a.astype(F32) + b.astype(F32)).astype(BF)
 
 
-def sum_over_dp(parts, tail, section):
+def after(values, event):
+    return lax.optimization_barrier((values, event))[0]
+
+
+def sum_over_dp(parts, tail, section, follow):
     count = lax.axis_size("dp")
     place = lax.axis_index("dp")
     depth = count.bit_length() - 1
@@ -499,6 +528,7 @@
     sizes = [tail, 0]
     current = list(parts)
     uppers = [[], []]
+    sent = []
     for stage in range(depth):
         got = []
         for part in range(2):
@@ -511,6 +541,10 @@
             if sizes[part]:
                 send = jnp.concatenate([send, value[main:]], axis=0)
             got.append(cross(send, count, bits))
+            if stage == 0:
+                sent.append(send)
+        if stage == 0:
+            followed = follow(sent)
         for part in range(2):
             value = current[part]
             main = value.shape[0] - sizes[part]
@@ -530,20 +564,21 @@
                 halves.append(pair)
             else:
                 current[part] = jnp.concatenate(pair, axis=0)
-    return halves, rest
+    return halves, rest, followed
 
 
 def shards(
     layer_input, out_cotangent, segment_ids, gain_attn, weight_qkv, weight_out, gain_mlp, weight_up, weight_down
 ):
     section = lax.axis_index("section")
-    gains = (gain_attn, gain_mlp)
+    here = section[None].astype(jnp.int32)
+    rows_in = prepare(here, layer_input.swapaxes(0, 1), out_cotangent.swapaxes(0, 1), segment_ids)
     mine = (weight_qkv, weight_out, weight_up, weight_down)
     other = tuple(partner(w) for w in mine)
-    other_gains = tuple(partner(g) for g in gains)
+    gains = jnp.concatenate([gain_attn, gain_mlp], axis=0)
+    other_gains = partner(gains)
     acts, acts_send, grads, grads_send, first, second, first_send, second_send = local_step(
-        section[None].astype(jnp.int32), layer_input.swapaxes(0, 1), out_cotangent.swapaxes(0, 1), segment_ids,
-        gains, other_gains, mine, other,
+        here, rows_in, layer_input.shape[1], gains, other_gains, mine, other,
     )
     got = partner(first_send), partner(second_send)
     parts = add(first, got[0]), add(second, got[1])
@@ -552,9 +587,13 @@
     def whole_rows(keep, got):
         return jnp.concatenate([jnp.where(low, keep, got), jnp.where(low, got, keep)], axis=0)
 
-    activations = whole_rows(acts, partner(acts_send))
-    input_grads = whole_rows(grads, partner(grads_send).astype(F32))
-    ((qkv, out_up), (up_down, down)), rest = sum_over_dp(parts, 16, section)
+    def rows_out(sent):
+        sends = (acts_send, grads_send)
+        got = partner(sends[0]), partner(sends[1])
+        got = after(got, sent[1])
+        return whole_rows(acts, got[0]), whole_rows(grads, got[1].astype(F32))
+
+    ((qkv, out_up), (up_down, down)), rest, (activations, input_grads) = sum_over_dp(parts, 16, section, rows_out)
     side = lambda *blocks: jnp.concatenate(blocks, axis=1).astype(F32)
     return (
         activations[None],

time: 115 us -> 112 us (0.974)
  starting transfers between devices: 33.1 us -> 27.6 us
  local copies, waits for them, and re-layouts: 6.86 us -> 9.6 us
  waiting for transfers between devices: 25.8 us -> 23.4 us
  Pallas kernels: 41.4 us -> 42.6 us
    ppermute x10 -> x9, waiting for transfers between devices: 6.93 us -> 0.02 us  [partner(): return lax.ppermute(value, 'section', [(0, 1), (1, 0)])]
    ppermute x16, starting transfers between devices: 30 us -> 24.9 us  [cross(): return lax.ppermute(value, ('section', 'dp'), pairs)]
    ppermute x16, waiting for transfers between devices: 18.9 us -> 23.4 us  [cross(): return lax.ppermute(value, ('section', 'dp'), pairs)]
    pallas_call x0 -> x1, Pallas kernels: none -> 4.12 us  [prepare(): pl.pallas_call(spread, in_specs=[pl.BlockSpec(memory_space=pltpu.SMEM), v...]
    pallas_call x1, Pallas kernels: 41.4 us -> 38.4 us  [local_step(): pl.pallas_call(kernel, grid_spec=pltpu.PrefetchScalarGridSpec(num_scalar_...]
    pallas_call x2, local copies, waits for them, and re-layouts: 1.75 us -> 3.45 us  [local_step(): pl.pallas_call(kernel, grid_spec=pltpu.PrefetchScalarGridSpec(num_scalar_...]
    ppermute x10 -> x9, starting transfers between devices: 3.06 us -> 2.69 us  [partner(): return lax.ppermute(value, 'section', [(0, 1), (1, 0)])]
  transfers between devices with their start and end apart: 26 -> 25, of which waited for: 19 -> 14; matrix products, arithmetic and copies ran while one was open for 7% -> 11% of each run, Pallas kernels for 0% -> 4%
where the time goes in v4:
time: 112 us
  Pallas kernels  42.6 us (38%)
  starting transfers between devices  27.6 us (25%)
  waiting for transfers between devices  23.4 us (21%)
  local copies, waits for them, and re-layouts  9.6 us (9%)
  other arithmetic  7.4 us (7%)
    pallas_call x1, Pallas kernels, local_step(): pl.pallas_call(kernel, grid_spec=pltpu.PrefetchScalarGridSpec(num_scalar_...  38.4 us
    ppermute x16, starting transfers between devices, cross(): return lax.ppermute(value, ('section', 'dp'), pairs)  24.9 us
    ppermute x16, waiting for transfers between devices, cross(): return lax.ppermute(value, ('section', 'dp'), pairs)  23.4 us
    unnamed x24, local copies, waits for them, and re-layouts  5.88 us
    pallas_call x1, Pallas kernels, prepare(): pl.pallas_call(spread, in_specs=[pl.BlockSpec(memory_space=pltpu.SMEM), v...  4.12 us
    pallas_call x2, local copies, waits for them, and re-layouts, local_step(): pl.pallas_call(kernel, grid_spec=pltpu.PrefetchScalarGridSpec(num_scalar_...  3.45 us
    ppermute x9, starting transfers between devices, partner(): return lax.ppermute(value, 'section', [(0, 1), (1, 0)])  2.69 us
  transfers between devices with their start and end apart: 25, of which 14 were waited for; matrix products, arithmetic and copies ran while one was open for 11% of the time, Pallas kernels for 4%

profile of v4, /device:TPU:0, one launch (start us, length us, event | category | flops | bytes accessed | tf_op | source)
XLA Modules:
  0.0 111.7 jit_solution(2487956695146176102)
XLA Ops:
  2.9 4.1 %shard_map.152 = (bf16[4,352,256]{2,1,0:T(8,128)(2,1)}, bf16[4,352,256]{2,1,0:T(8,128)(2,1)}, bf16[4,352,128]{2,1,0:T(8,128)(2,1)}, bf16[4,352,128]{2,1,0:T(8,128)(2,1)}) custom-call(s32[1]{0:T(128)} %bitcast.sec_ref, s32[8,340]{1,0:T(8,128)} %seg_ref.1, bf16[340,8,256]{2,1,0:T(8,128)(2,1)} %bitcast.30, bf16[340,8,256]{2,1,0:T(8,128)(2,1)} %bitcast.31), custom_call_target="tpu_custom_call" | custom-call | tf_op jit(solution)/shard_map/pallas_call | solution.py:447
  8.3 38.4 %shard_map.153 = (bf16[4,340,256]{2,1,0:T(8,128)(2,1)}, bf16[4,340,256]{2,1,0:T(8,128)(2,1)}, f32[4,340,256]{2,1,0:T(8,128)}, bf16[4,340,256]{2,1,0:T(8,128)(2,1...) custom-call(s32[1]{0:T(128)} %bitcast.sec_ref, ...), custom_call_target="tpu_custom_call" | custom-call | tf_op jit(solution)/shard_map/pallas_call | solution.py:470
  46.9 2.3 %copy.19 = bf16[4,340,256]{2,0,1:T(4,128)(2,1)} copy(bf16[4,340,256]{2,1,0:T(8,128)(2,1)} %get-tuple-element.27) | data formatting | bytes 1392640 | tf_op jit(solution)/shard_map/pallas_call | solution.py:470
  49.6 1.1 %copy.20 = bf16[4,340,256]{2,0,1:T(4,128)(2,1)} copy(bf16[4,340,256]{2,1,0:T(8,128)(2,1)S(1)} %copy-done.3) | data formatting | bytes 1392640 | tf_op jit(solution)/shard_map/pallas_call | solution.py:470
  51.5 2.6 %collective-permute-start.17 = (bf16[768,256]{1,0:T(8,128)(2,1)S(1)}, bf16[768,256]{1,0:T(8,128)(2,1)S(1)}, u32[]{:S(2)}, u32[]{:S(2)}) collective-permute-start(bf16[768,256]{1,0:T(8,128)(2,1)S(1)} %constant_dynamic-slice_fusion.11), channel_id=1, source_target_pairs={{0,1},{1,0},{2,3},{3,2},{4,5},{5,4},{6,7},{7,6},{8,9},{9,8},{10,11... | collective-permute-start | bytes 1179656 | tf_op jit(solution)/shard_map/ppermute | solution.py:508
  56.2 1.6 %collective-permute-start.9 = (bf16[784,256]{1,0:T(8,128)(2,1)S(1)}, bf16[784,256]{1,0:T(8,128)(2,1)S(1)}, u32[]{:S(2)}, u32[]{:S(2)}) collective-permute-start(bf16[784,256]{1,0:T(8,128)(2,1)S(1)} %pad_maximum_fusion), channel_id=1, source_target_pairs={{0,1},{1,0},{2,3},{3,2},{4,5},{5,4},{6,7},{7,6},{8,9},{9,8},{10,11... | collective-permute-start | bytes 1204232 | tf_op jit(solution)/shard_map/ppermute | solution.py:508
  58.0 2.4 %copy.25 = f32[1,8,340,256]{3,1,2,0:T(8,128)} copy(f32[1,8,340,256]{3,2,1,0:T(8,128)S(1)} %maximum_bitcast_fusion) | data formatting | bytes 5570560
  60.4 1.4 %copy.24 = bf16[1,8,340,256]{3,1,2,0:T(8,128)(2,1)} copy(bf16[1,8,340,256]{3,2,1,0:T(8,128)(2,1)S(1)} %maximum_bitcast_fusion.1) | data formatting | bytes 2785280
  61.9 1.6 %collective-permute-start.18 = (bf16[384,256]{1,0:T(8,128)(2,1)S(1)}, bf16[384,256]{1,0:T(8,128)(2,1)S(1)}, u32[]{:S(2)}, u32[]{:S(2)}) collective-permute-start(bf16[384,256]{1,0:T(8,128)(2,1)S(1)} %constant_dynamic-slice_fusion.2), channel_id=1, source_target_pairs={{0,4},{1,5},{2,6},{3,7},{4,0},{5,1},{6,2},{7,3},{8,12},{9,13},{10,... | collective-permute-start | bytes 589832 | tf_op jit(solution)/shard_map/ppermute | solution.py:508
  64.4 2.2 %collective-permute-start.10 = (bf16[400,256]{1,0:T(8,128)(2,1)S(1)}, bf16[400,256]{1,0:T(8,128)(2,1)S(1)}, u32[]{:S(2)}, u32[]{:S(2)}) collective-permute-start(bf16[400,256]{1,0:T(8,128)(2,1)S(1)} %pad_maximum_fusion.4), channel_id=1, source_target_pairs={{0,2},{1,3},{2,0},{3,1},{4,6},{5,7},{6,4},{7,5},{8,10},{9,11},{10,... | collective-permute-start | bytes 614408 | tf_op jit(solution)/shard_map/ppermute | solution.py:508
  66.6 2.3 %collective-permute-done.18 = bf16[384,256]{1,0:T(8,128)(2,1)S(1)} collective-permute-done((bf16[384,256]{1,0:T(8,128)(2,1)S(1)}, bf16[384,256]{1,0:T(8,128)(2,1)S(1)}, u32[]{:S(2)}, u32[]{:S(2)}) %collective-permute-start.18) | collective-permute-done | bytes 196640 | tf_op jit(solution)/shard_map/ppermute | solution.py:508
  69.4 0.9 collective-permute-done.10
  70.4 2.1 %collective-permute-start.11 = (bf16[208,256]{1,0:T(8,128)(2,1)S(1)}, bf16[208,256]{1,0:T(8,128)(2,1)S(1)}, u32[]{:S(2)}, u32[]{:S(2)}) collective-permute-start(bf16[208,256]{1,0:T(8,128)(2,1)S(1)} %pad_maximum_fusion.8), channel_id=1, source_target_pairs={{0,4},{1,5},{2,6},{3,7},{4,0},{5,1},{6,2},{7,3},{8,12},{9,13},{10,... | collective-permute-start | bytes 319496 | tf_op jit(solution)/shard_map/ppermute | solution.py:508
  72.6 1.1 collective-permute-done.19
  73.7 2.7 %collective-permute-start.20 = (bf16[96,256]{1,0:T(8,128)(2,1)S(1)}, bf16[96,256]{1,0:T(8,128)(2,1)S(1)}, u32[]{:S(2)}, u32[]{:S(2)}) collective-permute-start(bf16[96,256]{1,0:T(8,128)(2,1)S(1)} %constant_dynamic-slice_fusion), channel_id=1, source_target_pairs={{0,8},{1,9},{2,10},{3,11},{4,12},{5,13},{6,14},{7,15},{8,0},{9,1},... | collective-permute-start | bytes 147464 | tf_op jit(solution)/shard_map/ppermute | solution.py:508
  76.5 2.5 %collective-permute-start.12 = (bf16[112,256]{1,0:T(8,128)(2,1)S(1)}, bf16[112,256]{1,0:T(8,128)(2,1)S(1)}, u32[]{:S(2)}, u32[]{:S(2)}) collective-permute-start(bf16[112,256]{1,0:T(8,128)(2,1)S(1)} %pad_maximum_fusion.12), channel_id=1, source_target_pairs={{0,8},{1,9},{2,10},{3,11},{4,12},{5,13},{6,14},{7,15},{8,0},{9,1},... | collective-permute-start | bytes 172040 | tf_op jit(solution)/shard_map/ppermute | solution.py:508
  79.3 2.2 %collective-permute-start.21 = (bf16[96,256]{1,0:T(8,128)(2,1)S(1)}, bf16[96,256]{1,0:T(8,128)(2,1)S(1)}, u32[]{:S(2)}, u32[]{:S(2)}) collective-permute-start(bf16[96,256]{1,0:T(8,128)(2,1)S(1)} %add_convert_fusion.9), channel_id=1, source_target_pairs={{0,8},{1,9},{2,10},{3,11},{4,12},{5,13},{6,14},{7,15},{8,0},{9,1},... | collective-permute-start | bytes 147464 | tf_op jit(solution)/shard_map/ppermute | solution.py:508
  81.5 1.3 %collective-permute-done.12 = bf16[112,256]{1,0:T(8,128)(2,1)S(1)} collective-permute-done((bf16[112,256]{1,0:T(8,128)(2,1)S(1)}, bf16[112,256]{1,0:T(8,128)(2,1)S(1)}, u32[]{:S(2)}, u32[]{:S(2)}) %collective-permute-start.12) | collective-permute-done | bytes 57376 | tf_op jit(solution)/shard_map/ppermute | solution.py:508
  82.8 1.3 %collective-permute-start.13 = (bf16[96,256]{1,0:T(8,128)(2,1)S(1)}, bf16[96,256]{1,0:T(8,128)(2,1)S(1)}, u32[]{:S(2)}, u32[]{:S(2)}) collective-permute-start(bf16[96,256]{1,0:T(8,128)(2,1)S(1)} %slice.75), channel_id=1, source_target_pairs={{0,8},{1,9},{2,10},{3,11},{4,12},{5,13},{6,14},{7,15},{8,0},{9,1},... | collective-permute-start | bytes 147464 | tf_op jit(solution)/shard_map/ppermute | solution.py:508
  84.1 1.6 %collective-permute-done.21 = bf16[96,256]{1,0:T(8,128)(2,1)S(1)} collective-permute-done((bf16[96,256]{1,0:T(8,128)(2,1)S(1)}, bf16[96,256]{1,0:T(8,128)(2,1)S(1)}, u32[]{:S(2)}, u32[]{:S(2)}) %collective-permute-start.21) | collective-permute-done | bytes 49184 | tf_op jit(solution)/shard_map/ppermute | solution.py:508
  85.8 1.3 %collective-permute-start.22 = (bf16[192,256]{1,0:T(8,128)(2,1)S(1)}, bf16[192,256]{1,0:T(8,128)(2,1)S(1)}, u32[]{:S(2)}, u32[]{:S(2)}) collective-permute-start(bf16[192,256]{1,0:T(8,128)(2,1)S(1)} %pad_maximum_fusion.11), channel_id=1, source_target_pairs={{0,2},{1,3},{2,0},{3,1},{4,6},{5,7},{6,4},{7,5},{8,10},{9,11},{10,... | collective-permute-start | bytes 294920 | tf_op jit(solution)/shard_map/ppermute | solution.py:508
  87.9 1.3 %collective-permute-start.14 = (bf16[192,256]{1,0:T(8,128)(2,1)S(1)}, bf16[192,256]{1,0:T(8,128)(2,1)S(1)}, u32[]{:S(2)}, u32[]{:S(2)}) collective-permute-start(bf16[192,256]{1,0:T(8,128)(2,1)S(1)} %pad_maximum_fusion.10), channel_id=1, source_target_pairs={{0,4},{1,5},{2,6},{3,7},{4,0},{5,1},{6,2},{7,3},{8,12},{9,13},{10,... | collective-permute-start | bytes 294920 | tf_op jit(solution)/shard_map/ppermute | solution.py:508
  89.2 1.3 %collective-permute-done.22 = bf16[192,256]{1,0:T(8,128)(2,1)S(1)} collective-permute-done((bf16[192,256]{1,0:T(8,128)(2,1)S(1)}, bf16[192,256]{1,0:T(8,128)(2,1)S(1)}, u32[]{:S(2)}, u32[]{:S(2)}) %collective-permute-start.22) | collective-permute-done | bytes 98336 | tf_op jit(solution)/shard_map/ppermute | solution.py:508
  90.6 1.1 %collective-permute-start.23 = (bf16[384,256]{1,0:T(8,128)(2,1)S(1)}, bf16[384,256]{1,0:T(8,128)(2,1)S(1)}, u32[]{:S(2)}, u32[]{:S(2)}) collective-permute-start(bf16[384,256]{1,0:T(8,128)(2,1)S(1)} %pad_maximum_fusion.7), channel_id=1, source_target_pairs={{0,4},{1,5},{2,6},{3,7},{4,0},{5,1},{6,2},{7,3},{8,12},{9,13},{10,... | collective-permute-start | bytes 589832 | tf_op jit(solution)/shard_map/ppermute | solution.py:508
  91.7 1.1 collective-permute-done.14
  92.9 3.3 %collective-permute-done.23 = bf16[384,256]{1,0:T(8,128)(2,1)S(1)} collective-permute-done((bf16[384,256]{1,0:T(8,128)(2,1)S(1)}, bf16[384,256]{1,0:T(8,128)(2,1)S(1)}, u32[]{:S(2)}, u32[]{:S(2)}) %collective-permute-start.23) | collective-permute-done | bytes 196640 | tf_op jit(solution)/shard_map/ppermute | solution.py:508
  97.8 2.9 %collective-permute-done.15 = bf16[384,256]{1,0:T(8,128)(2,1)S(1)} collective-permute-done((bf16[384,256]{1,0:T(8,128)(2,1)S(1)}, bf16[384,256]{1,0:T(8,128)(2,1)S(1)}, u32[]{:S(2)}, u32[]{:S(2)}) %collective-permute-start.15) | collective-permute-done | bytes 196640 | tf_op jit(solution)/shard_map/ppermute | solution.py:508
  100.9 1.0 collective-permute-start.16
  101.9 2.4 %collective-permute-done.24 = bf16[768,256]{1,0:T(8,128)(2,1)S(1)} collective-permute-done((bf16[768,256]{1,0:T(8,128)(2,1)S(1)}, bf16[768,256]{1,0:T(8,128)(2,1)S(1)}, u32[]{:S(2)}, u32[]{:S(2)}) %collective-permute-start.24) | collective-permute-done | bytes 393248 | tf_op jit(solution)/shard_map/ppermute | solution.py:508
  104.4 1.0 maximum_convert_fusion.1
  105.5 3.3 %collective-permute-done.16 = bf16[768,256]{1,0:T(8,128)(2,1)S(1)} collective-permute-done((bf16[768,256]{1,0:T(8,128)(2,1)S(1)}, bf16[768,256]{1,0:T(8,128)(2,1)S(1)}, u32[]{:S(2)}, u32[]{:S(2)}) %collective-permute-start.16) | collective-permute-done | bytes 393248 | tf_op jit(solution)/shard_map/ppermute | solution.py:508
  110.6 1.1 maximum_convert_fusion
  (98 shorter events, 13.5 us)
Async XLA Ops:
  0.6 6.5 %collective-permute-start.3 = (bf16[1,256,1024]{2,1,0:T(8,128)(2,1)}, bf16[1,256,1024]{2,1,0:T(8,128)(2,1)S(1)}, u32[]{:S(2)}, u32[]{:S(2)}) collective-permute-start(bf16[1,256,1024]{2,1,0:T(8,128)(2,1)} %wup_mine.1), channel_id=1, source_target_pairs={{0,16},{16,0},{1,17},{17,1},{2,18},{18,2},{3,19},{19,3},{4,20},{20... | collective-permute-start | bytes 1572872 | tf_op jit(solution)/shard_map/ppermute | solution.py:503
  1.2 6.0 %collective-permute-start.4 = (bf16[1,1024,256]{2,1,0:T(8,128)(2,1)}, bf16[1,1024,256]{2,1,0:T(8,128)(2,1)S(1)}, u32[]{:S(2)}, u32[]{:S(2)}) collective-permute-start(bf16[1,1024,256]{2,1,0:T(8,128)(2,1)} %wdown_mine.1), channel_id=1, source_target_pairs={{0,16},{16,0},{1,17},{17,1},{2,18},{18,2},{3,19},{19,3},{4,20},{20... | collective-permute-start | bytes 1572872 | tf_op jit(solution)/shard_map/ppermute | solution.py:503
  1.2 5.9 %collective-permute-start.1 = (bf16[1,256,768]{2,1,0:T(8,128)(2,1)}, bf16[1,256,768]{2,1,0:T(8,128)(2,1)S(1)}, u32[]{:S(2)}, u32[]{:S(2)}) collective-permute-start(bf16[1,256,768]{2,1,0:T(8,128)(2,1)} %wqkv_mine.1), channel_id=1, source_target_pairs={{0,16},{16,0},{1,17},{17,1},{2,18},{18,2},{3,19},{19,3},{4,20},{20... | collective-permute-start | bytes 1179656 | tf_op jit(solution)/shard_map/ppermute | solution.py:503
  1.7 5.4 %collective-permute-start.2 = (bf16[1,256,256]{2,1,0:T(8,128)(2,1)}, bf16[1,256,256]{2,1,0:T(8,128)(2,1)S(1)}, u32[]{:S(2)}, u32[]{:S(2)}) collective-permute-start(bf16[1,256,256]{2,1,0:T(8,128)(2,1)} %wout_mine.1), channel_id=1, source_target_pairs={{0,16},{16,0},{1,17},{17,1},{2,18},{18,2},{3,19},{19,3},{4,20},{20... | collective-permute-start | bytes 393224 | tf_op jit(solution)/shard_map/ppermute | solution.py:503
  2.4 4.7 %copy-start.9 = (bf16[2,256]{1,0:T(2,128)(2,1)}, bf16[2,256]{1,0:T(2,128)(2,1)S(1)}, u32[]{:S(2)}) copy-start(bf16[2,256]{1,0:T(2,128)(2,1)S(1)} %pad_maximum_fusion.14.gains_mine) | copy-start | bytes 3076
  2.5 4.6 %collective-permute-start = (bf16[2,256]{1,0:T(2,128)(2,1)S(1)}, bf16[2,256]{1,0:T(2,128)(2,1)S(1)}, u32[]{:S(2)}, u32[]{:S(2)}) collective-permute-start(bf16[2,256]{1,0:T(2,128)(2,1)S(1)} %pad_maximum_fusion.14.gains_mine), channel_id=1, source_target_pairs={{0,16},{16,0},{1,17},{17,1},{2,18},{18,2},{3,19},{19,3},{4,20},{20... | collective-permute-start | bytes 3080 | tf_op jit(solution)/shard_map/ppermute | solution.py:503
  7.2 1.1 copy-start.6
  46.7 2.9 %copy-start.3 = (bf16[4,340,256]{2,1,0:T(8,128)(2,1)S(1)}, bf16[4,340,256]{2,1,0:T(8,128)(2,1)}, u32[]{:S(2)}) copy-start(bf16[4,340,256]{2,1,0:T(8,128)(2,1)} %get-tuple-element.28) | copy-start | bytes 2088964
  46.7 4.5 %collective-permute-start.7 = (bf16[1536,256]{1,0:T(8,128)(2,1)}, bf16[1536,256]{1,0:T(8,128)(2,1)S(1)}, u32[]{:S(2)}, u32[]{:S(2)}) collective-permute-start(bf16[1536,256]{1,0:T(8,128)(2,1)} %get-tuple-element.30), channel_id=1, source_target_pairs={{0,16},{16,0},{1,17},{17,1},{2,18},{18,2},{3,19},{19,3},{4,20},{20... | collective-permute-start | bytes 2359304 | tf_op jit(solution)/shard_map/ppermute | solution.py:503
  46.9 4.4 %copy-start.2 = (bf16[1536,256]{1,0:T(8,128)(2,1)S(1)}, bf16[1536,256]{1,0:T(8,128)(2,1)}, u32[]{:S(2)}) copy-start(bf16[1536,256]{1,0:T(8,128)(2,1)} %get-tuple-element.29) | copy-start | bytes 2359300
  49.2 5.0 %collective-permute-start.5 = (bf16[4,340,256]{2,0,1:T(4,128)(2,1)}, bf16[4,340,256]{2,0,1:T(4,128)(2,1)S(1)}, u32[]{:S(2)}, u32[]{:S(2)}) collective-permute-start(bf16[4,340,256]{2,0,1:T(4,128)(2,1)} %copy.19), channel_id=1, source_target_pairs={{0,16},{16,0},{1,17},{17,1},{2,18},{18,2},{3,19},{19,3},{4,20},{20... | collective-permute-start | bytes 2088968 | tf_op jit(solution)/shard_map/ppermute | solution.py:503
  50.7 3.4 %collective-permute-start.6 = (bf16[4,340,256]{2,0,1:T(4,128)(2,1)}, bf16[4,340,256]{2,0,1:T(4,128)(2,1)S(1)}, u32[]{:S(2)}, u32[]{:S(2)}) collective-permute-start(bf16[4,340,256]{2,0,1:T(4,128)(2,1)} %copy.20), channel_id=1, source_target_pairs={{0,16},{16,0},{1,17},{17,1},{2,18},{18,2},{3,19},{19,3},{4,20},{20... | collective-permute-start | bytes 2088968 | tf_op jit(solution)/shard_map/ppermute | solution.py:503
  50.9 4.8 %collective-permute-start.8 = (bf16[1552,256]{1,0:T(8,128)(2,1)}, bf16[1552,256]{1,0:T(8,128)(2,1)S(1)}, u32[]{:S(2)}, u32[]{:S(2)}) collective-permute-start(bf16[1552,256]{1,0:T(8,128)(2,1)} %get-tuple-element.35), channel_id=1, source_target_pairs={{0,16},{16,0},{1,17},{17,1},{2,18},{18,2},{3,19},{19,3},{4,20},{20... | collective-permute-start | bytes 2383880 | tf_op jit(solution)/shard_map/ppermute | solution.py:503
  51.3 2.9 %copy-start = (f32[4,340,256]{2,1,0:T(8,128)S(1)}, f32[4,340,256]{2,1,0:T(8,128)}, u32[]{:S(2)}) copy-start(f32[4,340,256]{2,1,0:T(8,128)} %get-tuple-element.32) | copy-start | bytes 4177924
  51.5 10.2 %collective-permute-start.17 = (bf16[768,256]{1,0:T(8,128)(2,1)S(1)}, bf16[768,256]{1,0:T(8,128)(2,1)S(1)}, u32[]{:S(2)}, u32[]{:S(2)}) collective-permute-start(bf16[768,256]{1,0:T(8,128)(2,1)S(1)} %constant_dynamic-slice_fusion.11), channel_id=1, source_target_pairs={{0,1},{1,0},{2,3},{3,2},{4,5},{5,4},{6,7},{7,6},{8,9},{9,8},{10,11... | collective-permute-start | bytes 1179656 | tf_op jit(solution)/shard_map/ppermute | solution.py:508
  54.4 1.1 copy-start.4
  54.6 1.2 %copy-start.1 = (bf16[1552,256]{1,0:T(8,128)(2,1)S(1)}, bf16[1552,256]{1,0:T(8,128)(2,1)}, u32[]{:S(2)}) copy-start(bf16[1552,256]{1,0:T(8,128)(2,1)} %get-tuple-element.34) | copy-start | bytes 2383876
  56.2 8.0 %collective-permute-start.9 = (bf16[784,256]{1,0:T(8,128)(2,1)S(1)}, bf16[784,256]{1,0:T(8,128)(2,1)S(1)}, u32[]{:S(2)}, u32[]{:S(2)}) collective-permute-start(bf16[784,256]{1,0:T(8,128)(2,1)S(1)} %pad_maximum_fusion), channel_id=1, source_target_pairs={{0,1},{1,0},{2,3},{3,2},{4,5},{5,4},{6,7},{7,6},{8,9},{9,8},{10,11... | collective-permute-start | bytes 1204232 | tf_op jit(solution)/shard_map/ppermute | solution.py:508
  61.9 7.0 %collective-permute-start.18 = (bf16[384,256]{1,0:T(8,128)(2,1)S(1)}, bf16[384,256]{1,0:T(8,128)(2,1)S(1)}, u32[]{:S(2)}, u32[]{:S(2)}) collective-permute-start(bf16[384,256]{1,0:T(8,128)(2,1)S(1)} %constant_dynamic-slice_fusion.2), channel_id=1, source_target_pairs={{0,4},{1,5},{2,6},{3,7},{4,0},{5,1},{6,2},{7,3},{8,12},{9,13},{10,... | collective-permute-start | bytes 589832 | tf_op jit(solution)/shard_map/ppermute | solution.py:508
  64.4 5.9 %collective-permute-start.10 = (bf16[400,256]{1,0:T(8,128)(2,1)S(1)}, bf16[400,256]{1,0:T(8,128)(2,1)S(1)}, u32[]{:S(2)}, u32[]{:S(2)}) collective-permute-start(bf16[400,256]{1,0:T(8,128)(2,1)S(1)} %pad_maximum_fusion.4), channel_id=1, source_target_pairs={{0,2},{1,3},{2,0},{3,1},{4,6},{5,7},{6,4},{7,5},{8,10},{9,11},{10,... | collective-permute-start | bytes 614408 | tf_op jit(solution)/shard_map/ppermute | solution.py:508
  69.0 4.7 %collective-permute-start.19 = (bf16[192,256]{1,0:T(8,128)(2,1)S(1)}, bf16[192,256]{1,0:T(8,128)(2,1)S(1)}, u32[]{:S(2)}, u32[]{:S(2)}) collective-permute-start(bf16[192,256]{1,0:T(8,128)(2,1)S(1)} %constant_dynamic-slice_fusion.1), channel_id=1, source_target_pairs={{0,2},{1,3},{2,0},{3,1},{4,6},{5,7},{6,4},{7,5},{8,10},{9,11},{10,... | collective-permute-start | bytes 294920 | tf_op jit(solution)/shard_map/ppermute | solution.py:508
  70.4 5.9 %collective-permute-start.11 = (bf16[208,256]{1,0:T(8,128)(2,1)S(1)}, bf16[208,256]{1,0:T(8,128)(2,1)S(1)}, u32[]{:S(2)}, u32[]{:S(2)}) collective-permute-start(bf16[208,256]{1,0:T(8,128)(2,1)S(1)} %pad_maximum_fusion.8), channel_id=1, source_target_pairs={{0,4},{1,5},{2,6},{3,7},{4,0},{5,1},{6,2},{7,3},{8,12},{9,13},{10,... | collective-permute-start | bytes 319496 | tf_op jit(solution)/shard_map/ppermute | solution.py:508
  73.7 5.5 %collective-permute-start.20 = (bf16[96,256]{1,0:T(8,128)(2,1)S(1)}, bf16[96,256]{1,0:T(8,128)(2,1)S(1)}, u32[]{:S(2)}, u32[]{:S(2)}) collective-permute-start(bf16[96,256]{1,0:T(8,128)(2,1)S(1)} %constant_dynamic-slice_fusion), channel_id=1, source_target_pairs={{0,8},{1,9},{2,10},{3,11},{4,12},{5,13},{6,14},{7,15},{8,0},{9,1},... | collective-permute-start | bytes 147464 | tf_op jit(solution)/shard_map/ppermute | solution.py:508
  76.5 6.3 %collective-permute-start.12 = (bf16[112,256]{1,0:T(8,128)(2,1)S(1)}, bf16[112,256]{1,0:T(8,128)(2,1)S(1)}, u32[]{:S(2)}, u32[]{:S(2)}) collective-permute-start(bf16[112,256]{1,0:T(8,128)(2,1)S(1)} %pad_maximum_fusion.12), channel_id=1, source_target_pairs={{0,8},{1,9},{2,10},{3,11},{4,12},{5,13},{6,14},{7,15},{8,0},{9,1},... | collective-permute-start | bytes 172040 | tf_op jit(solution)/shard_map/ppermute | solution.py:508
  79.3 6.5 %collective-permute-start.21 = (bf16[96,256]{1,0:T(8,128)(2,1)S(1)}, bf16[96,256]{1,0:T(8,128)(2,1)S(1)}, u32[]{:S(2)}, u32[]{:S(2)}) collective-permute-start(bf16[96,256]{1,0:T(8,128)(2,1)S(1)} %add_convert_fusion.9), channel_id=1, source_target_pairs={{0,8},{1,9},{2,10},{3,11},{4,12},{5,13},{6,14},{7,15},{8,0},{9,1},... | collective-permute-start | bytes 147464 | tf_op jit(solution)/shard_map/ppermute | solution.py:508
  82.8 5.1 %collective-permute-start.13 = (bf16[96,256]{1,0:T(8,128)(2,1)S(1)}, bf16[96,256]{1,0:T(8,128)(2,1)S(1)}, u32[]{:S(2)}, u32[]{:S(2)}) collective-permute-start(bf16[96,256]{1,0:T(8,128)(2,1)S(1)} %slice.75), channel_id=1, source_target_pairs={{0,8},{1,9},{2,10},{3,11},{4,12},{5,13},{6,14},{7,15},{8,0},{9,1},... | collective-permute-start | bytes 147464 | tf_op jit(solution)/shard_map/ppermute | solution.py:508
  85.8 4.7 %collective-permute-start.22 = (bf16[192,256]{1,0:T(8,128)(2,1)S(1)}, bf16[192,256]{1,0:T(8,128)(2,1)S(1)}, u32[]{:S(2)}, u32[]{:S(2)}) collective-permute-start(bf16[192,256]{1,0:T(8,128)(2,1)S(1)} %pad_maximum_fusion.11), channel_id=1, source_target_pairs={{0,2},{1,3},{2,0},{3,1},{4,6},{5,7},{6,4},{7,5},{8,10},{9,11},{10,... | collective-permute-start | bytes 294920 | tf_op jit(solution)/shard_map/ppermute | solution.py:508
  87.9 4.9 %collective-permute-start.14 = (bf16[192,256]{1,0:T(8,128)(2,1)S(1)}, bf16[192,256]{1,0:T(8,128)(2,1)S(1)}, u32[]{:S(2)}, u32[]{:S(2)}) collective-permute-start(bf16[192,256]{1,0:T(8,128)(2,1)S(1)} %pad_maximum_fusion.10), channel_id=1, source_target_pairs={{0,4},{1,5},{2,6},{3,7},{4,0},{5,1},{6,2},{7,3},{8,12},{9,13},{10,... | collective-permute-start | bytes 294920 | tf_op jit(solution)/shard_map/ppermute | solution.py:508
  90.6 5.7 %collective-permute-start.23 = (bf16[384,256]{1,0:T(8,128)(2,1)S(1)}, bf16[384,256]{1,0:T(8,128)(2,1)S(1)}, u32[]{:S(2)}, u32[]{:S(2)}) collective-permute-start(bf16[384,256]{1,0:T(8,128)(2,1)S(1)} %pad_maximum_fusion.7), channel_id=1, source_target_pairs={{0,4},{1,5},{2,6},{3,7},{4,0},{5,1},{6,2},{7,3},{8,12},{9,13},{10,... | collective-permute-start | bytes 589832 | tf_op jit(solution)/shard_map/ppermute | solution.py:508
  92.9 7.9 %collective-permute-start.15 = (bf16[384,256]{1,0:T(8,128)(2,1)S(1)}, bf16[384,256]{1,0:T(8,128)(2,1)S(1)}, u32[]{:S(2)}, u32[]{:S(2)}) collective-permute-start(bf16[384,256]{1,0:T(8,128)(2,1)S(1)} %pad_maximum_fusion.6), channel_id=1, source_target_pairs={{0,2},{1,3},{2,0},{3,1},{4,6},{5,7},{6,4},{7,5},{8,10},{9,11},{10,... | collective-permute-start | bytes 589832 | tf_op jit(solution)/shard_map/ppermute | solution.py:508
  96.4 7.8 %collective-permute-start.24 = (bf16[768,256]{1,0:T(8,128)(2,1)S(1)}, bf16[768,256]{1,0:T(8,128)(2,1)S(1)}, u32[]{:S(2)}, u32[]{:S(2)}) collective-permute-start(bf16[768,256]{1,0:T(8,128)(2,1)S(1)} %pad_maximum_fusion.3), channel_id=1, source_target_pairs={{0,1},{1,0},{2,3},{3,2},{4,5},{5,4},{6,7},{7,6},{8,9},{9,8},{10,11... | collective-permute-start | bytes 1179656 | tf_op jit(solution)/shard_map/ppermute | solution.py:508
  100.9 7.8 %collective-permute-start.16 = (bf16[768,256]{1,0:T(8,128)(2,1)S(1)}, bf16[768,256]{1,0:T(8,128)(2,1)S(1)}, u32[]{:S(2)}, u32[]{:S(2)}) collective-permute-start(bf16[768,256]{1,0:T(8,128)(2,1)S(1)} %pad_maximum_fusion.2), channel_id=1, source_target_pairs={{0,1},{1,0},{2,3},{3,2},{4,5},{5,4},{6,7},{7,6},{8,9},{9,8},{10,11... | collective-permute-start | bytes 1179656 | tf_op jit(solution)/shard_map/ppermute | solution.py:508
  (4 other events, 2.9 us)

commit v5 on v4

--- a/solution.py
+++ b/solution.py
@@ -231,7 +231,7 @@
                 end = min(hi, length)
                 y0, y1 = ybuf_ref[r, lo:hi, :][: end - lo], y[: end - lo]
                 yk_ref[r, lo:end, :] = jnp.where(first, y0, y1)
-                ys_ref[r, lo:end, :] = jnp.where(first, y1, y0)
+                ys_ref[r, lo:hi, :] = jnp.where(first, y, ybuf_ref[r, lo:hi, :])
 
         return [lambda: chunk(0, 0, LP), lambda: chunk(2, 0, LP), lambda: down(0, LP)]
 
@@ -318,7 +318,7 @@
                 end = min(hi, length)
                 d0, d1 = d_x[: end - lo], dbuf_ref[r, lo:hi, :][: end - lo]
                 dk_out_ref[r, lo:end, :] = jnp.where(first, d0, d1)
-                ds_out_ref[r, lo:end, :] = jnp.where(first, d1, d0).astype(BF)
+                ds_out_ref[r, lo:hi, :] = jnp.where(first, dbuf_ref[r, lo:hi, :], d_x).astype(BF)
 
         order = [(probs, 0), (probs, 1), (values, 0), (queries, 0), (probs, 2), (values, 1), (queries, 1)]
         order += [(probs, 3), (values, 2), (queries, 2), (values, 3), (queries, 3)]
@@ -389,71 +389,87 @@
             copies[-1].start()
 
         for n, l, p_out, q_out in ((0, 1 - sec, psend_hbm, qsend_hbm), (1, sec, pkeep_hbm, qkeep_hbm)):
-            for j in range(3):
-                grads_ref[n, 256 * j : 256 * j + 256, :] = aqkv_ref[l, :, 256 * j : 256 * j + 256].astype(BF)
-            grads_ref[n, 768:1024, :] = aout_ref[l].astype(BF)
+            for j in range(4):
+                grads_ref[n, 256 * j : 256 * j + 256, :] = aup_ref[l, :, 256 * j : 256 * j + 256].astype(BF)
             for j in range(2):
-                grads_ref[n, 1024 + 256 * j : 1280 + 256 * j, :] = aup_ref[l, :, 256 * j : 256 * j + 256].astype(BF)
+                grads_ref[n, 1024 + 256 * j : 1280 + 256 * j, :] = adown_ref[l, :, 256 * j : 256 * j + 256].astype(BF).T
             row = lax.broadcasted_iota(jnp.int32, (16, D), 0)
             attn = jnp.sum(again_ref[l, 0], axis=0, keepdims=True)
             mlp = jnp.sum(again_ref[l, 1], axis=0, keepdims=True)
             grads_ref[n, HALF : HALF + 16, :] = jnp.where(row == 0, attn, jnp.where(row == 1, mlp, 0.0)).astype(BF)
             hand(n, 0, HALF + 16, p_out)
+            for j in range(3):
+                grads_ref[n, 1552 + 256 * j : 1808 + 256 * j, :] = aqkv_ref[l, :, 256 * j : 256 * j + 256].astype(BF)
+            grads_ref[n, 2320:2576, :] = aout_ref[l].astype(BF)
             for j in range(2):
-                grads_ref[n, 1552 + 256 * j : 1808 + 256 * j, :] = aup_ref[l, :, 512 + 256 * j : 768 + 256 * j].astype(BF)
-            for j in range(4):
-                grads_ref[n, 2064 + 256 * j : 2320 + 256 * j, :] = adown_ref[l, :, 256 * j : 256 * j + 256].astype(BF).T
+                grads_ref[n, 2576 + 256 * j : 2832 + 256 * j, :] = adown_ref[l, :, 512 + 256 * j : 768 + 256 * j].astype(BF).T
             hand(n, HALF + 16, HALF, q_out)
         for copy in copies:
             copy.wait()
 
 
-def spread(sec_ref, seg_ref, x_hbm, cot_hbm, x_out, cot_out, eq_ref, ek_ref, x_ref, cot_ref, wide_ref, seg_pad_ref, sem):
+def spread(
+    sec_ref, seg_ref, x_hbm, cot_hbm, x_out, cot_out, eq_out, ek_out,
+    x_ref, cot_ref, x_rows, cot_rows, eq_ref, ek_ref, wide_ref, seg_pad_ref, sem, outsem,
+):
     length, count, _ = x_ref.shape
     begin = sec_ref[0] * (count // 2)
-    copies = [pltpu.make_async_copy(x_hbm, x_ref, sem.at[0]), pltpu.make_async_copy(cot_hbm, cot_ref, sem.at[1])]
-    for copy in copies:
+    loads = [pltpu.make_async_copy(x_hbm, x_ref, sem.at[0]), pltpu.make_async_copy(cot_hbm, cot_ref, sem.at[1])]
+    stores = [
+        pltpu.make_async_copy(held, out, outsem.at[n])
+        for n, (held, out) in enumerate(((eq_ref, eq_out), (ek_ref, ek_out), (x_rows, x_out), (cot_rows, cot_out)))
+    ]
+    for copy in loads:
         copy.start()
     seg_pad_ref[...] = jnp.full(seg_pad_ref.shape, -1, jnp.int32)
     seg_pad_ref[:, 0:length] = seg_ref[...]
     lane = lax.broadcasted_iota(jnp.int32, (LP, 128), 1)
     token = lax.broadcasted_iota(jnp.int32, (LP, 128), 0)
+    framed = lane < 64
     here = jnp.logical_and(token >= FRAME * lane, token < FRAME * lane + FRAME)
-    later = token >= FRAME * lane + FRAME
+    here = jnp.where(jnp.logical_and(framed, here), 1.0, 0.0)
+    later = jnp.where(jnp.logical_and(framed, token >= FRAME * lane + FRAME), BIG, 0.0)
+    piece = lax.broadcasted_iota(jnp.int32, (16, seg_pad_ref.shape[1]), 0)
+    column = lax.broadcasted_iota(jnp.int32, (16, 128), 1) - 64
+    unit = jnp.where(column == lax.broadcasted_iota(jnp.int32, (16, 128), 0), 1.0, 0.0).astype(BF)
     for r in range(count // 2):
-        seg = jnp.broadcast_to(seg_pad_ref[pl.ds(begin + r, 1), :], (128, seg_pad_ref.shape[1])).astype(F32).T[:LP]
-        same = seg == (lane - 64).astype(F32)
-        other = jnp.logical_and(jnp.logical_not(same), lane < 68)
-        eq_ref[r] = jnp.where(lane < 64, jnp.where(here, 1.0, 0.0), jnp.where(same, 1.0, 0.0)).astype(BF)
-        ek_ref[r] = jnp.where(lane < 64, jnp.where(later, BIG, 0.0), jnp.where(other, BIG, 0.0)).astype(BF)
-    for copy, taken, out in ((copies[0], x_ref, x_out), (copies[1], cot_ref, cot_out)):
-        copy.wait()
+        seg = jnp.broadcast_to(seg_pad_ref[pl.ds(begin + r, 1), :], piece.shape)
+        same = jnp.where(seg == piece, 1.0, 0.0).astype(BF)[:, :LP]
+        other = jnp.where(jnp.logical_and(seg != piece, piece < 4), BIG, 0.0).astype(BF)[:, :LP]
+        eq_ref[r] = (here + tmm(same, unit)).astype(BF)
+        ek_ref[r] = (later + tmm(other, unit)).astype(BF)
+    stores[0].start()
+    stores[1].start()
+    for n, (taken, rows) in enumerate(((x_ref, x_rows), (cot_ref, cot_rows))):
+        loads[n].wait()
         for p in range(2):
             wide_ref[p] = taken[:, :, 128 * p : 128 * p + 128].astype(F32).reshape(length * count, 128)
         for r in range(count // 2):
-            out[r, LP - 16 : LP, :] = jnp.zeros((16, D), BF)
+            rows[r, LP - 16 : LP, :] = jnp.zeros((16, D), BF)
             for p in range(2):
                 row = wide_ref[p, pl.ds(begin + r, length, stride=count), :]
-                out[r, 0:length, 128 * p : 128 * p + 128] = row.astype(BF)
+                rows[r, 0:length, 128 * p : 128 * p + 128] = row.astype(BF)
+        stores[2 + n].start()
+    for copy in stores:
+        copy.wait()
 
 
 def prepare(section, x, cot, segments):
     length, rows, _ = x.shape
     hbm = pl.BlockSpec(memory_space=pl.ANY)
-    vmem = pl.BlockSpec(memory_space=pltpu.VMEM)
     vm = pltpu.VMEM
-    tokens = jax.ShapeDtypeStruct((rows // 2, LP, D), BF)
-    columns = jax.ShapeDtypeStruct((rows // 2, LP, 128), BF)
+    tokens, columns = (rows // 2, LP, D), (rows // 2, LP, 128)
     return pl.pallas_call(
         spread,
-        in_specs=[pl.BlockSpec(memory_space=pltpu.SMEM), vmem, hbm, hbm],
-        out_specs=[vmem] * 4,
-        out_shape=[tokens, tokens, columns, columns],
+        in_specs=[pl.BlockSpec(memory_space=pltpu.SMEM), pl.BlockSpec(memory_space=pltpu.VMEM), hbm, hbm],
+        out_specs=[hbm] * 4,
+        out_shape=[jax.ShapeDtypeStruct(dims, BF) for dims in (tokens, tokens, columns, columns)],
         scratch_shapes=[
-            vm(x.shape, BF), vm(x.shape, BF), vm((2, length * rows, 128), F32), vm((rows, 384), jnp.int32),
-            pltpu.SemaphoreType.DMA((2,)),
+            vm(x.shape, BF), vm(x.shape, BF), vm(tokens, BF), vm(tokens, BF), vm(columns, BF), vm(columns, BF),
+            vm((2, length * rows, 128), F32), vm((rows, 384), jnp.int32),
+            pltpu.SemaphoreType.DMA((2,)), pltpu.SemaphoreType.DMA((4,)),
         ],
-        compiler_params=pltpu.CompilerParams(vmem_limit_bytes=60 * 1024 * 1024),
+        compiler_params=pltpu.CompilerParams(vmem_limit_bytes=65400 * 1024),
     )(section, segments, x, cot)
 
 
@@ -473,7 +489,7 @@
             num_scalar_prefetch=1,
             grid=(steps,),
             in_specs=[tok(D), tok(D), tok(128), tok(128)] + [whole((2, D))] * 2 + [hbm] * 8,
-            out_specs=[row_out, row_out, row_out, row_out, hbm, hbm, hbm, hbm],
+            out_specs=[row_out, tok(D), row_out, tok(D), hbm, hbm, hbm, hbm],
             scratch_shapes=[
                 vm((2, D, 3 * D), BF), vm((2, D, D), BF), vm((2, D, FF), BF), vm((2, FF, D), BF), pltpu.SemaphoreType.DMA((8,)), pltpu.SemaphoreType.DMA((4,)), vm((2, 3088, D), BF),
                 vm((2, 2, D), F32), vm((TWO, LP, D), BF), vm((TWO, LP, D), F32),
@@ -489,8 +505,8 @@
             ],
         ),
         out_shape=[
-            shape((count, length, D), BF), shape((count, length, D), BF),
-            shape((count, length, D), F32), shape((count, length, D), BF),
+            shape((count, length, D), BF), shape((count, LP, D), BF),
+            shape((count, length, D), F32), shape((count, LP, D), BF),
             shape((HALF + 16, D), BF), shape((HALF, D), BF), shape((HALF + 16, D), BF), shape((HALF, D), BF),
         ],
         compiler_params=pltpu.CompilerParams(
@@ -512,8 +528,20 @@
     return (a.astype(F32) + b.astype(F32)).astype(BF)
 
 
-def after(values, event):
-    return lax.optimization_barrier((values, event))[0]
+def idle(value_ref, event_ref, out_ref):
+    pass
+
+
+def after(value, event):
+    hbm = pl.BlockSpec(memory_space=pl.ANY)
+    return pl.pallas_call(
+        idle,
+        in_specs=[hbm, hbm],
+        out_specs=hbm,
+        out_shape=jax.ShapeDtypeStruct(value.shape, value.dtype),
+        input_output_aliases={0: 0},
+        compiler_params=pltpu.CompilerParams(vmem_limit_bytes=1024 * 1024),
+    )(value, event)
 
 
 def sum_over_dp(parts, tail, section, follow):
@@ -580,6 +608,8 @@
     acts, acts_send, grads, grads_send, first, second, first_send, second_send = local_step(
         here, rows_in, layer_input.shape[1], gains, other_gains, mine, other,
     )
+    length = layer_input.shape[1]
+    rows_sent = lambda a: partner(a.reshape(-1, D))
     got = partner(first_send), partner(second_send)
     parts = add(first, got[0]), add(second, got[1])
     low = section == 0
@@ -587,21 +617,22 @@
     def whole_rows(keep, got):
         return jnp.concatenate([jnp.where(low, keep, got), jnp.where(low, got, keep)], axis=0)
 
+    received = [rows_sent(a) for a in (acts_send, grads_send)]
+
     def rows_out(sent):
-        sends = (acts_send, grads_send)
-        got = partner(sends[0]), partner(sends[1])
-        got = after(got, sent[1])
+        got = [after(a, sent[0]) for a in received]
+        got = [a.reshape(acts_send.shape)[:, :length] for a in got]
         return whole_rows(acts, got[0]), whole_rows(grads, got[1].astype(F32))
 
-    ((qkv, out_up), (up_down, down)), rest, (activations, input_grads) = sum_over_dp(parts, 16, section, rows_out)
+    ((up, up_down), (qkv, out_down)), rest, (activations, input_grads) = sum_over_dp(parts, 16, section, rows_out)
     side = lambda *blocks: jnp.concatenate(blocks, axis=1).astype(F32)
     return (
         activations[None],
         input_grads[None],
         side(qkv[0:256], qkv[256:512], qkv[512:768])[None],
-        out_up[0:256].astype(F32)[None],
-        side(out_up[256:512], out_up[512:768], up_down[0:256], up_down[256:512])[None],
-        jnp.concatenate([up_down[512:768], down], axis=0).astype(F32)[None],
+        out_down[0:256].astype(F32)[None],
+        side(up[0:256], up[256:512], up[512:768], up_down[0:256])[None],
+        jnp.concatenate([up_down[256:768], out_down[256:768]], axis=0).astype(F32)[None],
         rest[0].astype(F32)[None],
         rest[1].astype(F32)[None],
     )

time: 112 us -> 110 us (0.982)
  local copies, waits for them, and re-layouts: 9.6 us -> 6.89 us
  waiting for transfers between devices: 23.4 us -> 21.4 us
  starting transfers between devices: 27.6 us -> 28.9 us
    pallas_call x2 -> x0, local copies, waits for them, and re-layouts: 3.45 us -> none  [local_step(): pl.pallas_call(kernel, grid_spec=pltpu.PrefetchScalarGridSpec(num_scalar_...]
    ppermute x16, waiting for transfers between devices: 23.4 us -> 20 us  [cross(): return lax.ppermute(value, ('section', 'dp'), pairs)]
    ppermute x9, waiting for transfers between devices: 0.02 us -> 1.5 us  [partner(): return lax.ppermute(value, 'section', [(0, 1), (1, 0)])]
    ppermute x16, starting transfers between devices: 24.9 us -> 26.2 us  [cross(): return lax.ppermute(value, ('section', 'dp'), pairs)]
    convert_element_type x10, other arithmetic: 0.93 us -> 2.06 us  [add(): return (a.astype(F32) + b.astype(F32)).astype(BF)]
    unnamed x24 -> x12, local copies, waits for them, and re-layouts: 5.88 us -> 6.54 us
    pallas_call x1 -> x3, Pallas kernels: 4.12 us -> 4.18 us  [the longest x1 4.18 us: prepare(): pl.pallas_call(spread, in_specs=[pl.BlockSpec(memory_space=pltpu.SMEM), p...]
  transfers between devices with their start and end apart: 25 -> 25, of which waited for: 14 -> 14; matrix products, arithmetic and copies ran while one was open for 11% -> 9% of each run, Pallas kernels for 4% -> 4%
where the time goes in v5:
time: 110 us; the launch traced here: 109 us
  Pallas kernels  42.6 us (39%)
  starting transfers between devices  28.9 us (26%)
  waiting for transfers between devices  21.4 us (19%)
  other arithmetic  8.48 us (8%)
  local copies, waits for them, and re-layouts  6.89 us (6%)
    pallas_call x1, Pallas kernels, local_step(): pl.pallas_call(kernel, grid_spec=pltpu.PrefetchScalarGridSpec(num_scalar_...  38.5 us
    ppermute x16, starting transfers between devices, cross(): return lax.ppermute(value, ('section', 'dp'), pairs)  26.2 us
    ppermute x16, waiting for transfers between devices, cross(): return lax.ppermute(value, ('section', 'dp'), pairs)  20 us
    unnamed x12, local copies, waits for them, and re-layouts  6.54 us
    pallas_call x1, Pallas kernels, prepare(): pl.pallas_call(spread, in_specs=[pl.BlockSpec(memory_space=pltpu.SMEM), p...  4.18 us
    ppermute x9, starting transfers between devices, partner(): return lax.ppermute(value, 'section', [(0, 1), (1, 0)])  2.69 us
  transfers between devices with their start and end apart: 25, of which 14 were waited for; matrix products, arithmetic and copies ran while one was open for 9% of the time, Pallas kernels for 4%

profile of v5, /device:TPU:0, one launch (start us, length us, event | category | flops | bytes accessed | tf_op | source)
XLA Modules:
  0.0 109.5 jit_solution(2556775975340185194)
XLA Ops:
  2.9 4.2 %shard_map.152 = (bf16[4,352,256]{2,1,0:T(8,128)(2,1)}, bf16[4,352,256]{2,1,0:T(8,128)(2,1)}, bf16[4,352,128]{2,1,0:T(8,128)(2,1)}, bf16[4,352,128]{2,1,0:T(8,128)(2,1)}) custom-call(s32[1]{0:T(128)} %bitcast.sec_ref, s32[8,340]{1,0:T(8,128)} %seg_ref.1, bf16[340,8,256]{2,1,0:T(8,128)(2,1)} %bitcast.36, bf16[340,8,256]{2,1,0:T(8,128)(2,1)} %bitcast.37), custom_call_target="tpu_custom_call" | custom-call | tf_op jit(solution)/shard_map/pallas_call | solution.py:462
  7.7 38.5 %shard_map.153 = (bf16[4,340,256]{2,1,0:T(8,128)(2,1)}, bf16[4,352,256]{2,1,0:T(8,128)(2,1)}, f32[4,340,256]{2,1,0:T(8,128)}, bf16[4,352,256]{2,1,0:T(8,128)(2,1...) custom-call(s32[1]{0:T(128)} %bitcast.sec_ref, ...), custom_call_target="tpu_custom_call" | custom-call | tf_op jit(solution)/shard_map/pallas_call | solution.py:486
  47.3 1.5 %collective-permute-done.8 = bf16[1536,256]{1,0:T(8,128)(2,1)S(1)} collective-permute-done((bf16[1536,256]{1,0:T(8,128)(2,1)}, bf16[1536,256]{1,0:T(8,128)(2,1)S(1)}, u32[]{:S(2)}, u32[]{:S(2)}) %collective-permute-start.8) | collective-permute-done | bytes 786464 | tf_op jit(solution)/shard_map/ppermute | solution.py:519
  48.7 1.4 %add_convert_fusion.1 = bf16[1536,256]{1,0:T(8,128)(2,1)S(1)} fusion(bf16[1536,256]{1,0:T(8,128)(2,1)S(1)} %collective-permute-done.8, bf16[1536,256]{1,0:T(8,128)(2,1)} %get-tuple-element.30), kind=kLoop, calls=%fused_computation.4 | loop fusion | flops 1572864 | bytes 2359296 | tf_op jit(solution)/shard_map/convert_element_type | solution.py:528
  50.2 2.7 %collective-permute-start.9 = (bf16[768,256]{1,0:T(8,128)(2,1)S(1)}, bf16[768,256]{1,0:T(8,128)(2,1)S(1)}, u32[]{:S(2)}, u32[]{:S(2)}) collective-permute-start(bf16[768,256]{1,0:T(8,128)(2,1)S(1)} %constant_dynamic-slice_fusion.10), channel_id=1, source_target_pairs={{0,1},{1,0},{2,3},{3,2},{4,5},{5,4},{6,7},{7,6},{8,9},{9,8},{10,11... | collective-permute-start | bytes 1179656 | tf_op jit(solution)/shard_map/ppermute | solution.py:524
  53.4 1.2 %copy-done = f32[4,340,256]{2,1,0:T(8,128)S(1)} copy-done((f32[4,340,256]{2,1,0:T(8,128)S(1)}, f32[4,340,256]{2,1,0:T(8,128)}, u32[]{:S(2)}) %copy-start) | copy-done | bytes 1392664
  55.0 1.1 copy-done.2
  56.3 1.4 %copy.19 = bf16[1,8,340,256]{3,1,2,0:T(8,128)(2,1)} copy(bf16[1,8,340,256]{3,2,1,0:T(8,128)(2,1)S(1)} %maximum_bitcast_fusion.1) | data formatting | bytes 2785280
  57.7 2.4 %copy.20 = f32[1,8,340,256]{3,1,2,0:T(8,128)} copy(f32[1,8,340,256]{3,2,1,0:T(8,128)S(1)} %maximum_bitcast_fusion) | data formatting | bytes 5570560
  60.3 1.6 %collective-permute-start.10 = (bf16[384,256]{1,0:T(8,128)(2,1)S(1)}, bf16[384,256]{1,0:T(8,128)(2,1)S(1)}, u32[]{:S(2)}, u32[]{:S(2)}) collective-permute-start(bf16[384,256]{1,0:T(8,128)(2,1)S(1)} %constant_dynamic-slice_fusion.9), channel_id=1, source_target_pairs={{0,4},{1,5},{2,6},{3,7},{4,0},{5,1},{6,2},{7,3},{8,12},{9,13},{10,... | collective-permute-start | bytes 589832 | tf_op jit(solution)/shard_map/ppermute | solution.py:524
  61.9 1.1 collective-permute-done.17
  63.2 2.1 %collective-permute-start.18 = (bf16[400,256]{1,0:T(8,128)(2,1)S(1)}, bf16[400,256]{1,0:T(8,128)(2,1)S(1)}, u32[]{:S(2)}, u32[]{:S(2)}) collective-permute-start(bf16[400,256]{1,0:T(8,128)(2,1)S(1)} %pad_maximum_fusion.4), channel_id=1, source_target_pairs={{0,2},{1,3},{2,0},{3,1},{4,6},{5,7},{6,4},{7,5},{8,10},{9,11},{10,... | collective-permute-start | bytes 614408 | tf_op jit(solution)/shard_map/ppermute | solution.py:524
  65.3 2.0 %collective-permute-done.10 = bf16[384,256]{1,0:T(8,128)(2,1)S(1)} collective-permute-done((bf16[384,256]{1,0:T(8,128)(2,1)S(1)}, bf16[384,256]{1,0:T(8,128)(2,1)S(1)}, u32[]{:S(2)}, u32[]{:S(2)}) %collective-permute-start.10) | collective-permute-done | bytes 196640 | tf_op jit(solution)/shard_map/ppermute | solution.py:524
  67.9 1.1 collective-permute-done.18
  69.1 2.2 %collective-permute-start.19 = (bf16[208,256]{1,0:T(8,128)(2,1)S(1)}, bf16[208,256]{1,0:T(8,128)(2,1)S(1)}, u32[]{:S(2)}, u32[]{:S(2)}) collective-permute-start(bf16[208,256]{1,0:T(8,128)(2,1)S(1)} %pad_maximum_fusion.8), channel_id=1, source_target_pairs={{0,4},{1,5},{2,6},{3,7},{4,0},{5,1},{6,2},{7,3},{8,12},{9,13},{10,... | collective-permute-start | bytes 319496 | tf_op jit(solution)/shard_map/ppermute | solution.py:524
  72.1 2.7 %collective-permute-start.12 = (bf16[96,256]{1,0:T(8,128)(2,1)S(1)}, bf16[96,256]{1,0:T(8,128)(2,1)S(1)}, u32[]{:S(2)}, u32[]{:S(2)}) collective-permute-start(bf16[96,256]{1,0:T(8,128)(2,1)S(1)} %constant_dynamic-slice_fusion.7), channel_id=1, source_target_pairs={{0,8},{1,9},{2,10},{3,11},{4,12},{5,13},{6,14},{7,15},{8,0},{9,1},... | collective-permute-start | bytes 147464 | tf_op jit(solution)/shard_map/ppermute | solution.py:524
  74.8 2.7 %collective-permute-start.20 = (bf16[112,256]{1,0:T(8,128)(2,1)S(1)}, bf16[112,256]{1,0:T(8,128)(2,1)S(1)}, u32[]{:S(2)}, u32[]{:S(2)}) collective-permute-start(bf16[112,256]{1,0:T(8,128)(2,1)S(1)} %pad_maximum_fusion.12), channel_id=1, source_target_pairs={{0,8},{1,9},{2,10},{3,11},{4,12},{5,13},{6,14},{7,15},{8,0},{9,1},... | collective-permute-start | bytes 172040 | tf_op jit(solution)/shard_map/ppermute | solution.py:524
  77.6 2.2 %collective-permute-start.13 = (bf16[96,256]{1,0:T(8,128)(2,1)S(1)}, bf16[96,256]{1,0:T(8,128)(2,1)S(1)}, u32[]{:S(2)}, u32[]{:S(2)}) collective-permute-start(bf16[96,256]{1,0:T(8,128)(2,1)S(1)} %add_convert_fusion.9), channel_id=1, source_target_pairs={{0,8},{1,9},{2,10},{3,11},{4,12},{5,13},{6,14},{7,15},{8,0},{9,1},... | collective-permute-start | bytes 147464 | tf_op jit(solution)/shard_map/ppermute | solution.py:524
  79.8 1.3 %collective-permute-done.20 = bf16[112,256]{1,0:T(8,128)(2,1)S(1)} collective-permute-done((bf16[112,256]{1,0:T(8,128)(2,1)S(1)}, bf16[112,256]{1,0:T(8,128)(2,1)S(1)}, u32[]{:S(2)}, u32[]{:S(2)}) %collective-permute-start.20) | collective-permute-done | bytes 57376 | tf_op jit(solution)/shard_map/ppermute | solution.py:524
  81.2 1.8 %collective-permute-start.21 = (bf16[96,256]{1,0:T(8,128)(2,1)S(1)}, bf16[96,256]{1,0:T(8,128)(2,1)S(1)}, u32[]{:S(2)}, u32[]{:S(2)}) collective-permute-start(bf16[96,256]{1,0:T(8,128)(2,1)S(1)} %slice.93), channel_id=1, source_target_pairs={{0,8},{1,9},{2,10},{3,11},{4,12},{5,13},{6,14},{7,15},{8,0},{9,1},... | collective-permute-start | bytes 147464 | tf_op jit(solution)/shard_map/ppermute | solution.py:524
  83.0 1.2 %collective-permute-done.13 = bf16[96,256]{1,0:T(8,128)(2,1)S(1)} collective-permute-done((bf16[96,256]{1,0:T(8,128)(2,1)S(1)}, bf16[96,256]{1,0:T(8,128)(2,1)S(1)}, u32[]{:S(2)}, u32[]{:S(2)}) %collective-permute-start.13) | collective-permute-done | bytes 49184 | tf_op jit(solution)/shard_map/ppermute | solution.py:524
  84.2 1.6 %collective-permute-start.14 = (bf16[192,256]{1,0:T(8,128)(2,1)S(1)}, bf16[192,256]{1,0:T(8,128)(2,1)S(1)}, u32[]{:S(2)}, u32[]{:S(2)}) collective-permute-start(bf16[192,256]{1,0:T(8,128)(2,1)S(1)} %pad_maximum_fusion.10), channel_id=1, source_target_pairs={{0,2},{1,3},{2,0},{3,1},{4,6},{5,7},{6,4},{7,5},{8,10},{9,11},{10,... | collective-permute-start | bytes 294920 | tf_op jit(solution)/shard_map/ppermute | solution.py:524
  86.3 1.2 %collective-permute-start.22 = (bf16[192,256]{1,0:T(8,128)(2,1)S(1)}, bf16[192,256]{1,0:T(8,128)(2,1)S(1)}, u32[]{:S(2)}, u32[]{:S(2)}) collective-permute-start(bf16[192,256]{1,0:T(8,128)(2,1)S(1)} %pad_maximum_fusion.11), channel_id=1, source_target_pairs={{0,4},{1,5},{2,6},{3,7},{4,0},{5,1},{6,2},{7,3},{8,12},{9,13},{10,... | collective-permute-start | bytes 294920 | tf_op jit(solution)/shard_map/ppermute | solution.py:524
  87.5 1.3 %collective-permute-done.14 = bf16[192,256]{1,0:T(8,128)(2,1)S(1)} collective-permute-done((bf16[192,256]{1,0:T(8,128)(2,1)S(1)}, bf16[192,256]{1,0:T(8,128)(2,1)S(1)}, u32[]{:S(2)}, u32[]{:S(2)}) %collective-permute-start.14) | collective-permute-done | bytes 98336 | tf_op jit(solution)/shard_map/ppermute | solution.py:524
  88.9 1.2 %collective-permute-start.15 = (bf16[384,256]{1,0:T(8,128)(2,1)S(1)}, bf16[384,256]{1,0:T(8,128)(2,1)S(1)}, u32[]{:S(2)}, u32[]{:S(2)}) collective-permute-start(bf16[384,256]{1,0:T(8,128)(2,1)S(1)} %pad_maximum_fusion.6), channel_id=1, source_target_pairs={{0,4},{1,5},{2,6},{3,7},{4,0},{5,1},{6,2},{7,3},{8,12},{9,13},{10,... | collective-permute-start | bytes 589832 | tf_op jit(solution)/shard_map/ppermute | solution.py:524
  91.6 3.0 %collective-permute-done.15 = bf16[384,256]{1,0:T(8,128)(2,1)S(1)} collective-permute-done((bf16[384,256]{1,0:T(8,128)(2,1)S(1)}, bf16[384,256]{1,0:T(8,128)(2,1)S(1)}, u32[]{:S(2)}, u32[]{:S(2)}) %collective-permute-start.15) | collective-permute-done | bytes 196640 | tf_op jit(solution)/shard_map/ppermute | solution.py:524
  94.8 1.6 %collective-permute-start.16 = (bf16[768,256]{1,0:T(8,128)(2,1)S(1)}, bf16[768,256]{1,0:T(8,128)(2,1)S(1)}, u32[]{:S(2)}, u32[]{:S(2)}) collective-permute-start(bf16[768,256]{1,0:T(8,128)(2,1)S(1)} %pad_maximum_fusion.2), channel_id=1, source_target_pairs={{0,1},{1,0},{2,3},{3,2},{4,5},{5,4},{6,7},{7,6},{8,9},{9,8},{10,11... | collective-permute-start | bytes 1179656 | tf_op jit(solution)/shard_map/ppermute | solution.py:524
  96.9 2.2 %collective-permute-done.23 = bf16[384,256]{1,0:T(8,128)(2,1)S(1)} collective-permute-done((bf16[384,256]{1,0:T(8,128)(2,1)S(1)}, bf16[384,256]{1,0:T(8,128)(2,1)S(1)}, u32[]{:S(2)}, u32[]{:S(2)}) %collective-permute-start.23) | collective-permute-done | bytes 196640 | tf_op jit(solution)/shard_map/ppermute | solution.py:524
  99.2 1.6 %collective-permute-start.24 = (bf16[768,256]{1,0:T(8,128)(2,1)S(1)}, bf16[768,256]{1,0:T(8,128)(2,1)S(1)}, u32[]{:S(2)}, u32[]{:S(2)}) collective-permute-start(bf16[768,256]{1,0:T(8,128)(2,1)S(1)} %pad_maximum_fusion.3), channel_id=1, source_target_pairs={{0,1},{1,0},{2,3},{3,2},{4,5},{5,4},{6,7},{7,6},{8,9},{9,8},{10,11... | collective-permute-start | bytes 1179656 | tf_op jit(solution)/shard_map/ppermute | solution.py:524
  100.8 1.8 %collective-permute-done.16 = bf16[768,256]{1,0:T(8,128)(2,1)S(1)} collective-permute-done((bf16[768,256]{1,0:T(8,128)(2,1)S(1)}, bf16[768,256]{1,0:T(8,128)(2,1)S(1)}, u32[]{:S(2)}, u32[]{:S(2)}) %collective-permute-start.16) | collective-permute-done | bytes 393248 | tf_op jit(solution)/shard_map/ppermute | solution.py:524
  104.5 2.6 %collective-permute-done.24 = bf16[768,256]{1,0:T(8,128)(2,1)S(1)} collective-permute-done((bf16[768,256]{1,0:T(8,128)(2,1)S(1)}, bf16[768,256]{1,0:T(8,128)(2,1)S(1)}, u32[]{:S(2)}, u32[]{:S(2)}) %collective-permute-start.24) | collective-permute-done | bytes 393248 | tf_op jit(solution)/shard_map/ppermute | solution.py:524
  108.4 1.1 maximum_convert_fusion
  (90 shorter events, 12.9 us)
Async XLA Ops:
  0.6 6.5 %collective-permute-start.3 = (bf16[1,256,1024]{2,1,0:T(8,128)(2,1)}, bf16[1,256,1024]{2,1,0:T(8,128)(2,1)}, u32[]{:S(2)}, u32[]{:S(2)}) collective-permute-start(bf16[1,256,1024]{2,1,0:T(8,128)(2,1)} %wup_mine.1), channel_id=1, source_target_pairs={{0,16},{16,0},{1,17},{17,1},{2,18},{18,2},{3,19},{19,3},{4,20},{20... | collective-permute-start | bytes 1572872 | tf_op jit(solution)/shard_map/ppermute | solution.py:519
  1.2 6.0 %collective-permute-start.4 = (bf16[1,1024,256]{2,1,0:T(8,128)(2,1)}, bf16[1,1024,256]{2,1,0:T(8,128)(2,1)}, u32[]{:S(2)}, u32[]{:S(2)}) collective-permute-start(bf16[1,1024,256]{2,1,0:T(8,128)(2,1)} %wdown_mine.1), channel_id=1, source_target_pairs={{0,16},{16,0},{1,17},{17,1},{2,18},{18,2},{3,19},{19,3},{4,20},{20... | collective-permute-start | bytes 1572872 | tf_op jit(solution)/shard_map/ppermute | solution.py:519
  1.2 5.9 %collective-permute-start.1 = (bf16[1,256,768]{2,1,0:T(8,128)(2,1)}, bf16[1,256,768]{2,1,0:T(8,128)(2,1)}, u32[]{:S(2)}, u32[]{:S(2)}) collective-permute-start(bf16[1,256,768]{2,1,0:T(8,128)(2,1)} %wqkv_mine.1), channel_id=1, source_target_pairs={{0,16},{16,0},{1,17},{17,1},{2,18},{18,2},{3,19},{19,3},{4,20},{20... | collective-permute-start | bytes 1179656 | tf_op jit(solution)/shard_map/ppermute | solution.py:519
  1.7 5.5 %collective-permute-start.2 = (bf16[1,256,256]{2,1,0:T(8,128)(2,1)}, bf16[1,256,256]{2,1,0:T(8,128)(2,1)}, u32[]{:S(2)}, u32[]{:S(2)}) collective-permute-start(bf16[1,256,256]{2,1,0:T(8,128)(2,1)} %wout_mine.1), channel_id=1, source_target_pairs={{0,16},{16,0},{1,17},{17,1},{2,18},{18,2},{3,19},{19,3},{4,20},{20... | collective-permute-start | bytes 393224 | tf_op jit(solution)/shard_map/ppermute | solution.py:519
  2.4 4.8 %copy-start.3 = (bf16[2,256]{1,0:T(2,128)(2,1)}, bf16[2,256]{1,0:T(2,128)(2,1)S(1)}, u32[]{:S(2)}) copy-start(bf16[2,256]{1,0:T(2,128)(2,1)S(1)} %pad_maximum_fusion.14.gains_mine) | copy-start | bytes 3076
  2.5 4.7 %collective-permute-start = (bf16[2,256]{1,0:T(2,128)(2,1)S(1)}, bf16[2,256]{1,0:T(2,128)(2,1)S(1)}, u32[]{:S(2)}, u32[]{:S(2)}) collective-permute-start(bf16[2,256]{1,0:T(2,128)(2,1)S(1)} %pad_maximum_fusion.14.gains_mine), channel_id=1, source_target_pairs={{0,16},{16,0},{1,17},{17,1},{2,18},{18,2},{3,19},{19,3},{4,20},{20... | collective-permute-start | bytes 3080 | tf_op jit(solution)/shard_map/ppermute | solution.py:519
  7.1 0.6 copy-start.4
  46.2 2.6 %collective-permute-start.8 = (bf16[1536,256]{1,0:T(8,128)(2,1)}, bf16[1536,256]{1,0:T(8,128)(2,1)S(1)}, u32[]{:S(2)}, u32[]{:S(2)}) collective-permute-start(bf16[1536,256]{1,0:T(8,128)(2,1)} %get-tuple-element.31), channel_id=1, source_target_pairs={{0,16},{16,0},{1,17},{17,1},{2,18},{18,2},{3,19},{19,3},{4,20},{20... | collective-permute-start | bytes 2359304 | tf_op jit(solution)/shard_map/ppermute | solution.py:519
  46.3 6.6 %collective-permute-start.6 = (bf16[1552,256]{1,0:T(8,128)(2,1)}, bf16[1552,256]{1,0:T(8,128)(2,1)S(1)}, u32[]{:S(2)}, u32[]{:S(2)}) collective-permute-start(bf16[1552,256]{1,0:T(8,128)(2,1)} %get-tuple-element.27), channel_id=1, source_target_pairs={{0,16},{16,0},{1,17},{17,1},{2,18},{18,2},{3,19},{19,3},{4,20},{20... | collective-permute-start | bytes 2383880 | tf_op jit(solution)/shard_map/ppermute | solution.py:519
  46.7 8.3 %collective-permute-start.5 = (bf16[1408,256]{1,0:T(8,128)(2,1)}, bf16[1408,256]{1,0:T(8,128)(2,1)S(1)}, u32[]{:S(2)}, u32[]{:S(2)}) collective-permute-start(bf16[1408,256]{1,0:T(8,128)(2,1)} %bitcast.38), channel_id=1, source_target_pairs={{0,16},{16,0},{1,17},{17,1},{2,18},{18,2},{3,19},{19,3},{4,20},{20... | collective-permute-start | bytes 2162696 | tf_op jit(solution)/shard_map/ppermute | solution.py:519
  46.8 6.5 %collective-permute-start.7 = (bf16[1408,256]{1,0:T(8,128)(2,1)}, bf16[1408,256]{1,0:T(8,128)(2,1)S(1)}, u32[]{:S(2)}, u32[]{:S(2)}) collective-permute-start(bf16[1408,256]{1,0:T(8,128)(2,1)} %bitcast.39), channel_id=1, source_target_pairs={{0,16},{16,0},{1,17},{17,1},{2,18},{18,2},{3,19},{19,3},{4,20},{20... | collective-permute-start | bytes 2162696 | tf_op jit(solution)/shard_map/ppermute | solution.py:519
  48.7 4.2 %copy-start.1 = (bf16[1552,256]{1,0:T(8,128)(2,1)S(1)}, bf16[1552,256]{1,0:T(8,128)(2,1)}, u32[]{:S(2)}) copy-start(bf16[1552,256]{1,0:T(8,128)(2,1)} %get-tuple-element.26) | copy-start | bytes 2383876
  50.2 9.9 %collective-permute-start.9 = (bf16[768,256]{1,0:T(8,128)(2,1)S(1)}, bf16[768,256]{1,0:T(8,128)(2,1)S(1)}, u32[]{:S(2)}, u32[]{:S(2)}) collective-permute-start(bf16[768,256]{1,0:T(8,128)(2,1)S(1)} %constant_dynamic-slice_fusion.10), channel_id=1, source_target_pairs={{0,1},{1,0},{2,3},{3,2},{4,5},{5,4},{6,7},{7,6},{8,9},{9,8},{10,11... | collective-permute-start | bytes 1179656 | tf_op jit(solution)/shard_map/ppermute | solution.py:524
  53.2 1.4 %copy-start = (f32[4,340,256]{2,1,0:T(8,128)S(1)}, f32[4,340,256]{2,1,0:T(8,128)}, u32[]{:S(2)}) copy-start(f32[4,340,256]{2,1,0:T(8,128)} %get-tuple-element.28) | copy-start | bytes 4177924
  53.3 9.7 %collective-permute-start.17 = (bf16[784,256]{1,0:T(8,128)(2,1)S(1)}, bf16[784,256]{1,0:T(8,128)(2,1)S(1)}, u32[]{:S(2)}, u32[]{:S(2)}) collective-permute-start(bf16[784,256]{1,0:T(8,128)(2,1)S(1)} %pad_maximum_fusion.1.event_ref), channel_id=1, source_target_pairs={{0,1},{1,0},{2,3},{3,2},{4,5},{5,4},{6,7},{7,6},{8,9},{9,8},{10,11... | collective-permute-start | bytes 1204232 | tf_op jit(solution)/shard_map/ppermute | solution.py:524
  55.0 1.1 %copy-start.2 = (bf16[4,340,256]{2,1,0:T(8,128)(2,1)S(1)}, bf16[4,340,256]{2,1,0:T(8,128)(2,1)}, u32[]{:S(2)}) copy-start(bf16[4,340,256]{2,1,0:T(8,128)(2,1)} %get-tuple-element.24) | copy-start | bytes 2088964
  60.3 7.0 %collective-permute-start.10 = (bf16[384,256]{1,0:T(8,128)(2,1)S(1)}, bf16[384,256]{1,0:T(8,128)(2,1)S(1)}, u32[]{:S(2)}, u32[]{:S(2)}) collective-permute-start(bf16[384,256]{1,0:T(8,128)(2,1)S(1)} %constant_dynamic-slice_fusion.9), channel_id=1, source_target_pairs={{0,4},{1,5},{2,6},{3,7},{4,0},{5,1},{6,2},{7,3},{8,12},{9,13},{10,... | collective-permute-start | bytes 589832 | tf_op jit(solution)/shard_map/ppermute | solution.py:524
  63.2 5.9 %collective-permute-start.18 = (bf16[400,256]{1,0:T(8,128)(2,1)S(1)}, bf16[400,256]{1,0:T(8,128)(2,1)S(1)}, u32[]{:S(2)}, u32[]{:S(2)}) collective-permute-start(bf16[400,256]{1,0:T(8,128)(2,1)S(1)} %pad_maximum_fusion.4), channel_id=1, source_target_pairs={{0,2},{1,3},{2,0},{3,1},{4,6},{5,7},{6,4},{7,5},{8,10},{9,11},{10,... | collective-permute-start | bytes 614408 | tf_op jit(solution)/shard_map/ppermute | solution.py:524
  67.3 4.7 %collective-permute-start.11 = (bf16[192,256]{1,0:T(8,128)(2,1)S(1)}, bf16[192,256]{1,0:T(8,128)(2,1)S(1)}, u32[]{:S(2)}, u32[]{:S(2)}) collective-permute-start(bf16[192,256]{1,0:T(8,128)(2,1)S(1)} %constant_dynamic-slice_fusion.8), channel_id=1, source_target_pairs={{0,2},{1,3},{2,0},{3,1},{4,6},{5,7},{6,4},{7,5},{8,10},{9,11},{10,... | collective-permute-start | bytes 294920 | tf_op jit(solution)/shard_map/ppermute | solution.py:524
  69.1 5.6 %collective-permute-start.19 = (bf16[208,256]{1,0:T(8,128)(2,1)S(1)}, bf16[208,256]{1,0:T(8,128)(2,1)S(1)}, u32[]{:S(2)}, u32[]{:S(2)}) collective-permute-start(bf16[208,256]{1,0:T(8,128)(2,1)S(1)} %pad_maximum_fusion.8), channel_id=1, source_target_pairs={{0,4},{1,5},{2,6},{3,7},{4,0},{5,1},{6,2},{7,3},{8,12},{9,13},{10,... | collective-permute-start | bytes 319496 | tf_op jit(solution)/shard_map/ppermute | solution.py:524
  72.1 5.5 %collective-permute-start.12 = (bf16[96,256]{1,0:T(8,128)(2,1)S(1)}, bf16[96,256]{1,0:T(8,128)(2,1)S(1)}, u32[]{:S(2)}, u32[]{:S(2)}) collective-permute-start(bf16[96,256]{1,0:T(8,128)(2,1)S(1)} %constant_dynamic-slice_fusion.7), channel_id=1, source_target_pairs={{0,8},{1,9},{2,10},{3,11},{4,12},{5,13},{6,14},{7,15},{8,0},{9,1},... | collective-permute-start | bytes 147464 | tf_op jit(solution)/shard_map/ppermute | solution.py:524
  74.8 6.3 %collective-permute-start.20 = (bf16[112,256]{1,0:T(8,128)(2,1)S(1)}, bf16[112,256]{1,0:T(8,128)(2,1)S(1)}, u32[]{:S(2)}, u32[]{:S(2)}) collective-permute-start(bf16[112,256]{1,0:T(8,128)(2,1)S(1)} %pad_maximum_fusion.12), channel_id=1, source_target_pairs={{0,8},{1,9},{2,10},{3,11},{4,12},{5,13},{6,14},{7,15},{8,0},{9,1},... | collective-permute-start | bytes 172040 | tf_op jit(solution)/shard_map/ppermute | solution.py:524
  77.6 6.5 %collective-permute-start.13 = (bf16[96,256]{1,0:T(8,128)(2,1)S(1)}, bf16[96,256]{1,0:T(8,128)(2,1)S(1)}, u32[]{:S(2)}, u32[]{:S(2)}) collective-permute-start(bf16[96,256]{1,0:T(8,128)(2,1)S(1)} %add_convert_fusion.9), channel_id=1, source_target_pairs={{0,8},{1,9},{2,10},{3,11},{4,12},{5,13},{6,14},{7,15},{8,0},{9,1},... | collective-permute-start | bytes 147464 | tf_op jit(solution)/shard_map/ppermute | solution.py:524
  81.2 5.1 %collective-permute-start.21 = (bf16[96,256]{1,0:T(8,128)(2,1)S(1)}, bf16[96,256]{1,0:T(8,128)(2,1)S(1)}, u32[]{:S(2)}, u32[]{:S(2)}) collective-permute-start(bf16[96,256]{1,0:T(8,128)(2,1)S(1)} %slice.93), channel_id=1, source_target_pairs={{0,8},{1,9},{2,10},{3,11},{4,12},{5,13},{6,14},{7,15},{8,0},{9,1},... | collective-permute-start | bytes 147464 | tf_op jit(solution)/shard_map/ppermute | solution.py:524
  84.2 4.7 %collective-permute-start.14 = (bf16[192,256]{1,0:T(8,128)(2,1)S(1)}, bf16[192,256]{1,0:T(8,128)(2,1)S(1)}, u32[]{:S(2)}, u32[]{:S(2)}) collective-permute-start(bf16[192,256]{1,0:T(8,128)(2,1)S(1)} %pad_maximum_fusion.10), channel_id=1, source_target_pairs={{0,2},{1,3},{2,0},{3,1},{4,6},{5,7},{6,4},{7,5},{8,10},{9,11},{10,... | collective-permute-start | bytes 294920 | tf_op jit(solution)/shard_map/ppermute | solution.py:524
  86.3 4.9 %collective-permute-start.22 = (bf16[192,256]{1,0:T(8,128)(2,1)S(1)}, bf16[192,256]{1,0:T(8,128)(2,1)S(1)}, u32[]{:S(2)}, u32[]{:S(2)}) collective-permute-start(bf16[192,256]{1,0:T(8,128)(2,1)S(1)} %pad_maximum_fusion.11), channel_id=1, source_target_pairs={{0,4},{1,5},{2,6},{3,7},{4,0},{5,1},{6,2},{7,3},{8,12},{9,13},{10,... | collective-permute-start | bytes 294920 | tf_op jit(solution)/shard_map/ppermute | solution.py:524
  88.9 5.7 %collective-permute-start.15 = (bf16[384,256]{1,0:T(8,128)(2,1)S(1)}, bf16[384,256]{1,0:T(8,128)(2,1)S(1)}, u32[]{:S(2)}, u32[]{:S(2)}) collective-permute-start(bf16[384,256]{1,0:T(8,128)(2,1)S(1)} %pad_maximum_fusion.6), channel_id=1, source_target_pairs={{0,4},{1,5},{2,6},{3,7},{4,0},{5,1},{6,2},{7,3},{8,12},{9,13},{10,... | collective-permute-start | bytes 589832 | tf_op jit(solution)/shard_map/ppermute | solution.py:524
  91.2 7.9 %collective-permute-start.23 = (bf16[384,256]{1,0:T(8,128)(2,1)S(1)}, bf16[384,256]{1,0:T(8,128)(2,1)S(1)}, u32[]{:S(2)}, u32[]{:S(2)}) collective-permute-start(bf16[384,256]{1,0:T(8,128)(2,1)S(1)} %pad_maximum_fusion.7), channel_id=1, source_target_pairs={{0,2},{1,3},{2,0},{3,1},{4,6},{5,7},{6,4},{7,5},{8,10},{9,11},{10,... | collective-permute-start | bytes 589832 | tf_op jit(solution)/shard_map/ppermute | solution.py:524
  94.8 7.8 %collective-permute-start.16 = (bf16[768,256]{1,0:T(8,128)(2,1)S(1)}, bf16[768,256]{1,0:T(8,128)(2,1)S(1)}, u32[]{:S(2)}, u32[]{:S(2)}) collective-permute-start(bf16[768,256]{1,0:T(8,128)(2,1)S(1)} %pad_maximum_fusion.2), channel_id=1, source_target_pairs={{0,1},{1,0},{2,3},{3,2},{4,5},{5,4},{6,7},{7,6},{8,9},{9,8},{10,11... | collective-permute-start | bytes 1179656 | tf_op jit(solution)/shard_map/ppermute | solution.py:524
  99.2 7.8 %collective-permute-start.24 = (bf16[768,256]{1,0:T(8,128)(2,1)S(1)}, bf16[768,256]{1,0:T(8,128)(2,1)S(1)}, u32[]{:S(2)}, u32[]{:S(2)}) collective-permute-start(bf16[768,256]{1,0:T(8,128)(2,1)S(1)} %pad_maximum_fusion.3), channel_id=1, source_target_pairs={{0,1},{1,0},{2,3},{3,2},{4,5},{5,4},{6,7},{7,6},{8,9},{9,8},{10,11... | collective-permute-start | bytes 1179656 | tf_op jit(solution)/shard_map/ppermute | solution.py:524

commit v6 on v5

--- a/solution.py
+++ b/solution.py
@@ -544,6 +544,16 @@
     )(value, event)
 
 
+def half_of(terms, tail, upper):
+    main = terms[0].shape[0] - tail
+    halves = [lax.dynamic_slice_in_dim(term, upper * (main // 2), main // 2, 0) for term in terms]
+    out = halves[0] if len(terms) == 1 else add(*halves)
+    if tail:
+        ends = [term[main:] for term in terms]
+        out = jnp.concatenate([out, ends[0] if len(terms) == 1 else add(*ends)], axis=0)
+    return out
+
+
 def sum_over_dp(parts, tail, section, follow):
     count = lax.axis_size("dp")
     place = lax.axis_index("dp")
@@ -563,23 +573,17 @@
             bits = orders[part][stage]
             upper = jnp.where(section == 0, place >> bits[0], place >> bits[1]) & 1
             uppers[part].append(upper)
-            value = current[part]
-            main = value.shape[0] - sizes[part]
-            send = lax.dynamic_slice_in_dim(value, (1 - upper) * (main // 2), main // 2, 0)
-            if sizes[part]:
-                send = jnp.concatenate([send, value[main:]], axis=0)
+            send = half_of(current[part], sizes[part], 1 - upper)
             got.append(cross(send, count, bits))
-            if stage == 0:
-                sent.append(send)
+            sent.append(send)
         if stage == 0:
             followed = follow(sent)
+        elif stage == 1:
+            followed = followed[0], after(followed[1], sent[3])
         for part in range(2):
-            value = current[part]
-            main = value.shape[0] - sizes[part]
-            keep = lax.dynamic_slice_in_dim(value, uppers[part][stage] * (main // 2), main // 2, 0)
-            if sizes[part]:
-                keep = jnp.concatenate([keep, value[main:]], axis=0)
-            current[part] = add(keep, got[part])
+            keep = half_of(current[part], sizes[part], uppers[part][stage])
+            current[part] = (add(keep, got[part]),)
+    current = [value for value, in current]
     rest = current[0][current[0].shape[0] - tail :]
     current[0] = current[0][: current[0].shape[0] - tail]
     halves = []
@@ -611,7 +615,7 @@
     length = layer_input.shape[1]
     rows_sent = lambda a: partner(a.reshape(-1, D))
     got = partner(first_send), partner(second_send)
-    parts = add(first, got[0]), add(second, got[1])
+    parts = (first, got[0]), (second, got[1])
     low = section == 0
 
     def whole_rows(keep, got):

time: 110 us -> 109 us (level)
  waiting for transfers between devices: 21.4 us -> 19.7 us
    ppermute x16, waiting for transfers between devices: 20 us -> 18.2 us  [cross(): return lax.ppermute(value, ('section', 'dp'), pairs)]
    convert_element_type x10 -> x11, other arithmetic: 2.06 us -> 2.49 us  [add(): return (a.astype(F32) + b.astype(F32)).astype(BF)]
    unnamed x12 -> x14, local copies, waits for them, and re-layouts: 6.54 us -> 6.56 us
  transfers between devices with their start and end apart: 25 -> 25, of which waited for: 14 -> 14; matrix products, arithmetic and copies ran while one was open for 9% -> 10% of each run, Pallas kernels for 4% -> 4%
where the time goes in v6:
time: 109 us; the launch traced here: 108 us
  Pallas kernels  42.6 us (39%)
  starting transfers between devices  29.4 us (27%)
  waiting for transfers between devices  19.7 us (18%)
  other arithmetic  8.89 us (8%)
  local copies, waits for them, and re-layouts  6.81 us (6%)
    pallas_call x1, Pallas kernels, local_step(): pl.pallas_call(kernel, grid_spec=pltpu.PrefetchScalarGridSpec(num_scalar_...  38.5 us
    ppermute x16, starting transfers between devices, cross(): return lax.ppermute(value, ('section', 'dp'), pairs)  26.7 us
    ppermute x16, waiting for transfers between devices, cross(): return lax.ppermute(value, ('section', 'dp'), pairs)  18.2 us
    unnamed x14, local copies, waits for them, and re-layouts  6.56 us
    pallas_call x1, Pallas kernels, prepare(): pl.pallas_call(spread, in_specs=[pl.BlockSpec(memory_space=pltpu.SMEM), p...  4.18 us
    ppermute x9, starting transfers between devices, partner(): return lax.ppermute(value, 'section', [(0, 1), (1, 0)])  2.69 us
    convert_element_type x11, other arithmetic, add(): return (a.astype(F32) + b.astype(F32)).astype(BF)  2.49 us
  transfers between devices with their start and end apart: 25, of which 14 were waited for; matrix products, arithmetic and copies ran while one was open for 10% of the time, Pallas kernels for 4%

profile of v6, /device:TPU:0, one launch (start us, length us, event | category | flops | bytes accessed | tf_op | source)
XLA Modules:
  0.0 108.5 jit_solution(12275653978102782481)
XLA Ops:
  2.9 4.2 %shard_map.152 = (bf16[4,352,256]{2,1,0:T(8,128)(2,1)}, bf16[4,352,256]{2,1,0:T(8,128)(2,1)}, bf16[4,352,128]{2,1,0:T(8,128)(2,1)}, bf16[4,352,128]{2,1,0:T(8,128)(2,1)}) custom-call(s32[1]{0:T(128)} %bitcast.sec_ref, s32[8,340]{1,0:T(8,128)} %seg_ref.1, bf16[340,8,256]{2,1,0:T(8,128)(2,1)} %bitcast.36, bf16[340,8,256]{2,1,0:T(8,128)(2,1)} %bitcast.37), custom_call_target="tpu_custom_call" | custom-call | tf_op jit(solution)/shard_map/pallas_call | solution.py:462
  7.7 38.5 %shard_map.153 = (bf16[4,340,256]{2,1,0:T(8,128)(2,1)}, bf16[4,352,256]{2,1,0:T(8,128)(2,1)}, f32[4,340,256]{2,1,0:T(8,128)}, bf16[4,352,256]{2,1,0:T(8,128)(2,1...) custom-call(s32[1]{0:T(128)} %bitcast.sec_ref, ...), custom_call_target="tpu_custom_call" | custom-call | tf_op jit(solution)/shard_map/pallas_call | solution.py:486
  47.3 1.5 %collective-permute-done.8 = bf16[1536,256]{1,0:T(8,128)(2,1)S(1)} collective-permute-done((bf16[1536,256]{1,0:T(8,128)(2,1)}, bf16[1536,256]{1,0:T(8,128)(2,1)S(1)}, u32[]{:S(2)}, u32[]{:S(2)}) %collective-permute-start.8) | collective-permute-done | bytes 786464 | tf_op jit(solution)/shard_map/ppermute | solution.py:519
  48.7 1.1 %add_convert_fusion.3 = bf16[768,256]{1,0:T(8,128)(2,1)S(1)} fusion(bf16[1536,256]{1,0:T(8,128)(2,1)S(1)} %collective-permute-done.8, s32[]{:T(128)S(6)} %select_n.179, bf16[1536,256]{1,0:T(8,128)(2,1)} %get-tuple-element.30), kind=kLoop, calls=%fused_computation.7 | loop fusion | flops 786432 | bytes 1179652 | tf_op jit(solution)/shard_map/convert_element_type | solution.py:528
  49.8 2.7 %collective-permute-start.9 = (bf16[768,256]{1,0:T(8,128)(2,1)S(1)}, bf16[768,256]{1,0:T(8,128)(2,1)S(1)}, u32[]{:S(2)}, u32[]{:S(2)}) collective-permute-start(bf16[768,256]{1,0:T(8,128)(2,1)S(1)} %add_convert_fusion.3), channel_id=1, source_target_pairs={{0,1},{1,0},{2,3},{3,2},{4,5},{5,4},{6,7},{7,6},{8,9},{9,8},{10,11... | collective-permute-start | bytes 1179656 | tf_op jit(solution)/shard_map/ppermute | solution.py:524
  53.6 1.2 %copy-done = f32[4,340,256]{2,1,0:T(8,128)S(1)} copy-done((f32[4,340,256]{2,1,0:T(8,128)S(1)}, f32[4,340,256]{2,1,0:T(8,128)}, u32[]{:S(2)}) %copy-start) | copy-done | bytes 1392664
  55.3 1.1 copy-done.3
  56.6 1.4 %copy.20 = bf16[1,8,340,256]{3,1,2,0:T(8,128)(2,1)} copy(bf16[1,8,340,256]{3,2,1,0:T(8,128)(2,1)S(1)} %maximum_bitcast_fusion) | data formatting | bytes 2785280
  58.5 2.2 %collective-permute-start.10 = (bf16[384,256]{1,0:T(8,128)(2,1)S(1)}, bf16[384,256]{1,0:T(8,128)(2,1)S(1)}, u32[]{:S(2)}, u32[]{:S(2)}) collective-permute-start(bf16[384,256]{1,0:T(8,128)(2,1)S(1)} %constant_dynamic-slice_fusion.6.event_ref), channel_id=1, source_target_pairs={{0,4},{1,5},{2,6},{3,7},{4,0},{5,1},{6,2},{7,3},{8,12},{9,13},{10,... | collective-permute-start | bytes 589832 | tf_op jit(solution)/shard_map/ppermute | solution.py:524
  60.7 2.4 %copy.21 = f32[1,8,340,256]{3,1,2,0:T(8,128)} copy(f32[1,8,340,256]{3,2,1,0:T(8,128)S(1)} %bitcast.33) | data formatting | bytes 5570560
  63.2 1.6 %collective-permute-start.18 = (bf16[400,256]{1,0:T(8,128)(2,1)S(1)}, bf16[400,256]{1,0:T(8,128)(2,1)S(1)}, u32[]{:S(2)}, u32[]{:S(2)}) collective-permute-start(bf16[400,256]{1,0:T(8,128)(2,1)S(1)} %pad_maximum_fusion.5), channel_id=1, source_target_pairs={{0,2},{1,3},{2,0},{3,1},{4,6},{5,7},{6,4},{7,5},{8,10},{9,11},{10,... | collective-permute-start | bytes 614408 | tf_op jit(solution)/shard_map/ppermute | solution.py:524
  65.3 1.7 %collective-permute-start.11 = (bf16[192,256]{1,0:T(8,128)(2,1)S(1)}, bf16[192,256]{1,0:T(8,128)(2,1)S(1)}, u32[]{:S(2)}, u32[]{:S(2)}) collective-permute-start(bf16[192,256]{1,0:T(8,128)(2,1)S(1)} %constant_dynamic-slice_fusion.5), channel_id=1, source_target_pairs={{0,2},{1,3},{2,0},{3,1},{4,6},{5,7},{6,4},{7,5},{8,10},{9,11},{10,... | collective-permute-start | bytes 294920 | tf_op jit(solution)/shard_map/ppermute | solution.py:524
  67.1 2.0 %collective-permute-done.18 = bf16[400,256]{1,0:T(8,128)(2,1)S(1)} collective-permute-done((bf16[400,256]{1,0:T(8,128)(2,1)S(1)}, bf16[400,256]{1,0:T(8,128)(2,1)S(1)}, u32[]{:S(2)}, u32[]{:S(2)}) %collective-permute-start.18) | collective-permute-done | bytes 204832 | tf_op jit(solution)/shard_map/ppermute | solution.py:524
  69.2 1.7 %collective-permute-start.19 = (bf16[208,256]{1,0:T(8,128)(2,1)S(1)}, bf16[208,256]{1,0:T(8,128)(2,1)S(1)}, u32[]{:S(2)}, u32[]{:S(2)}) collective-permute-start(bf16[208,256]{1,0:T(8,128)(2,1)S(1)} %pad_maximum_fusion.9), channel_id=1, source_target_pairs={{0,4},{1,5},{2,6},{3,7},{4,0},{5,1},{6,2},{7,3},{8,12},{9,13},{10,... | collective-permute-start | bytes 319496 | tf_op jit(solution)/shard_map/ppermute | solution.py:524
  70.9 2.7 %collective-permute-start.12 = (bf16[96,256]{1,0:T(8,128)(2,1)S(1)}, bf16[96,256]{1,0:T(8,128)(2,1)S(1)}, u32[]{:S(2)}, u32[]{:S(2)}) collective-permute-start(bf16[96,256]{1,0:T(8,128)(2,1)S(1)} %constant_dynamic-slice_fusion.4), channel_id=1, source_target_pairs={{0,8},{1,9},{2,10},{3,11},{4,12},{5,13},{6,14},{7,15},{8,0},{9,1},... | collective-permute-start | bytes 147464 | tf_op jit(solution)/shard_map/ppermute | solution.py:524
  74.6 2.2 %collective-permute-start.20 = (bf16[112,256]{1,0:T(8,128)(2,1)S(1)}, bf16[112,256]{1,0:T(8,128)(2,1)S(1)}, u32[]{:S(2)}, u32[]{:S(2)}) collective-permute-start(bf16[112,256]{1,0:T(8,128)(2,1)S(1)} %pad_maximum_fusion.13), channel_id=1, source_target_pairs={{0,8},{1,9},{2,10},{3,11},{4,12},{5,13},{6,14},{7,15},{8,0},{9,1},... | collective-permute-start | bytes 172040 | tf_op jit(solution)/shard_map/ppermute | solution.py:524
  77.7 1.4 %collective-permute-start.13 = (bf16[96,256]{1,0:T(8,128)(2,1)S(1)}, bf16[96,256]{1,0:T(8,128)(2,1)S(1)}, u32[]{:S(2)}, u32[]{:S(2)}) collective-permute-start(bf16[96,256]{1,0:T(8,128)(2,1)S(1)} %add_convert_fusion.11), channel_id=1, source_target_pairs={{0,8},{1,9},{2,10},{3,11},{4,12},{5,13},{6,14},{7,15},{8,0},{9,1},... | collective-permute-start | bytes 147464 | tf_op jit(solution)/shard_map/ppermute | solution.py:524
  79.8 2.2 %collective-permute-start.21 = (bf16[96,256]{1,0:T(8,128)(2,1)S(1)}, bf16[96,256]{1,0:T(8,128)(2,1)S(1)}, u32[]{:S(2)}, u32[]{:S(2)}) collective-permute-start(bf16[96,256]{1,0:T(8,128)(2,1)S(1)} %slice.98), channel_id=1, source_target_pairs={{0,8},{1,9},{2,10},{3,11},{4,12},{5,13},{6,14},{7,15},{8,0},{9,1},... | collective-permute-start | bytes 147464 | tf_op jit(solution)/shard_map/ppermute | solution.py:524
  81.9 1.5 %collective-permute-done.13 = bf16[96,256]{1,0:T(8,128)(2,1)S(1)} collective-permute-done((bf16[96,256]{1,0:T(8,128)(2,1)S(1)}, bf16[96,256]{1,0:T(8,128)(2,1)S(1)}, u32[]{:S(2)}, u32[]{:S(2)}) %collective-permute-start.13) | collective-permute-done | bytes 49184 | tf_op jit(solution)/shard_map/ppermute | solution.py:524
  83.5 1.5 %collective-permute-start.14 = (bf16[192,256]{1,0:T(8,128)(2,1)S(1)}, bf16[192,256]{1,0:T(8,128)(2,1)S(1)}, u32[]{:S(2)}, u32[]{:S(2)}) collective-permute-start(bf16[192,256]{1,0:T(8,128)(2,1)S(1)} %pad_maximum_fusion.11), channel_id=1, source_target_pairs={{0,2},{1,3},{2,0},{3,1},{4,6},{5,7},{6,4},{7,5},{8,10},{9,11},{10,... | collective-permute-start | bytes 294920 | tf_op jit(solution)/shard_map/ppermute | solution.py:524
  85.0 1.5 %collective-permute-start.22 = (bf16[192,256]{1,0:T(8,128)(2,1)S(1)}, bf16[192,256]{1,0:T(8,128)(2,1)S(1)}, u32[]{:S(2)}, u32[]{:S(2)}) collective-permute-start(bf16[192,256]{1,0:T(8,128)(2,1)S(1)} %pad_maximum_fusion.12), channel_id=1, source_target_pairs={{0,4},{1,5},{2,6},{3,7},{4,0},{5,1},{6,2},{7,3},{8,12},{9,13},{10,... | collective-permute-start | bytes 294920 | tf_op jit(solution)/shard_map/ppermute | solution.py:524
  86.5 1.6 %collective-permute-done.14 = bf16[192,256]{1,0:T(8,128)(2,1)S(1)} collective-permute-done((bf16[192,256]{1,0:T(8,128)(2,1)S(1)}, bf16[192,256]{1,0:T(8,128)(2,1)S(1)}, u32[]{:S(2)}, u32[]{:S(2)}) %collective-permute-start.14) | collective-permute-done | bytes 98336 | tf_op jit(solution)/shard_map/ppermute | solution.py:524
  88.8 1.2 %collective-permute-done.22 = bf16[192,256]{1,0:T(8,128)(2,1)S(1)} collective-permute-done((bf16[192,256]{1,0:T(8,128)(2,1)S(1)}, bf16[192,256]{1,0:T(8,128)(2,1)S(1)}, u32[]{:S(2)}, u32[]{:S(2)}) %collective-permute-start.22) | collective-permute-done | bytes 98336 | tf_op jit(solution)/shard_map/ppermute | solution.py:524
  90.1 1.5 %collective-permute-start.23 = (bf16[384,256]{1,0:T(8,128)(2,1)S(1)}, bf16[384,256]{1,0:T(8,128)(2,1)S(1)}, u32[]{:S(2)}, u32[]{:S(2)}) collective-permute-start(bf16[384,256]{1,0:T(8,128)(2,1)S(1)} %pad_maximum_fusion.8), channel_id=1, source_target_pairs={{0,2},{1,3},{2,0},{3,1},{4,6},{5,7},{6,4},{7,5},{8,10},{9,11},{10,... | collective-permute-start | bytes 589832 | tf_op jit(solution)/shard_map/ppermute | solution.py:524
  91.7 2.3 %collective-permute-done.15 = bf16[384,256]{1,0:T(8,128)(2,1)S(1)} collective-permute-done((bf16[384,256]{1,0:T(8,128)(2,1)S(1)}, bf16[384,256]{1,0:T(8,128)(2,1)S(1)}, u32[]{:S(2)}, u32[]{:S(2)}) %collective-permute-start.15) | collective-permute-done | bytes 196640 | tf_op jit(solution)/shard_map/ppermute | solution.py:524
  94.0 1.5 %collective-permute-start.16 = (bf16[768,256]{1,0:T(8,128)(2,1)S(1)}, bf16[768,256]{1,0:T(8,128)(2,1)S(1)}, u32[]{:S(2)}, u32[]{:S(2)}) collective-permute-start(bf16[768,256]{1,0:T(8,128)(2,1)S(1)} %pad_maximum_fusion.3), channel_id=1, source_target_pairs={{0,1},{1,0},{2,3},{3,2},{4,5},{5,4},{6,7},{7,6},{8,9},{9,8},{10,11... | collective-permute-start | bytes 1179656 | tf_op jit(solution)/shard_map/ppermute | solution.py:524
  96.1 1.9 %collective-permute-done.23 = bf16[384,256]{1,0:T(8,128)(2,1)S(1)} collective-permute-done((bf16[384,256]{1,0:T(8,128)(2,1)S(1)}, bf16[384,256]{1,0:T(8,128)(2,1)S(1)}, u32[]{:S(2)}, u32[]{:S(2)}) %collective-permute-start.23) | collective-permute-done | bytes 196640 | tf_op jit(solution)/shard_map/ppermute | solution.py:524
  98.2 1.5 %collective-permute-start.24 = (bf16[768,256]{1,0:T(8,128)(2,1)S(1)}, bf16[768,256]{1,0:T(8,128)(2,1)S(1)}, u32[]{:S(2)}, u32[]{:S(2)}) collective-permute-start(bf16[768,256]{1,0:T(8,128)(2,1)S(1)} %pad_maximum_fusion.4), channel_id=1, source_target_pairs={{0,1},{1,0},{2,3},{3,2},{4,5},{5,4},{6,7},{7,6},{8,9},{9,8},{10,11... | collective-permute-start | bytes 1179656 | tf_op jit(solution)/shard_map/ppermute | solution.py:524
  99.7 2.2 %collective-permute-done.16 = bf16[768,256]{1,0:T(8,128)(2,1)S(1)} collective-permute-done((bf16[768,256]{1,0:T(8,128)(2,1)S(1)}, bf16[768,256]{1,0:T(8,128)(2,1)S(1)}, u32[]{:S(2)}, u32[]{:S(2)}) %collective-permute-start.16) | collective-permute-done | bytes 393248 | tf_op jit(solution)/shard_map/ppermute | solution.py:524
  103.7 2.4 %collective-permute-done.24 = bf16[768,256]{1,0:T(8,128)(2,1)S(1)} collective-permute-done((bf16[768,256]{1,0:T(8,128)(2,1)S(1)}, bf16[768,256]{1,0:T(8,128)(2,1)S(1)}, u32[]{:S(2)}, u32[]{:S(2)}) %collective-permute-start.24) | collective-permute-done | bytes 393248 | tf_op jit(solution)/shard_map/ppermute | solution.py:524
  106.3 1.0 maximum_convert_fusion.1
  107.4 1.1 %maximum_convert_fusion = f32[1,256,1024]{2,1,0:T(8,128)} fusion(bf16[1,256,256]{2,1,0:T(8,128)(2,1)S(1)} %slice_bitcast_fusion.2, bf16[1,256,256]{2,1,0:T(8,128)(2,1)S(1)} %get-tuple-element.53, bf16[1,256,256]{2,1,0:T(8,128)(2,1)S(1)} %get-tuple-element.54, bf16[1,256,256]{2,1,0:T(8,128)(2,1)S(1)} %get-tuple-element.52), kind=kLoop, calls=%fused_computation.14 | loop fusion | flops 2097152 | bytes 1572864 | tf_op jit(solution)/shard_map/convert_element_type | solution.py:632
  (91 shorter events, 13.0 us)
Async XLA Ops:
  0.6 6.5 %collective-permute-start.3 = (bf16[1,256,1024]{2,1,0:T(8,128)(2,1)}, bf16[1,256,1024]{2,1,0:T(8,128)(2,1)}, u32[]{:S(2)}, u32[]{:S(2)}) collective-permute-start(bf16[1,256,1024]{2,1,0:T(8,128)(2,1)} %wup_mine.1), channel_id=1, source_target_pairs={{0,16},{16,0},{1,17},{17,1},{2,18},{18,2},{3,19},{19,3},{4,20},{20... | collective-permute-start | bytes 1572872 | tf_op jit(solution)/shard_map/ppermute | solution.py:519
  1.2 6.0 %collective-permute-start.4 = (bf16[1,1024,256]{2,1,0:T(8,128)(2,1)}, bf16[1,1024,256]{2,1,0:T(8,128)(2,1)}, u32[]{:S(2)}, u32[]{:S(2)}) collective-permute-start(bf16[1,1024,256]{2,1,0:T(8,128)(2,1)} %wdown_mine.1), channel_id=1, source_target_pairs={{0,16},{16,0},{1,17},{17,1},{2,18},{18,2},{3,19},{19,3},{4,20},{20... | collective-permute-start | bytes 1572872 | tf_op jit(solution)/shard_map/ppermute | solution.py:519
  1.2 5.9 %collective-permute-start.1 = (bf16[1,256,768]{2,1,0:T(8,128)(2,1)}, bf16[1,256,768]{2,1,0:T(8,128)(2,1)}, u32[]{:S(2)}, u32[]{:S(2)}) collective-permute-start(bf16[1,256,768]{2,1,0:T(8,128)(2,1)} %wqkv_mine.1), channel_id=1, source_target_pairs={{0,16},{16,0},{1,17},{17,1},{2,18},{18,2},{3,19},{19,3},{4,20},{20... | collective-permute-start | bytes 1179656 | tf_op jit(solution)/shard_map/ppermute | solution.py:519
  1.7 5.5 %collective-permute-start.2 = (bf16[1,256,256]{2,1,0:T(8,128)(2,1)}, bf16[1,256,256]{2,1,0:T(8,128)(2,1)}, u32[]{:S(2)}, u32[]{:S(2)}) collective-permute-start(bf16[1,256,256]{2,1,0:T(8,128)(2,1)} %wout_mine.1), channel_id=1, source_target_pairs={{0,16},{16,0},{1,17},{17,1},{2,18},{18,2},{3,19},{19,3},{4,20},{20... | collective-permute-start | bytes 393224 | tf_op jit(solution)/shard_map/ppermute | solution.py:519
  2.4 4.7 %copy-start.4 = (bf16[2,256]{1,0:T(2,128)(2,1)}, bf16[2,256]{1,0:T(2,128)(2,1)S(1)}, u32[]{:S(2)}) copy-start(bf16[2,256]{1,0:T(2,128)(2,1)S(1)} %pad_maximum_fusion.15.gains_mine) | copy-start | bytes 3076
  2.5 4.7 %collective-permute-start = (bf16[2,256]{1,0:T(2,128)(2,1)S(1)}, bf16[2,256]{1,0:T(2,128)(2,1)S(1)}, u32[]{:S(2)}, u32[]{:S(2)}) collective-permute-start(bf16[2,256]{1,0:T(2,128)(2,1)S(1)} %pad_maximum_fusion.15.gains_mine), channel_id=1, source_target_pairs={{0,16},{16,0},{1,17},{17,1},{2,18},{18,2},{3,19},{19,3},{4,20},{20... | collective-permute-start | bytes 3080 | tf_op jit(solution)/shard_map/ppermute | solution.py:519
  7.1 0.6 copy-start.5
  46.2 7.1 %copy-start.1 = (bf16[1552,256]{1,0:T(8,128)(2,1)S(1)}, bf16[1552,256]{1,0:T(8,128)(2,1)}, u32[]{:S(2)}) copy-start(bf16[1552,256]{1,0:T(8,128)(2,1)} %get-tuple-element.26) | copy-start | bytes 2383876
  46.2 2.6 %collective-permute-start.8 = (bf16[1536,256]{1,0:T(8,128)(2,1)}, bf16[1536,256]{1,0:T(8,128)(2,1)S(1)}, u32[]{:S(2)}, u32[]{:S(2)}) collective-permute-start(bf16[1536,256]{1,0:T(8,128)(2,1)} %get-tuple-element.31), channel_id=1, source_target_pairs={{0,16},{16,0},{1,17},{17,1},{2,18},{18,2},{3,19},{19,3},{4,20},{20... | collective-permute-start | bytes 2359304 | tf_op jit(solution)/shard_map/ppermute | solution.py:519
  46.3 6.2 %collective-permute-start.6 = (bf16[1552,256]{1,0:T(8,128)(2,1)}, bf16[1552,256]{1,0:T(8,128)(2,1)S(1)}, u32[]{:S(2)}, u32[]{:S(2)}) collective-permute-start(bf16[1552,256]{1,0:T(8,128)(2,1)} %get-tuple-element.27), channel_id=1, source_target_pairs={{0,16},{16,0},{1,17},{17,1},{2,18},{18,2},{3,19},{19,3},{4,20},{20... | collective-permute-start | bytes 2383880 | tf_op jit(solution)/shard_map/ppermute | solution.py:519
  46.8 6.8 %collective-permute-start.7 = (bf16[1408,256]{1,0:T(8,128)(2,1)}, bf16[1408,256]{1,0:T(8,128)(2,1)S(1)}, u32[]{:S(2)}, u32[]{:S(2)}) collective-permute-start(bf16[1408,256]{1,0:T(8,128)(2,1)} %bitcast.39), channel_id=1, source_target_pairs={{0,16},{16,0},{1,17},{17,1},{2,18},{18,2},{3,19},{19,3},{4,20},{20... | collective-permute-start | bytes 2162696 | tf_op jit(solution)/shard_map/ppermute | solution.py:519
  46.8 8.4 %collective-permute-start.5 = (bf16[1408,256]{1,0:T(8,128)(2,1)}, bf16[1408,256]{1,0:T(8,128)(2,1)S(1)}, u32[]{:S(2)}, u32[]{:S(2)}) collective-permute-start(bf16[1408,256]{1,0:T(8,128)(2,1)} %bitcast.38), channel_id=1, source_target_pairs={{0,16},{16,0},{1,17},{17,1},{2,18},{18,2},{3,19},{19,3},{4,20},{20... | collective-permute-start | bytes 2162696 | tf_op jit(solution)/shard_map/ppermute | solution.py:519
  49.8 8.4 %collective-permute-start.9 = (bf16[768,256]{1,0:T(8,128)(2,1)S(1)}, bf16[768,256]{1,0:T(8,128)(2,1)S(1)}, u32[]{:S(2)}, u32[]{:S(2)}) collective-permute-start(bf16[768,256]{1,0:T(8,128)(2,1)S(1)} %add_convert_fusion.3), channel_id=1, source_target_pairs={{0,1},{1,0},{2,3},{3,2},{4,5},{5,4},{6,7},{7,6},{8,9},{9,8},{10,11... | collective-permute-start | bytes 1179656 | tf_op jit(solution)/shard_map/ppermute | solution.py:524
  53.4 1.4 %copy-start = (f32[4,340,256]{2,1,0:T(8,128)S(1)}, f32[4,340,256]{2,1,0:T(8,128)}, u32[]{:S(2)}) copy-start(f32[4,340,256]{2,1,0:T(8,128)} %get-tuple-element.28) | copy-start | bytes 4177924
  53.5 9.6 %collective-permute-start.17 = (bf16[784,256]{1,0:T(8,128)(2,1)S(1)}, bf16[784,256]{1,0:T(8,128)(2,1)S(1)}, u32[]{:S(2)}, u32[]{:S(2)}) collective-permute-start(bf16[784,256]{1,0:T(8,128)(2,1)S(1)} %pad_maximum_fusion.2.event_ref), channel_id=1, source_target_pairs={{0,1},{1,0},{2,3},{3,2},{4,5},{5,4},{6,7},{7,6},{8,9},{9,8},{10,11... | collective-permute-start | bytes 1204232 | tf_op jit(solution)/shard_map/ppermute | solution.py:524
  55.2 1.1 %copy-start.3 = (bf16[4,340,256]{2,1,0:T(8,128)(2,1)S(1)}, bf16[4,340,256]{2,1,0:T(8,128)(2,1)}, u32[]{:S(2)}) copy-start(bf16[4,340,256]{2,1,0:T(8,128)(2,1)} %get-tuple-element.24) | copy-start | bytes 2088964
  56.6 1.7 %copy-start.2 = (bf16[1536,256]{1,0:T(8,128)(2,1)S(1)}, bf16[1536,256]{1,0:T(8,128)(2,1)}, u32[]{:S(2)}) copy-start(bf16[1536,256]{1,0:T(8,128)(2,1)} %get-tuple-element.30) | copy-start | bytes 2359300
  58.5 6.8 %collective-permute-start.10 = (bf16[384,256]{1,0:T(8,128)(2,1)S(1)}, bf16[384,256]{1,0:T(8,128)(2,1)S(1)}, u32[]{:S(2)}, u32[]{:S(2)}) collective-permute-start(bf16[384,256]{1,0:T(8,128)(2,1)S(1)} %constant_dynamic-slice_fusion.6.event_ref), channel_id=1, source_target_pairs={{0,4},{1,5},{2,6},{3,7},{4,0},{5,1},{6,2},{7,3},{8,12},{9,13},{10,... | collective-permute-start | bytes 589832 | tf_op jit(solution)/shard_map/ppermute | solution.py:524
  63.2 5.8 %collective-permute-start.18 = (bf16[400,256]{1,0:T(8,128)(2,1)S(1)}, bf16[400,256]{1,0:T(8,128)(2,1)S(1)}, u32[]{:S(2)}, u32[]{:S(2)}) collective-permute-start(bf16[400,256]{1,0:T(8,128)(2,1)S(1)} %pad_maximum_fusion.5), channel_id=1, source_target_pairs={{0,2},{1,3},{2,0},{3,1},{4,6},{5,7},{6,4},{7,5},{8,10},{9,11},{10,... | collective-permute-start | bytes 614408 | tf_op jit(solution)/shard_map/ppermute | solution.py:524
  65.3 5.5 %collective-permute-start.11 = (bf16[192,256]{1,0:T(8,128)(2,1)S(1)}, bf16[192,256]{1,0:T(8,128)(2,1)S(1)}, u32[]{:S(2)}, u32[]{:S(2)}) collective-permute-start(bf16[192,256]{1,0:T(8,128)(2,1)S(1)} %constant_dynamic-slice_fusion.5), channel_id=1, source_target_pairs={{0,2},{1,3},{2,0},{3,1},{4,6},{5,7},{6,4},{7,5},{8,10},{9,11},{10,... | collective-permute-start | bytes 294920 | tf_op jit(solution)/shard_map/ppermute | solution.py:524
  69.2 5.3 %collective-permute-start.19 = (bf16[208,256]{1,0:T(8,128)(2,1)S(1)}, bf16[208,256]{1,0:T(8,128)(2,1)S(1)}, u32[]{:S(2)}, u32[]{:S(2)}) collective-permute-start(bf16[208,256]{1,0:T(8,128)(2,1)S(1)} %pad_maximum_fusion.9), channel_id=1, source_target_pairs={{0,4},{1,5},{2,6},{3,7},{4,0},{5,1},{6,2},{7,3},{8,12},{9,13},{10,... | collective-permute-start | bytes 319496 | tf_op jit(solution)/shard_map/ppermute | solution.py:524
  70.9 6.7 %collective-permute-start.12 = (bf16[96,256]{1,0:T(8,128)(2,1)S(1)}, bf16[96,256]{1,0:T(8,128)(2,1)S(1)}, u32[]{:S(2)}, u32[]{:S(2)}) collective-permute-start(bf16[96,256]{1,0:T(8,128)(2,1)S(1)} %constant_dynamic-slice_fusion.4), channel_id=1, source_target_pairs={{0,8},{1,9},{2,10},{3,11},{4,12},{5,13},{6,14},{7,15},{8,0},{9,1},... | collective-permute-start | bytes 147464 | tf_op jit(solution)/shard_map/ppermute | solution.py:524
  74.6 5.2 %collective-permute-start.20 = (bf16[112,256]{1,0:T(8,128)(2,1)S(1)}, bf16[112,256]{1,0:T(8,128)(2,1)S(1)}, u32[]{:S(2)}, u32[]{:S(2)}) collective-permute-start(bf16[112,256]{1,0:T(8,128)(2,1)S(1)} %pad_maximum_fusion.13), channel_id=1, source_target_pairs={{0,8},{1,9},{2,10},{3,11},{4,12},{5,13},{6,14},{7,15},{8,0},{9,1},... | collective-permute-start | bytes 172040 | tf_op jit(solution)/shard_map/ppermute | solution.py:524
  77.7 5.7 %collective-permute-start.13 = (bf16[96,256]{1,0:T(8,128)(2,1)S(1)}, bf16[96,256]{1,0:T(8,128)(2,1)S(1)}, u32[]{:S(2)}, u32[]{:S(2)}) collective-permute-start(bf16[96,256]{1,0:T(8,128)(2,1)S(1)} %add_convert_fusion.11), channel_id=1, source_target_pairs={{0,8},{1,9},{2,10},{3,11},{4,12},{5,13},{6,14},{7,15},{8,0},{9,1},... | collective-permute-start | bytes 147464 | tf_op jit(solution)/shard_map/ppermute | solution.py:524
  79.8 5.2 %collective-permute-start.21 = (bf16[96,256]{1,0:T(8,128)(2,1)S(1)}, bf16[96,256]{1,0:T(8,128)(2,1)S(1)}, u32[]{:S(2)}, u32[]{:S(2)}) collective-permute-start(bf16[96,256]{1,0:T(8,128)(2,1)S(1)} %slice.98), channel_id=1, source_target_pairs={{0,8},{1,9},{2,10},{3,11},{4,12},{5,13},{6,14},{7,15},{8,0},{9,1},... | collective-permute-start | bytes 147464 | tf_op jit(solution)/shard_map/ppermute | solution.py:524
  83.5 4.7 %collective-permute-start.14 = (bf16[192,256]{1,0:T(8,128)(2,1)S(1)}, bf16[192,256]{1,0:T(8,128)(2,1)S(1)}, u32[]{:S(2)}, u32[]{:S(2)}) collective-permute-start(bf16[192,256]{1,0:T(8,128)(2,1)S(1)} %pad_maximum_fusion.11), channel_id=1, source_target_pairs={{0,2},{1,3},{2,0},{3,1},{4,6},{5,7},{6,4},{7,5},{8,10},{9,11},{10,... | collective-permute-start | bytes 294920 | tf_op jit(solution)/shard_map/ppermute | solution.py:524
  85.0 5.1 %collective-permute-start.22 = (bf16[192,256]{1,0:T(8,128)(2,1)S(1)}, bf16[192,256]{1,0:T(8,128)(2,1)S(1)}, u32[]{:S(2)}, u32[]{:S(2)}) collective-permute-start(bf16[192,256]{1,0:T(8,128)(2,1)S(1)} %pad_maximum_fusion.12), channel_id=1, source_target_pairs={{0,4},{1,5},{2,6},{3,7},{4,0},{5,1},{6,2},{7,3},{8,12},{9,13},{10,... | collective-permute-start | bytes 294920 | tf_op jit(solution)/shard_map/ppermute | solution.py:524
  88.2 5.7 %collective-permute-start.15 = (bf16[384,256]{1,0:T(8,128)(2,1)S(1)}, bf16[384,256]{1,0:T(8,128)(2,1)S(1)}, u32[]{:S(2)}, u32[]{:S(2)}) collective-permute-start(bf16[384,256]{1,0:T(8,128)(2,1)S(1)} %pad_maximum_fusion.7), channel_id=1, source_target_pairs={{0,4},{1,5},{2,6},{3,7},{4,0},{5,1},{6,2},{7,3},{8,12},{9,13},{10,... | collective-permute-start | bytes 589832 | tf_op jit(solution)/shard_map/ppermute | solution.py:524
  90.1 7.9 %collective-permute-start.23 = (bf16[384,256]{1,0:T(8,128)(2,1)S(1)}, bf16[384,256]{1,0:T(8,128)(2,1)S(1)}, u32[]{:S(2)}, u32[]{:S(2)}) collective-permute-start(bf16[384,256]{1,0:T(8,128)(2,1)S(1)} %pad_maximum_fusion.8), channel_id=1, source_target_pairs={{0,2},{1,3},{2,0},{3,1},{4,6},{5,7},{6,4},{7,5},{8,10},{9,11},{10,... | collective-permute-start | bytes 589832 | tf_op jit(solution)/shard_map/ppermute | solution.py:524
  94.0 7.8 %collective-permute-start.16 = (bf16[768,256]{1,0:T(8,128)(2,1)S(1)}, bf16[768,256]{1,0:T(8,128)(2,1)S(1)}, u32[]{:S(2)}, u32[]{:S(2)}) collective-permute-start(bf16[768,256]{1,0:T(8,128)(2,1)S(1)} %pad_maximum_fusion.3), channel_id=1, source_target_pairs={{0,1},{1,0},{2,3},{3,2},{4,5},{5,4},{6,7},{7,6},{8,9},{9,8},{10,11... | collective-permute-start | bytes 1179656 | tf_op jit(solution)/shard_map/ppermute | solution.py:524
  98.2 7.9 %collective-permute-start.24 = (bf16[768,256]{1,0:T(8,128)(2,1)S(1)}, bf16[768,256]{1,0:T(8,128)(2,1)S(1)}, u32[]{:S(2)}, u32[]{:S(2)}) collective-permute-start(bf16[768,256]{1,0:T(8,128)(2,1)S(1)} %pad_maximum_fusion.4), channel_id=1, source_target_pairs={{0,1},{1,0},{2,3},{3,2},{4,5},{5,4},{6,7},{7,6},{8,9},{9,8},{10,11... | collective-permute-start | bytes 1179656 | tf_op jit(solution)/shard_map/ppermute | solution.py:524

commit v7 on v6

--- a/solution.py
+++ b/solution.py
@@ -188,7 +188,7 @@
             for p, _ in PAIRS:
                 s = held[q0][p]
                 e = jnp.exp(s - jnp.max(s, axis=-1, keepdims=True))
-                prob = (e * (1.0 / jnp.sum(e, axis=-1, keepdims=True))).astype(BF)
+                prob = (e * pl.reciprocal(jnp.sum(e, axis=-1, keepdims=True), approx=True)).astype(BF)
                 p_ref[l, r, pair_rows(p, q0, q1), 0 : k1 - k0] = prob
                 probs.append(prob)
             o = mm(jnp.concatenate(probs, axis=0), v_ref[l, r, k0:k1, :])

time: 109 us -> 109 us (level)
  no operation moved by 1% of the time
where the time goes in v7:
time: 109 us; the launch traced here: 108 us
  Pallas kernels  42.6 us (39%)
  starting transfers between devices  29.4 us (27%)
  waiting for transfers between devices  19.7 us (18%)
  other arithmetic  8.89 us (8%)
  local copies, waits for them, and re-layouts  6.81 us (6%)
    pallas_call x1, Pallas kernels, local_step(): pl.pallas_call(kernel, grid_spec=pltpu.PrefetchScalarGridSpec(num_scalar_...  38.5 us
    ppermute x16, starting transfers between devices, cross(): return lax.ppermute(value, ('section', 'dp'), pairs)  26.7 us
    ppermute x16, waiting for transfers between devices, cross(): return lax.ppermute(value, ('section', 'dp'), pairs)  18.2 us
    unnamed x14, local copies, waits for them, and re-layouts  6.56 us
    pallas_call x1, Pallas kernels, prepare(): pl.pallas_call(spread, in_specs=[pl.BlockSpec(memory_space=pltpu.SMEM), p...  4.18 us
    ppermute x9, starting transfers between devices, partner(): return lax.ppermute(value, 'section', [(0, 1), (1, 0)])  2.69 us
    convert_element_type x11, other arithmetic, add(): return (a.astype(F32) + b.astype(F32)).astype(BF)  2.49 us
  transfers between devices with their start and end apart: 25, of which 14 were waited for; matrix products, arithmetic and copies ran while one was open for 10% of the time, Pallas kernels for 4%

profile of v7, /device:TPU:0, one launch (start us, length us, event | category | flops | bytes accessed | tf_op | source)
XLA Modules:
  0.0 108.5 jit_solution(12275653978102782481)
XLA Ops:
  2.9 4.2 %shard_map.152 = (bf16[4,352,256]{2,1,0:T(8,128)(2,1)}, bf16[4,352,256]{2,1,0:T(8,128)(2,1)}, bf16[4,352,128]{2,1,0:T(8,128)(2,1)}, bf16[4,352,128]{2,1,0:T(8,128)(2,1)}) custom-call(s32[1]{0:T(128)} %bitcast.sec_ref, s32[8,340]{1,0:T(8,128)} %seg_ref.1, bf16[340,8,256]{2,1,0:T(8,128)(2,1)} %bitcast.36, bf16[340,8,256]{2,1,0:T(8,128)(2,1)} %bitcast.37), custom_call_target="tpu_custom_call" | custom-call | tf_op jit(solution)/shard_map/pallas_call | solution.py:462
  7.7 38.5 %shard_map.153 = (bf16[4,340,256]{2,1,0:T(8,128)(2,1)}, bf16[4,352,256]{2,1,0:T(8,128)(2,1)}, f32[4,340,256]{2,1,0:T(8,128)}, bf16[4,352,256]{2,1,0:T(8,128)(2,1...) custom-call(s32[1]{0:T(128)} %bitcast.sec_ref, ...), custom_call_target="tpu_custom_call" | custom-call | tf_op jit(solution)/shard_map/pallas_call | solution.py:486
  47.3 1.5 %collective-permute-done.8 = bf16[1536,256]{1,0:T(8,128)(2,1)S(1)} collective-permute-done((bf16[1536,256]{1,0:T(8,128)(2,1)}, bf16[1536,256]{1,0:T(8,128)(2,1)S(1)}, u32[]{:S(2)}, u32[]{:S(2)}) %collective-permute-start.8) | collective-permute-done | bytes 786464 | tf_op jit(solution)/shard_map/ppermute | solution.py:519
  48.7 1.1 %add_convert_fusion.3 = bf16[768,256]{1,0:T(8,128)(2,1)S(1)} fusion(bf16[1536,256]{1,0:T(8,128)(2,1)S(1)} %collective-permute-done.8, s32[]{:T(128)S(6)} %select_n.179, bf16[1536,256]{1,0:T(8,128)(2,1)} %get-tuple-element.30), kind=kLoop, calls=%fused_computation.7 | loop fusion | flops 786432 | bytes 1179652 | tf_op jit(solution)/shard_map/convert_element_type | solution.py:528
  49.8 2.7 %collective-permute-start.9 = (bf16[768,256]{1,0:T(8,128)(2,1)S(1)}, bf16[768,256]{1,0:T(8,128)(2,1)S(1)}, u32[]{:S(2)}, u32[]{:S(2)}) collective-permute-start(bf16[768,256]{1,0:T(8,128)(2,1)S(1)} %add_convert_fusion.3), channel_id=1, source_target_pairs={{0,1},{1,0},{2,3},{3,2},{4,5},{5,4},{6,7},{7,6},{8,9},{9,8},{10,11... | collective-permute-start | bytes 1179656 | tf_op jit(solution)/shard_map/ppermute | solution.py:524
  53.6 1.2 %copy-done = f32[4,340,256]{2,1,0:T(8,128)S(1)} copy-done((f32[4,340,256]{2,1,0:T(8,128)S(1)}, f32[4,340,256]{2,1,0:T(8,128)}, u32[]{:S(2)}) %copy-start) | copy-done | bytes 1392664
  55.3 1.1 copy-done.3
  56.6 1.4 %copy.20 = bf16[1,8,340,256]{3,1,2,0:T(8,128)(2,1)} copy(bf16[1,8,340,256]{3,2,1,0:T(8,128)(2,1)S(1)} %maximum_bitcast_fusion) | data formatting | bytes 2785280
  58.5 2.2 %collective-permute-start.10 = (bf16[384,256]{1,0:T(8,128)(2,1)S(1)}, bf16[384,256]{1,0:T(8,128)(2,1)S(1)}, u32[]{:S(2)}, u32[]{:S(2)}) collective-permute-start(bf16[384,256]{1,0:T(8,128)(2,1)S(1)} %constant_dynamic-slice_fusion.6.event_ref), channel_id=1, source_target_pairs={{0,4},{1,5},{2,6},{3,7},{4,0},{5,1},{6,2},{7,3},{8,12},{9,13},{10,... | collective-permute-start | bytes 589832 | tf_op jit(solution)/shard_map/ppermute | solution.py:524
  60.7 2.4 %copy.21 = f32[1,8,340,256]{3,1,2,0:T(8,128)} copy(f32[1,8,340,256]{3,2,1,0:T(8,128)S(1)} %bitcast.33) | data formatting | bytes 5570560
  63.2 1.6 %collective-permute-start.18 = (bf16[400,256]{1,0:T(8,128)(2,1)S(1)}, bf16[400,256]{1,0:T(8,128)(2,1)S(1)}, u32[]{:S(2)}, u32[]{:S(2)}) collective-permute-start(bf16[400,256]{1,0:T(8,128)(2,1)S(1)} %pad_maximum_fusion.5), channel_id=1, source_target_pairs={{0,2},{1,3},{2,0},{3,1},{4,6},{5,7},{6,4},{7,5},{8,10},{9,11},{10,... | collective-permute-start | bytes 614408 | tf_op jit(solution)/shard_map/ppermute | solution.py:524
  65.3 1.7 %collective-permute-start.11 = (bf16[192,256]{1,0:T(8,128)(2,1)S(1)}, bf16[192,256]{1,0:T(8,128)(2,1)S(1)}, u32[]{:S(2)}, u32[]{:S(2)}) collective-permute-start(bf16[192,256]{1,0:T(8,128)(2,1)S(1)} %constant_dynamic-slice_fusion.5), channel_id=1, source_target_pairs={{0,2},{1,3},{2,0},{3,1},{4,6},{5,7},{6,4},{7,5},{8,10},{9,11},{10,... | collective-permute-start | bytes 294920 | tf_op jit(solution)/shard_map/ppermute | solution.py:524
  67.1 2.0 %collective-permute-done.18 = bf16[400,256]{1,0:T(8,128)(2,1)S(1)} collective-permute-done((bf16[400,256]{1,0:T(8,128)(2,1)S(1)}, bf16[400,256]{1,0:T(8,128)(2,1)S(1)}, u32[]{:S(2)}, u32[]{:S(2)}) %collective-permute-start.18) | collective-permute-done | bytes 204832 | tf_op jit(solution)/shard_map/ppermute | solution.py:524
  69.2 1.7 %collective-permute-start.19 = (bf16[208,256]{1,0:T(8,128)(2,1)S(1)}, bf16[208,256]{1,0:T(8,128)(2,1)S(1)}, u32[]{:S(2)}, u32[]{:S(2)}) collective-permute-start(bf16[208,256]{1,0:T(8,128)(2,1)S(1)} %pad_maximum_fusion.9), channel_id=1, source_target_pairs={{0,4},{1,5},{2,6},{3,7},{4,0},{5,1},{6,2},{7,3},{8,12},{9,13},{10,... | collective-permute-start | bytes 319496 | tf_op jit(solution)/shard_map/ppermute | solution.py:524
  70.9 2.7 %collective-permute-start.12 = (bf16[96,256]{1,0:T(8,128)(2,1)S(1)}, bf16[96,256]{1,0:T(8,128)(2,1)S(1)}, u32[]{:S(2)}, u32[]{:S(2)}) collective-permute-start(bf16[96,256]{1,0:T(8,128)(2,1)S(1)} %constant_dynamic-slice_fusion.4), channel_id=1, source_target_pairs={{0,8},{1,9},{2,10},{3,11},{4,12},{5,13},{6,14},{7,15},{8,0},{9,1},... | collective-permute-start | bytes 147464 | tf_op jit(solution)/shard_map/ppermute | solution.py:524
  74.6 2.2 %collective-permute-start.20 = (bf16[112,256]{1,0:T(8,128)(2,1)S(1)}, bf16[112,256]{1,0:T(8,128)(2,1)S(1)}, u32[]{:S(2)}, u32[]{:S(2)}) collective-permute-start(bf16[112,256]{1,0:T(8,128)(2,1)S(1)} %pad_maximum_fusion.13), channel_id=1, source_target_pairs={{0,8},{1,9},{2,10},{3,11},{4,12},{5,13},{6,14},{7,15},{8,0},{9,1},... | collective-permute-start | bytes 172040 | tf_op jit(solution)/shard_map/ppermute | solution.py:524
  77.7 1.4 %collective-permute-start.13 = (bf16[96,256]{1,0:T(8,128)(2,1)S(1)}, bf16[96,256]{1,0:T(8,128)(2,1)S(1)}, u32[]{:S(2)}, u32[]{:S(2)}) collective-permute-start(bf16[96,256]{1,0:T(8,128)(2,1)S(1)} %add_convert_fusion.11), channel_id=1, source_target_pairs={{0,8},{1,9},{2,10},{3,11},{4,12},{5,13},{6,14},{7,15},{8,0},{9,1},... | collective-permute-start | bytes 147464 | tf_op jit(solution)/shard_map/ppermute | solution.py:524
  79.8 2.2 %collective-permute-start.21 = (bf16[96,256]{1,0:T(8,128)(2,1)S(1)}, bf16[96,256]{1,0:T(8,128)(2,1)S(1)}, u32[]{:S(2)}, u32[]{:S(2)}) collective-permute-start(bf16[96,256]{1,0:T(8,128)(2,1)S(1)} %slice.98), channel_id=1, source_target_pairs={{0,8},{1,9},{2,10},{3,11},{4,12},{5,13},{6,14},{7,15},{8,0},{9,1},... | collective-permute-start | bytes 147464 | tf_op jit(solution)/shard_map/ppermute | solution.py:524
  81.9 1.5 %collective-permute-done.13 = bf16[96,256]{1,0:T(8,128)(2,1)S(1)} collective-permute-done((bf16[96,256]{1,0:T(8,128)(2,1)S(1)}, bf16[96,256]{1,0:T(8,128)(2,1)S(1)}, u32[]{:S(2)}, u32[]{:S(2)}) %collective-permute-start.13) | collective-permute-done | bytes 49184 | tf_op jit(solution)/shard_map/ppermute | solution.py:524
  83.5 1.5 %collective-permute-start.14 = (bf16[192,256]{1,0:T(8,128)(2,1)S(1)}, bf16[192,256]{1,0:T(8,128)(2,1)S(1)}, u32[]{:S(2)}, u32[]{:S(2)}) collective-permute-start(bf16[192,256]{1,0:T(8,128)(2,1)S(1)} %pad_maximum_fusion.11), channel_id=1, source_target_pairs={{0,2},{1,3},{2,0},{3,1},{4,6},{5,7},{6,4},{7,5},{8,10},{9,11},{10,... | collective-permute-start | bytes 294920 | tf_op jit(solution)/shard_map/ppermute | solution.py:524
  85.0 1.5 %collective-permute-start.22 = (bf16[192,256]{1,0:T(8,128)(2,1)S(1)}, bf16[192,256]{1,0:T(8,128)(2,1)S(1)}, u32[]{:S(2)}, u32[]{:S(2)}) collective-permute-start(bf16[192,256]{1,0:T(8,128)(2,1)S(1)} %pad_maximum_fusion.12), channel_id=1, source_target_pairs={{0,4},{1,5},{2,6},{3,7},{4,0},{5,1},{6,2},{7,3},{8,12},{9,13},{10,... | collective-permute-start | bytes 294920 | tf_op jit(solution)/shard_map/ppermute | solution.py:524
  86.5 1.6 %collective-permute-done.14 = bf16[192,256]{1,0:T(8,128)(2,1)S(1)} collective-permute-done((bf16[192,256]{1,0:T(8,128)(2,1)S(1)}, bf16[192,256]{1,0:T(8,128)(2,1)S(1)}, u32[]{:S(2)}, u32[]{:S(2)}) %collective-permute-start.14) | collective-permute-done | bytes 98336 | tf_op jit(solution)/shard_map/ppermute | solution.py:524
  88.8 1.2 %collective-permute-done.22 = bf16[192,256]{1,0:T(8,128)(2,1)S(1)} collective-permute-done((bf16[192,256]{1,0:T(8,128)(2,1)S(1)}, bf16[192,256]{1,0:T(8,128)(2,1)S(1)}, u32[]{:S(2)}, u32[]{:S(2)}) %collective-permute-start.22) | collective-permute-done | bytes 98336 | tf_op jit(solution)/shard_map/ppermute | solution.py:524
  90.1 1.5 %collective-permute-start.23 = (bf16[384,256]{1,0:T(8,128)(2,1)S(1)}, bf16[384,256]{1,0:T(8,128)(2,1)S(1)}, u32[]{:S(2)}, u32[]{:S(2)}) collective-permute-start(bf16[384,256]{1,0:T(8,128)(2,1)S(1)} %pad_maximum_fusion.8), channel_id=1, source_target_pairs={{0,2},{1,3},{2,0},{3,1},{4,6},{5,7},{6,4},{7,5},{8,10},{9,11},{10,... | collective-permute-start | bytes 589832 | tf_op jit(solution)/shard_map/ppermute | solution.py:524
  91.7 2.3 %collective-permute-done.15 = bf16[384,256]{1,0:T(8,128)(2,1)S(1)} collective-permute-done((bf16[384,256]{1,0:T(8,128)(2,1)S(1)}, bf16[384,256]{1,0:T(8,128)(2,1)S(1)}, u32[]{:S(2)}, u32[]{:S(2)}) %collective-permute-start.15) | collective-permute-done | bytes 196640 | tf_op jit(solution)/shard_map/ppermute | solution.py:524
  94.0 1.5 %collective-permute-start.16 = (bf16[768,256]{1,0:T(8,128)(2,1)S(1)}, bf16[768,256]{1,0:T(8,128)(2,1)S(1)}, u32[]{:S(2)}, u32[]{:S(2)}) collective-permute-start(bf16[768,256]{1,0:T(8,128)(2,1)S(1)} %pad_maximum_fusion.3), channel_id=1, source_target_pairs={{0,1},{1,0},{2,3},{3,2},{4,5},{5,4},{6,7},{7,6},{8,9},{9,8},{10,11... | collective-permute-start | bytes 1179656 | tf_op jit(solution)/shard_map/ppermute | solution.py:524
  96.1 1.9 %collective-permute-done.23 = bf16[384,256]{1,0:T(8,128)(2,1)S(1)} collective-permute-done((bf16[384,256]{1,0:T(8,128)(2,1)S(1)}, bf16[384,256]{1,0:T(8,128)(2,1)S(1)}, u32[]{:S(2)}, u32[]{:S(2)}) %collective-permute-start.23) | collective-permute-done | bytes 196640 | tf_op jit(solution)/shard_map/ppermute | solution.py:524
  98.2 1.5 %collective-permute-start.24 = (bf16[768,256]{1,0:T(8,128)(2,1)S(1)}, bf16[768,256]{1,0:T(8,128)(2,1)S(1)}, u32[]{:S(2)}, u32[]{:S(2)}) collective-permute-start(bf16[768,256]{1,0:T(8,128)(2,1)S(1)} %pad_maximum_fusion.4), channel_id=1, source_target_pairs={{0,1},{1,0},{2,3},{3,2},{4,5},{5,4},{6,7},{7,6},{8,9},{9,8},{10,11... | collective-permute-start | bytes 1179656 | tf_op jit(solution)/shard_map/ppermute | solution.py:524
  99.7 2.2 %collective-permute-done.16 = bf16[768,256]{1,0:T(8,128)(2,1)S(1)} collective-permute-done((bf16[768,256]{1,0:T(8,128)(2,1)S(1)}, bf16[768,256]{1,0:T(8,128)(2,1)S(1)}, u32[]{:S(2)}, u32[]{:S(2)}) %collective-permute-start.16) | collective-permute-done | bytes 393248 | tf_op jit(solution)/shard_map/ppermute | solution.py:524
  103.7 2.4 %collective-permute-done.24 = bf16[768,256]{1,0:T(8,128)(2,1)S(1)} collective-permute-done((bf16[768,256]{1,0:T(8,128)(2,1)S(1)}, bf16[768,256]{1,0:T(8,128)(2,1)S(1)}, u32[]{:S(2)}, u32[]{:S(2)}) %collective-permute-start.24) | collective-permute-done | bytes 393248 | tf_op jit(solution)/shard_map/ppermute | solution.py:524
  106.3 1.0 maximum_convert_fusion.1
  107.4 1.1 %maximum_convert_fusion = f32[1,256,1024]{2,1,0:T(8,128)} fusion(bf16[1,256,256]{2,1,0:T(8,128)(2,1)S(1)} %slice_bitcast_fusion.2, bf16[1,256,256]{2,1,0:T(8,128)(2,1)S(1)} %get-tuple-element.53, bf16[1,256,256]{2,1,0:T(8,128)(2,1)S(1)} %get-tuple-element.54, bf16[1,256,256]{2,1,0:T(8,128)(2,1)S(1)} %get-tuple-element.52), kind=kLoop, calls=%fused_computation.14 | loop fusion | flops 2097152 | bytes 1572864 | tf_op jit(solution)/shard_map/convert_element_type | solution.py:632
  (91 shorter events, 13.0 us)
Async XLA Ops:
  0.6 6.5 %collective-permute-start.3 = (bf16[1,256,1024]{2,1,0:T(8,128)(2,1)}, bf16[1,256,1024]{2,1,0:T(8,128)(2,1)}, u32[]{:S(2)}, u32[]{:S(2)}) collective-permute-start(bf16[1,256,1024]{2,1,0:T(8,128)(2,1)} %wup_mine.1), channel_id=1, source_target_pairs={{0,16},{16,0},{1,17},{17,1},{2,18},{18,2},{3,19},{19,3},{4,20},{20... | collective-permute-start | bytes 1572872 | tf_op jit(solution)/shard_map/ppermute | solution.py:519
  1.2 6.0 %collective-permute-start.4 = (bf16[1,1024,256]{2,1,0:T(8,128)(2,1)}, bf16[1,1024,256]{2,1,0:T(8,128)(2,1)}, u32[]{:S(2)}, u32[]{:S(2)}) collective-permute-start(bf16[1,1024,256]{2,1,0:T(8,128)(2,1)} %wdown_mine.1), channel_id=1, source_target_pairs={{0,16},{16,0},{1,17},{17,1},{2,18},{18,2},{3,19},{19,3},{4,20},{20... | collective-permute-start | bytes 1572872 | tf_op jit(solution)/shard_map/ppermute | solution.py:519
  1.2 5.9 %collective-permute-start.1 = (bf16[1,256,768]{2,1,0:T(8,128)(2,1)}, bf16[1,256,768]{2,1,0:T(8,128)(2,1)}, u32[]{:S(2)}, u32[]{:S(2)}) collective-permute-start(bf16[1,256,768]{2,1,0:T(8,128)(2,1)} %wqkv_mine.1), channel_id=1, source_target_pairs={{0,16},{16,0},{1,17},{17,1},{2,18},{18,2},{3,19},{19,3},{4,20},{20... | collective-permute-start | bytes 1179656 | tf_op jit(solution)/shard_map/ppermute | solution.py:519
  1.7 5.5 %collective-permute-start.2 = (bf16[1,256,256]{2,1,0:T(8,128)(2,1)}, bf16[1,256,256]{2,1,0:T(8,128)(2,1)}, u32[]{:S(2)}, u32[]{:S(2)}) collective-permute-start(bf16[1,256,256]{2,1,0:T(8,128)(2,1)} %wout_mine.1), channel_id=1, source_target_pairs={{0,16},{16,0},{1,17},{17,1},{2,18},{18,2},{3,19},{19,3},{4,20},{20... | collective-permute-start | bytes 393224 | tf_op jit(solution)/shard_map/ppermute | solution.py:519
  2.4 4.7 %copy-start.4 = (bf16[2,256]{1,0:T(2,128)(2,1)}, bf16[2,256]{1,0:T(2,128)(2,1)S(1)}, u32[]{:S(2)}) copy-start(bf16[2,256]{1,0:T(2,128)(2,1)S(1)} %pad_maximum_fusion.15.gains_mine) | copy-start | bytes 3076
  2.5 4.7 %collective-permute-start = (bf16[2,256]{1,0:T(2,128)(2,1)S(1)}, bf16[2,256]{1,0:T(2,128)(2,1)S(1)}, u32[]{:S(2)}, u32[]{:S(2)}) collective-permute-start(bf16[2,256]{1,0:T(2,128)(2,1)S(1)} %pad_maximum_fusion.15.gains_mine), channel_id=1, source_target_pairs={{0,16},{16,0},{1,17},{17,1},{2,18},{18,2},{3,19},{19,3},{4,20},{20... | collective-permute-start | bytes 3080 | tf_op jit(solution)/shard_map/ppermute | solution.py:519
  7.1 0.6 copy-start.5
  46.2 7.1 %copy-start.1 = (bf16[1552,256]{1,0:T(8,128)(2,1)S(1)}, bf16[1552,256]{1,0:T(8,128)(2,1)}, u32[]{:S(2)}) copy-start(bf16[1552,256]{1,0:T(8,128)(2,1)} %get-tuple-element.26) | copy-start | bytes 2383876
  46.2 2.6 %collective-permute-start.8 = (bf16[1536,256]{1,0:T(8,128)(2,1)}, bf16[1536,256]{1,0:T(8,128)(2,1)S(1)}, u32[]{:S(2)}, u32[]{:S(2)}) collective-permute-start(bf16[1536,256]{1,0:T(8,128)(2,1)} %get-tuple-element.31), channel_id=1, source_target_pairs={{0,16},{16,0},{1,17},{17,1},{2,18},{18,2},{3,19},{19,3},{4,20},{20... | collective-permute-start | bytes 2359304 | tf_op jit(solution)/shard_map/ppermute | solution.py:519
  46.3 6.2 %collective-permute-start.6 = (bf16[1552,256]{1,0:T(8,128)(2,1)}, bf16[1552,256]{1,0:T(8,128)(2,1)S(1)}, u32[]{:S(2)}, u32[]{:S(2)}) collective-permute-start(bf16[1552,256]{1,0:T(8,128)(2,1)} %get-tuple-element.27), channel_id=1, source_target_pairs={{0,16},{16,0},{1,17},{17,1},{2,18},{18,2},{3,19},{19,3},{4,20},{20... | collective-permute-start | bytes 2383880 | tf_op jit(solution)/shard_map/ppermute | solution.py:519
  46.8 6.8 %collective-permute-start.7 = (bf16[1408,256]{1,0:T(8,128)(2,1)}, bf16[1408,256]{1,0:T(8,128)(2,1)S(1)}, u32[]{:S(2)}, u32[]{:S(2)}) collective-permute-start(bf16[1408,256]{1,0:T(8,128)(2,1)} %bitcast.39), channel_id=1, source_target_pairs={{0,16},{16,0},{1,17},{17,1},{2,18},{18,2},{3,19},{19,3},{4,20},{20... | collective-permute-start | bytes 2162696 | tf_op jit(solution)/shard_map/ppermute | solution.py:519
  46.8 8.4 %collective-permute-start.5 = (bf16[1408,256]{1,0:T(8,128)(2,1)}, bf16[1408,256]{1,0:T(8,128)(2,1)S(1)}, u32[]{:S(2)}, u32[]{:S(2)}) collective-permute-start(bf16[1408,256]{1,0:T(8,128)(2,1)} %bitcast.38), channel_id=1, source_target_pairs={{0,16},{16,0},{1,17},{17,1},{2,18},{18,2},{3,19},{19,3},{4,20},{20... | collective-permute-start | bytes 2162696 | tf_op jit(solution)/shard_map/ppermute | solution.py:519
  49.8 8.4 %collective-permute-start.9 = (bf16[768,256]{1,0:T(8,128)(2,1)S(1)}, bf16[768,256]{1,0:T(8,128)(2,1)S(1)}, u32[]{:S(2)}, u32[]{:S(2)}) collective-permute-start(bf16[768,256]{1,0:T(8,128)(2,1)S(1)} %add_convert_fusion.3), channel_id=1, source_target_pairs={{0,1},{1,0},{2,3},{3,2},{4,5},{5,4},{6,7},{7,6},{8,9},{9,8},{10,11... | collective-permute-start | bytes 1179656 | tf_op jit(solution)/shard_map/ppermute | solution.py:524
  53.4 1.4 %copy-start = (f32[4,340,256]{2,1,0:T(8,128)S(1)}, f32[4,340,256]{2,1,0:T(8,128)}, u32[]{:S(2)}) copy-start(f32[4,340,256]{2,1,0:T(8,128)} %get-tuple-element.28) | copy-start | bytes 4177924
  53.5 9.6 %collective-permute-start.17 = (bf16[784,256]{1,0:T(8,128)(2,1)S(1)}, bf16[784,256]{1,0:T(8,128)(2,1)S(1)}, u32[]{:S(2)}, u32[]{:S(2)}) collective-permute-start(bf16[784,256]{1,0:T(8,128)(2,1)S(1)} %pad_maximum_fusion.2.event_ref), channel_id=1, source_target_pairs={{0,1},{1,0},{2,3},{3,2},{4,5},{5,4},{6,7},{7,6},{8,9},{9,8},{10,11... | collective-permute-start | bytes 1204232 | tf_op jit(solution)/shard_map/ppermute | solution.py:524
  55.2 1.1 %copy-start.3 = (bf16[4,340,256]{2,1,0:T(8,128)(2,1)S(1)}, bf16[4,340,256]{2,1,0:T(8,128)(2,1)}, u32[]{:S(2)}) copy-start(bf16[4,340,256]{2,1,0:T(8,128)(2,1)} %get-tuple-element.24) | copy-start | bytes 2088964
  56.6 1.7 %copy-start.2 = (bf16[1536,256]{1,0:T(8,128)(2,1)S(1)}, bf16[1536,256]{1,0:T(8,128)(2,1)}, u32[]{:S(2)}) copy-start(bf16[1536,256]{1,0:T(8,128)(2,1)} %get-tuple-element.30) | copy-start | bytes 2359300
  58.5 6.8 %collective-permute-start.10 = (bf16[384,256]{1,0:T(8,128)(2,1)S(1)}, bf16[384,256]{1,0:T(8,128)(2,1)S(1)}, u32[]{:S(2)}, u32[]{:S(2)}) collective-permute-start(bf16[384,256]{1,0:T(8,128)(2,1)S(1)} %constant_dynamic-slice_fusion.6.event_ref), channel_id=1, source_target_pairs={{0,4},{1,5},{2,6},{3,7},{4,0},{5,1},{6,2},{7,3},{8,12},{9,13},{10,... | collective-permute-start | bytes 589832 | tf_op jit(solution)/shard_map/ppermute | solution.py:524
  63.2 5.8 %collective-permute-start.18 = (bf16[400,256]{1,0:T(8,128)(2,1)S(1)}, bf16[400,256]{1,0:T(8,128)(2,1)S(1)}, u32[]{:S(2)}, u32[]{:S(2)}) collective-permute-start(bf16[400,256]{1,0:T(8,128)(2,1)S(1)} %pad_maximum_fusion.5), channel_id=1, source_target_pairs={{0,2},{1,3},{2,0},{3,1},{4,6},{5,7},{6,4},{7,5},{8,10},{9,11},{10,... | collective-permute-start | bytes 614408 | tf_op jit(solution)/shard_map/ppermute | solution.py:524
  65.3 5.5 %collective-permute-start.11 = (bf16[192,256]{1,0:T(8,128)(2,1)S(1)}, bf16[192,256]{1,0:T(8,128)(2,1)S(1)}, u32[]{:S(2)}, u32[]{:S(2)}) collective-permute-start(bf16[192,256]{1,0:T(8,128)(2,1)S(1)} %constant_dynamic-slice_fusion.5), channel_id=1, source_target_pairs={{0,2},{1,3},{2,0},{3,1},{4,6},{5,7},{6,4},{7,5},{8,10},{9,11},{10,... | collective-permute-start | bytes 294920 | tf_op jit(solution)/shard_map/ppermute | solution.py:524
  69.2 5.3 %collective-permute-start.19 = (bf16[208,256]{1,0:T(8,128)(2,1)S(1)}, bf16[208,256]{1,0:T(8,128)(2,1)S(1)}, u32[]{:S(2)}, u32[]{:S(2)}) collective-permute-start(bf16[208,256]{1,0:T(8,128)(2,1)S(1)} %pad_maximum_fusion.9), channel_id=1, source_target_pairs={{0,4},{1,5},{2,6},{3,7},{4,0},{5,1},{6,2},{7,3},{8,12},{9,13},{10,... | collective-permute-start | bytes 319496 | tf_op jit(solution)/shard_map/ppermute | solution.py:524
  70.9 6.7 %collective-permute-start.12 = (bf16[96,256]{1,0:T(8,128)(2,1)S(1)}, bf16[96,256]{1,0:T(8,128)(2,1)S(1)}, u32[]{:S(2)}, u32[]{:S(2)}) collective-permute-start(bf16[96,256]{1,0:T(8,128)(2,1)S(1)} %constant_dynamic-slice_fusion.4), channel_id=1, source_target_pairs={{0,8},{1,9},{2,10},{3,11},{4,12},{5,13},{6,14},{7,15},{8,0},{9,1},... | collective-permute-start | bytes 147464 | tf_op jit(solution)/shard_map/ppermute | solution.py:524
  74.6 5.2 %collective-permute-start.20 = (bf16[112,256]{1,0:T(8,128)(2,1)S(1)}, bf16[112,256]{1,0:T(8,128)(2,1)S(1)}, u32[]{:S(2)}, u32[]{:S(2)}) collective-permute-start(bf16[112,256]{1,0:T(8,128)(2,1)S(1)} %pad_maximum_fusion.13), channel_id=1, source_target_pairs={{0,8},{1,9},{2,10},{3,11},{4,12},{5,13},{6,14},{7,15},{8,0},{9,1},... | collective-permute-start | bytes 172040 | tf_op jit(solution)/shard_map/ppermute | solution.py:524
  77.7 5.7 %collective-permute-start.13 = (bf16[96,256]{1,0:T(8,128)(2,1)S(1)}, bf16[96,256]{1,0:T(8,128)(2,1)S(1)}, u32[]{:S(2)}, u32[]{:S(2)}) collective-permute-start(bf16[96,256]{1,0:T(8,128)(2,1)S(1)} %add_convert_fusion.11), channel_id=1, source_target_pairs={{0,8},{1,9},{2,10},{3,11},{4,12},{5,13},{6,14},{7,15},{8,0},{9,1},... | collective-permute-start | bytes 147464 | tf_op jit(solution)/shard_map/ppermute | solution.py:524
  79.8 5.2 %collective-permute-start.21 = (bf16[96,256]{1,0:T(8,128)(2,1)S(1)}, bf16[96,256]{1,0:T(8,128)(2,1)S(1)}, u32[]{:S(2)}, u32[]{:S(2)}) collective-permute-start(bf16[96,256]{1,0:T(8,128)(2,1)S(1)} %slice.98), channel_id=1, source_target_pairs={{0,8},{1,9},{2,10},{3,11},{4,12},{5,13},{6,14},{7,15},{8,0},{9,1},... | collective-permute-start | bytes 147464 | tf_op jit(solution)/shard_map/ppermute | solution.py:524
  83.5 4.7 %collective-permute-start.14 = (bf16[192,256]{1,0:T(8,128)(2,1)S(1)}, bf16[192,256]{1,0:T(8,128)(2,1)S(1)}, u32[]{:S(2)}, u32[]{:S(2)}) collective-permute-start(bf16[192,256]{1,0:T(8,128)(2,1)S(1)} %pad_maximum_fusion.11), channel_id=1, source_target_pairs={{0,2},{1,3},{2,0},{3,1},{4,6},{5,7},{6,4},{7,5},{8,10},{9,11},{10,... | collective-permute-start | bytes 294920 | tf_op jit(solution)/shard_map/ppermute | solution.py:524
  85.0 5.1 %collective-permute-start.22 = (bf16[192,256]{1,0:T(8,128)(2,1)S(1)}, bf16[192,256]{1,0:T(8,128)(2,1)S(1)}, u32[]{:S(2)}, u32[]{:S(2)}) collective-permute-start(bf16[192,256]{1,0:T(8,128)(2,1)S(1)} %pad_maximum_fusion.12), channel_id=1, source_target_pairs={{0,4},{1,5},{2,6},{3,7},{4,0},{5,1},{6,2},{7,3},{8,12},{9,13},{10,... | collective-permute-start | bytes 294920 | tf_op jit(solution)/shard_map/ppermute | solution.py:524
  88.2 5.7 %collective-permute-start.15 = (bf16[384,256]{1,0:T(8,128)(2,1)S(1)}, bf16[384,256]{1,0:T(8,128)(2,1)S(1)}, u32[]{:S(2)}, u32[]{:S(2)}) collective-permute-start(bf16[384,256]{1,0:T(8,128)(2,1)S(1)} %pad_maximum_fusion.7), channel_id=1, source_target_pairs={{0,4},{1,5},{2,6},{3,7},{4,0},{5,1},{6,2},{7,3},{8,12},{9,13},{10,... | collective-permute-start | bytes 589832 | tf_op jit(solution)/shard_map/ppermute | solution.py:524
  90.1 7.9 %collective-permute-start.23 = (bf16[384,256]{1,0:T(8,128)(2,1)S(1)}, bf16[384,256]{1,0:T(8,128)(2,1)S(1)}, u32[]{:S(2)}, u32[]{:S(2)}) collective-permute-start(bf16[384,256]{1,0:T(8,128)(2,1)S(1)} %pad_maximum_fusion.8), channel_id=1, source_target_pairs={{0,2},{1,3},{2,0},{3,1},{4,6},{5,7},{6,4},{7,5},{8,10},{9,11},{10,... | collective-permute-start | bytes 589832 | tf_op jit(solution)/shard_map/ppermute | solution.py:524
  94.0 7.8 %collective-permute-start.16 = (bf16[768,256]{1,0:T(8,128)(2,1)S(1)}, bf16[768,256]{1,0:T(8,128)(2,1)S(1)}, u32[]{:S(2)}, u32[]{:S(2)}) collective-permute-start(bf16[768,256]{1,0:T(8,128)(2,1)S(1)} %pad_maximum_fusion.3), channel_id=1, source_target_pairs={{0,1},{1,0},{2,3},{3,2},{4,5},{5,4},{6,7},{7,6},{8,9},{9,8},{10,11... | collective-permute-start | bytes 1179656 | tf_op jit(solution)/shard_map/ppermute | solution.py:524
  98.2 7.9 %collective-permute-start.24 = (bf16[768,256]{1,0:T(8,128)(2,1)S(1)}, bf16[768,256]{1,0:T(8,128)(2,1)S(1)}, u32[]{:S(2)}, u32[]{:S(2)}) collective-permute-start(bf16[768,256]{1,0:T(8,128)(2,1)S(1)} %pad_maximum_fusion.4), channel_id=1, source_target_pairs={{0,1},{1,0},{2,3},{3,2},{4,5},{5,4},{6,7},{7,6},{8,9},{9,8},{10,11... | collective-permute-start | bytes 1179656 | tf_op jit(solution)/shard_map/ppermute | solution.py:524
